TPU v7x, 32 devices: a whole 2x2x4 slice. The times are simulated.
32 devices in a mesh: cam: 2 (over x), band: 4 (over z), obj: 4 (over y, core).
Axes of the slice: x: 2, y: 2, z: 4, core: 2. Of those that a mesh axis runs over, the one named last changes fastest.
Arguments:
- queries: bfloat16 [4, 6, 4, 128, 1280], P('obj', 'cam', 'band'), may hold values from -6 to 6
- keys: bfloat16 [4, 6, 4, 128, 1280], P('obj', 'cam', 'band'), may hold values from -6 to 6
- values: bfloat16 [4, 6, 4, 128, 1280], P('obj', 'cam', 'band'), may hold values from -6 to 6
- d_out: bfloat16 [4, 6, 4, 128, 2432], P('obj', 'cam', 'band'), may hold values from -6 to 6
- w_out: bfloat16 [1280, 2432], P(('band', 'obj'), 'cam'), may hold values from -0.15625 to 0.15625
Outputs:
- grad_q: bfloat16 [4, 6, 4, 128, 1280], P('obj', 'cam', 'band')
- grad_k: bfloat16 [4, 6, 4, 128, 1280], P('obj', 'cam', 'band')
- grad_v: bfloat16 [4, 6, 4, 128, 1280], P('obj', 'cam', 'band')
- grad_wo: float32 [1280, 2432], P(('band', 'obj'), 'cam')
All inputs are finite; a program needn't handle non-finite values.
Results may differ from a plain program's by a relative error of at most 0.0095.
Values may be sent and summed in bfloat16 or wider, within the bound.
No kernel may reach another device: no remote copies, remote signals or barrier semaphores. Data moves between devices by JAX's collectives and lax.ppermute only.
A program may use at most 128 MiB of HBM per device.

v0:
```python
import jax
import jax.numpy as jnp
from jax import lax
from jax.sharding import PartitionSpec as P


def to_pairs(x):
    objects, views, rows, cols, width = x.shape
    grouped = x.transpose(0, 2, 1, 3, 4).reshape(objects * rows, views * cols, width // 128, 128)
    return grouped.transpose(2, 0, 1, 3)


def from_pairs(x, objects, views, rows, cols):
    width = x.shape[0] * 128
    merged = x.transpose(1, 2, 0, 3).reshape(objects, rows, views, cols, width)
    return merged.transpose(0, 2, 1, 3, 4)


def pair_backward(parts):
    q_pair, k_pair, v_pair, d_pair = parts
    groups, n_query = (q_pair.shape[0], q_pair.shape[1])
    n_key = k_pair.shape[1]
    q_heads = q_pair.reshape(groups, n_query, 2, 64)
    k_heads = k_pair.reshape(groups, n_key, 2, 64)
    v_heads = v_pair.reshape(groups, n_key, 2, 64)
    d_heads = d_pair.reshape(groups, n_query, 2, 64)
    scores = (
        jnp.einsum("gqhe,gkhe->ghqk", q_heads, k_heads, preferred_element_type=jnp.float32) * 0.125
    )
    top = jnp.max(scores, axis=-1, keepdims=True)
    expd = jnp.exp(scores - top)
    probs = expd / jnp.sum(expd, axis=-1, keepdims=True)
    probs_b = probs.astype(jnp.bfloat16)
    att = jnp.einsum(
        "ghqk,gkhe->gqhe", probs_b, v_heads, preferred_element_type=jnp.float32
    ).astype(jnp.bfloat16)
    d_probs = jnp.einsum("gqhe,gkhe->ghqk", d_heads, v_heads, preferred_element_type=jnp.float32)
    delta = jnp.sum(probs * d_probs, axis=-1, keepdims=True)
    d_scores_b = (probs * (d_probs - delta)).astype(jnp.bfloat16)
    grad_q = (
        jnp.einsum("ghqk,gkhe->gqhe", d_scores_b, k_heads, preferred_element_type=jnp.float32)
        * 0.125
    )
    grad_k = (
        jnp.einsum("ghqk,gqhe->gkhe", d_scores_b, q_heads, preferred_element_type=jnp.float32)
        * 0.125
    )
    grad_v = jnp.einsum("ghqk,gqhe->gkhe", probs_b, d_heads, preferred_element_type=jnp.float32)
    return (
        grad_q.astype(jnp.bfloat16).reshape(groups, n_query, 128),
        grad_k.reshape(groups, n_key, 128),
        grad_v.reshape(groups, n_key, 128),
        att.reshape(groups, n_query, 128),
    )


def attend(q_part, k_part, v_part, d_part):
    objects, q_views, rows, cols, width = q_part.shape
    k_views = k_part.shape[1]
    results = lax.map(
        pair_backward, (to_pairs(q_part), to_pairs(k_part), to_pairs(v_part), to_pairs(d_part))
    )
    grad_q = from_pairs(results[0], objects, q_views, rows, cols)
    grad_k = from_pairs(results[1], objects, k_views, rows, cols)
    grad_v = from_pairs(results[2], objects, k_views, rows, cols)
    att = from_pairs(results[3], objects, q_views, rows, cols)
    return (grad_q, grad_k, grad_v, att)


def body(queries, keys, values, d_out, w_out):
    objects, views, rows, cols, width = queries.shape
    model_width = d_out.shape[4]
    flat_out = d_out.reshape(-1, model_width)
    total = flat_out.shape[0] * lax.axis_size("cam") * lax.axis_size("band") * lax.axis_size("obj")
    full_cols = lax.all_gather(w_out, "cam", axis=1, tiled=True)
    d_att = lax.dot_general(
        flat_out,
        lax.all_gather(full_cols, ("band", "obj"), axis=0, tiled=True),
        (((1,), (1,)), ((), ())),
        preferred_element_type=jnp.float32,
    )
    d_att = d_att.astype(jnp.bfloat16).reshape(objects, views, rows, cols, width)
    local_q = lax.all_to_all(queries, "cam", split_axis=4, concat_axis=1, tiled=True)
    local_k = lax.all_to_all(keys, "cam", split_axis=4, concat_axis=1, tiled=True)
    local_v = lax.all_to_all(values, "cam", split_axis=4, concat_axis=1, tiled=True)
    local_d = lax.all_to_all(d_att, "cam", split_axis=4, concat_axis=1, tiled=True)
    head_q, head_k, head_v, head_att = attend(local_q, local_k, local_v, local_d)
    grad_q = lax.all_to_all(head_q, "cam", split_axis=1, concat_axis=4, tiled=True)
    grad_k = lax.all_to_all(
        head_k.astype(jnp.bfloat16), "cam", split_axis=1, concat_axis=4, tiled=True
    )
    grad_v = lax.all_to_all(
        head_v.astype(jnp.bfloat16), "cam", split_axis=1, concat_axis=4, tiled=True
    )
    att = lax.all_to_all(head_att, "cam", split_axis=1, concat_axis=4, tiled=True)
    flat_att = att.reshape(-1, width)
    row_sums = lax.psum_scatter(
        lax.dot_general(
            flat_att, flat_out, (((0,), (0,)), ((), ())), preferred_element_type=jnp.float32
        ),
        ("band", "obj"),
        scatter_dimension=0,
        tiled=True,
    )
    grad_wo = lax.psum_scatter(
        row_sums.astype(jnp.bfloat16), "cam", scatter_dimension=1, tiled=True
    ).astype(jnp.float32)
    grad_wo = grad_wo * float(total) ** (-0.5)
    return (grad_q, grad_k, grad_v, grad_wo)


def solution(mesh):
    placed = (
        P("obj", "cam", "band", None, None),
        P("obj", "cam", "band", None, None),
        P("obj", "cam", "band", None, None),
        P("obj", "cam", "band", None, None),
        P(("band", "obj"), "cam"),
    )
    return jax.shard_map(
        body,
        mesh=mesh,
        in_specs=placed,
        out_specs=(
            P("obj", "cam", "band", None, None),
            P("obj", "cam", "band", None, None),
            P("obj", "cam", "band", None, None),
            P(("band", "obj"), "cam"),
        ),
        check_vma=False,
    )
```

profile of v0, /device:TPU:0, one launch (start us, length us, event | category | flops | bytes accessed | tf_op | source)
XLA Modules:
  0.0 396.4 jit_solution(4541480296580207560)
XLA Ops:
  7.2 9.0 %all-gather = bf16[2,1216,80]{1,2,0:T(8,128)(2,1)S(1)} all-gather(bf16[1,1216,80]{1,2,0:T(8,128)(2,1)} %bitcast.200), channel_id=1, replica_groups=mesh['cam'=2,'band'=4,'obj'=4] {'cam'}, dimensions={0}, use_global_device_ids=true | all-gather | bytes 583680 | tf_op jit(solution)/shard_map/all_gather | solution.py:75
  19.8 3.6 all-to-all-start
  26.9 12.7 %all-to-all-done = bf16[1,3,1,128,1280]{3,1,2,0,4:T(4,128)(2,1)S(1)} async-done(((bf16[1,3,1,128,1280]{3,1,2,0,4:T(4,128)(2,1)}), bf16[1,3,1,128,1280]{3,1,2,0,4:T(4,128)(2,1)S(1)}, u32[]{:S(2)}, u32[]{:S(2)}) %all-to-all-start) | async-done | bytes 983072 | tf_op jit(solution)/shard_map/all_to_all | solution.py:84
  39.6 4.5 %all-to-all-start.1 = ((bf16[1,3,1,128,1280]{3,1,2,0,4:T(4,128)(2,1)}), bf16[1,3,1,128,1280]{3,1,2,0,4:T(4,128)(2,1)}, u32[]{:S(2)}, u32[]{:S(2)}) async-start(bf16[1,3,1,128,1280]{3,1,2,0,4:T(4,128)(2,1)} %copy.127), calls=%async_computation.1 | async-start | bytes 2621440 | tf_op jit(solution)/shard_map/all_to_all | solution.py:83
  47.5 12.0 %all-to-all-done.1 = bf16[1,3,1,128,1280]{3,1,2,0,4:T(4,128)(2,1)} async-done(((bf16[1,3,1,128,1280]{3,1,2,0,4:T(4,128)(2,1)}), bf16[1,3,1,128,1280]{3,1,2,0,4:T(4,128)(2,1)}, u32[]{:S(2)}, u32[]{:S(2)}) %all-to-all-start.1) | async-done | bytes 983072 | tf_op jit(solution)/shard_map/all_to_all | solution.py:83
  59.5 4.6 %all-to-all-start.3 = ((bf16[1,3,1,128,1280]{3,1,2,0,4:T(4,128)(2,1)}), bf16[1,3,1,128,1280]{3,1,2,0,4:T(4,128)(2,1)}, u32[]{:S(2)}, u32[]{:S(2)}) async-start(bf16[1,3,1,128,1280]{3,1,2,0,4:T(4,128)(2,1)} %copy.134), calls=%async_computation.3 | async-start | bytes 2621440 | tf_op jit(solution)/shard_map/all_to_all | solution.py:85
  64.1 16.8 %all-gather.3.cloned.1.call-done = bf16[1280,2432]{1,0:T(8,128)(2,1)} async-done(((bf16[80,2432]{1,0:T(8,128)(2,1)}), bf16[1280,2432]{1,0:T(8,128)(2,1)}) %all-gather.3.cloned.1.call-update) | async-done | bytes 6225936 | tf_op jit(solution)/shard_map/all_gather | solution.py:78
  80.8 6.4 %convolution_convert_fusion = bf16[384,1280]{1,0:T(8,128)(2,1)} fusion(bf16[384,2432]{1,0:T(8,128)(2,1)S(1)} %bitcast.161, bf16[1280,2432]{1,0:T(8,128)(2,1)} %all-gather.3.cloned.1.call-done), kind=kOutput, calls=%fused_computation.26 | convolution fusion | flops 2391244800 | bytes 9076736 | tf_op jit(solution)/shard_map/dot_general | solution.py:76
  90.7 4.5 %all-to-all-start.2 = ((bf16[1,3,1,128,1280]{3,1,2,0,4:T(4,128)(2,1)}), bf16[1,3,1,128,1280]{3,1,2,0,4:T(4,128)(2,1)}, u32[]{:S(2)}, u32[]{:S(2)}) async-start(bf16[1,3,1,128,1280]{3,1,2,0,4:T(4,128)(2,1)} %copy.131), calls=%async_computation.2 | async-start | bytes 2621440 | tf_op jit(solution)/shard_map/all_to_all | solution.py:86
  106.0 6.3 %all-to-all-done.2 = bf16[1,3,1,128,1280]{3,1,2,0,4:T(4,128)(2,1)} async-done(((bf16[1,3,1,128,1280]{3,1,2,0,4:T(4,128)(2,1)}), bf16[1,3,1,128,1280]{3,1,2,0,4:T(4,128)(2,1)}, u32[]{:S(2)}, u32[]{:S(2)}) %all-to-all-start.2) | async-done | bytes 983072 | tf_op jit(solution)/shard_map/all_to_all | solution.py:86
  116.3 80.9 %while.16 = (s32[]{:T(128)}, bf16[5,1,768,128]{2,3,1,0:T(8,128)(2,1)}, bf16[5,1,768,128]{2,3,1,0:T(8,128)(2,1)}, bf16[5,1,768,128]{2,3,1,0:T(8,128)(2,1)}, bf16[...) while((s32[]{:T(128)}, ...), condition=%wide.region_4.5_spmd, body=%wide.region_0.4_spmd.sunk | while | flops 922975488 | bytes 59813028 | solution.py:60
  118.2 3.7 fusion.62
  134.4 3.7 fusion.62
  150.6 3.7 fusion.62
  166.8 3.7 fusion.62
  183.0 3.7 fusion.62
  201.7 16.3 %all_to_all.129 = bf16[1,6,1,128,640]{4,3,2,0,1:T(8,128)(2,1)S(1)} all-to-all(bf16[1,6,1,128,640]{4,3,2,0,1:T(8,128)(2,1)} %copy.147), channel_id=1, replica_groups=mesh['cam'=2,'band'=4,'obj'=4] {'cam'}, dimensions={1} | all-to-all | bytes 1966080 | tf_op jit(solution)/shard_map/all_to_all | solution.py:95
  219.2 6.4 %fusion.17 = f32[1280,2432]{1,0:T(8,128)} fusion(bf16[384,1280]{1,0:T(8,128)(2,1)S(1)} %bitcast.177, bf16[384,2432]{1,0:T(8,128)(2,1)S(1)} %bitcast.162), kind=kOutput, calls=%fused_computation.31 | convolution fusion | flops 2390753280 | bytes 15302656 | tf_op jit(solution)/shard_map/dot_general | solution.py:98
  230.0 4.4 %all-to-all-start.4 = ((bf16[1,6,1,128,640]{4,3,2,0,1:T(8,128)(2,1)}), bf16[1,6,1,128,640]{4,3,2,0,1:T(8,128)(2,1)}, u32[]{:S(2)}, u32[]{:S(2)}) async-start(bf16[1,6,1,128,640]{4,3,2,0,1:T(8,128)(2,1)} %copy.141), calls=%async_computation.4 | async-start | bytes 1966080 | tf_op jit(solution)/shard_map/all_to_all | solution.py:88
  238.9 7.5 %all-to-all-done.4 = bf16[1,6,1,128,640]{4,3,2,0,1:T(8,128)(2,1)} async-done(((bf16[1,6,1,128,640]{4,3,2,0,1:T(8,128)(2,1)}), bf16[1,6,1,128,640]{4,3,2,0,1:T(8,128)(2,1)}, u32[]{:S(2)}, u32[]{:S(2)}) %all-to-all-start.4) | async-done | bytes 983072 | tf_op jit(solution)/shard_map/all_to_all | solution.py:88
  246.4 4.4 %all-to-all-start.5 = ((bf16[1,6,1,128,640]{4,3,2,0,1:T(8,128)(2,1)}), bf16[1,6,1,128,640]{4,3,2,0,1:T(8,128)(2,1)}, u32[]{:S(2)}, u32[]{:S(2)}) async-start(bf16[1,6,1,128,640]{4,3,2,0,1:T(8,128)(2,1)} %copy.143), calls=%async_computation.5 | async-start | bytes 1966080 | tf_op jit(solution)/shard_map/all_to_all | solution.py:89
  250.8 106.8 %reduce-scatter.5.cloned.1.call-done = f32[80,2432]{1,0:T(8,128)} async-done(((f32[1280,2432]{1,0:T(8,128)}), f32[80,2432]{1,0:T(8,128)}) %reduce-scatter.5.cloned.1.call-update) | async-done | bytes 778256 | tf_op jit(solution)/shard_map/reduce_scatter | solution.py:97
  364.4 3.6 all-to-all-start.6
  376.9 7.4 %all-to-all-done.6 = bf16[1,6,1,128,640]{4,3,2,0,1:T(8,128)(2,1)S(1)} async-done(((bf16[1,6,1,128,640]{4,3,2,0,1:T(8,128)(2,1)}), bf16[1,6,1,128,640]{4,3,2,0,1:T(8,128)(2,1)S(1)}, u32[]{:S(2)}, u32[]{:S(2)}) %all-to-all-start.6) | async-done | bytes 983072 | tf_op jit(solution)/shard_map/all_to_all | solution.py:92
  (140 shorter events, 126.5 us)
Async XLA Ops:
  7.2 73.7 %copy-start = (bf16[1,3,1,128,2432]{4,3,2,1,0:T(8,128)(2,1)S(1)}, bf16[1,3,1,128,2432]{4,3,2,1,0:T(8,128)(2,1)}, u32[]{:S(2)}) copy-start(bf16[1,3,1,128,2432]{4,3,2,1,0:T(8,128)(2,1)} %param.10) | copy-start | bytes 5603332
  7.2 10.5 %copy-start.1 = (bf16[1,3,1,128,1280]{4,3,2,1,0:T(8,128)(2,1)S(1)}, bf16[1,3,1,128,1280]{4,3,2,1,0:T(8,128)(2,1)}, u32[]{:S(2)}) copy-start(bf16[1,3,1,128,1280]{4,3,2,1,0:T(8,128)(2,1)} %param.8) | copy-start | bytes 2949124
  7.2 73.6 %all-gather.3.cloned.1.call-start = ((), (), s32[]{:S(2)}) async-start(), calls=%async_computation.10 | async-start | bytes 6615040 | tf_op jit(solution)/shard_map/all_gather | solution.py:78
  19.8 19.7 %all-to-all-start = ((bf16[1,3,1,128,1280]{3,1,2,0,4:T(4,128)(2,1)}), bf16[1,3,1,128,1280]{3,1,2,0,4:T(4,128)(2,1)S(1)}, u32[]{:S(2)}, u32[]{:S(2)}) async-start(bf16[1,3,1,128,1280]{3,1,2,0,4:T(4,128)(2,1)} %copy.124), calls=%async_computation | async-start | bytes 2621440 | tf_op jit(solution)/shard_map/all_to_all | solution.py:84
  39.6 19.9 %all-to-all-start.1 = ((bf16[1,3,1,128,1280]{3,1,2,0,4:T(4,128)(2,1)}), bf16[1,3,1,128,1280]{3,1,2,0,4:T(4,128)(2,1)}, u32[]{:S(2)}, u32[]{:S(2)}) async-start(bf16[1,3,1,128,1280]{3,1,2,0,4:T(4,128)(2,1)} %copy.127), calls=%async_computation.1 | async-start | bytes 2621440 | tf_op jit(solution)/shard_map/all_to_all | solution.py:83
  59.5 31.2 %all-to-all-start.3 = ((bf16[1,3,1,128,1280]{3,1,2,0,4:T(4,128)(2,1)}), bf16[1,3,1,128,1280]{3,1,2,0,4:T(4,128)(2,1)}, u32[]{:S(2)}, u32[]{:S(2)}) async-start(bf16[1,3,1,128,1280]{3,1,2,0,4:T(4,128)(2,1)} %copy.134), calls=%async_computation.3 | async-start | bytes 2621440 | tf_op jit(solution)/shard_map/all_to_all | solution.py:85
  90.7 21.7 %all-to-all-start.2 = ((bf16[1,3,1,128,1280]{3,1,2,0,4:T(4,128)(2,1)}), bf16[1,3,1,128,1280]{3,1,2,0,4:T(4,128)(2,1)}, u32[]{:S(2)}, u32[]{:S(2)}) async-start(bf16[1,3,1,128,1280]{3,1,2,0,4:T(4,128)(2,1)} %copy.131), calls=%async_computation.2 | async-start | bytes 2621440 | tf_op jit(solution)/shard_map/all_to_all | solution.py:86
  95.2 262.5 %reduce-scatter.5.cloned.1.call-start = ((), (), s32[]{:S(2)}) async-start(), calls=%async_computation.11 | async-start | bytes 13230080 | tf_op jit(solution)/shard_map/reduce_scatter | solution.py:97
  121.9 5.2 %slice-start = ((s8[4718592]{0:T(1024)(128)(4,1)}), s8[4194304]{0:T(1024)(128)(4,1)S(1)}, s32[]{:S(2)}) async-start(s8[4718592]{0:T(1024)(128)(4,1)} %bitcast.163), calls=%async_computation.13 | async-start | bytes 8388608 | tf_op jit(solution)/shard_map/while
  123.0 4.1 %slice-start.1 = ((s8[4718592]{0:T(1024)(128)(4,1)}), s8[524288]{0:T(1024)(128)(4,1)S(1)}, s32[]{:S(2)}) async-start(s8[4718592]{0:T(1024)(128)(4,1)} %bitcast.163), calls=%async_computation.14 | async-start | bytes 1048576 | tf_op jit(solution)/shard_map/while
  138.1 5.2 %slice-start = ((s8[4718592]{0:T(1024)(128)(4,1)}), s8[4194304]{0:T(1024)(128)(4,1)S(1)}, s32[]{:S(2)}) async-start(s8[4718592]{0:T(1024)(128)(4,1)} %bitcast.163), calls=%async_computation.13 | async-start | bytes 8388608 | tf_op jit(solution)/shard_map/while
  139.2 4.1 %slice-start.1 = ((s8[4718592]{0:T(1024)(128)(4,1)}), s8[524288]{0:T(1024)(128)(4,1)S(1)}, s32[]{:S(2)}) async-start(s8[4718592]{0:T(1024)(128)(4,1)} %bitcast.163), calls=%async_computation.14 | async-start | bytes 1048576 | tf_op jit(solution)/shard_map/while
  154.3 5.2 %slice-start = ((s8[4718592]{0:T(1024)(128)(4,1)}), s8[4194304]{0:T(1024)(128)(4,1)S(1)}, s32[]{:S(2)}) async-start(s8[4718592]{0:T(1024)(128)(4,1)} %bitcast.163), calls=%async_computation.13 | async-start | bytes 8388608 | tf_op jit(solution)/shard_map/while
  155.4 4.1 %slice-start.1 = ((s8[4718592]{0:T(1024)(128)(4,1)}), s8[524288]{0:T(1024)(128)(4,1)S(1)}, s32[]{:S(2)}) async-start(s8[4718592]{0:T(1024)(128)(4,1)} %bitcast.163), calls=%async_computation.14 | async-start | bytes 1048576 | tf_op jit(solution)/shard_map/while
  170.4 5.2 %slice-start = ((s8[4718592]{0:T(1024)(128)(4,1)}), s8[4194304]{0:T(1024)(128)(4,1)S(1)}, s32[]{:S(2)}) async-start(s8[4718592]{0:T(1024)(128)(4,1)} %bitcast.163), calls=%async_computation.13 | async-start | bytes 8388608 | tf_op jit(solution)/shard_map/while
  171.5 4.1 %slice-start.1 = ((s8[4718592]{0:T(1024)(128)(4,1)}), s8[524288]{0:T(1024)(128)(4,1)S(1)}, s32[]{:S(2)}) async-start(s8[4718592]{0:T(1024)(128)(4,1)} %bitcast.163), calls=%async_computation.14 | async-start | bytes 1048576 | tf_op jit(solution)/shard_map/while
  186.6 5.2 %slice-start = ((s8[4718592]{0:T(1024)(128)(4,1)}), s8[4194304]{0:T(1024)(128)(4,1)S(1)}, s32[]{:S(2)}) async-start(s8[4718592]{0:T(1024)(128)(4,1)} %bitcast.163), calls=%async_computation.13 | async-start | bytes 8388608 | tf_op jit(solution)/shard_map/while
  187.7 4.1 %slice-start.1 = ((s8[4718592]{0:T(1024)(128)(4,1)}), s8[524288]{0:T(1024)(128)(4,1)S(1)}, s32[]{:S(2)}) async-start(s8[4718592]{0:T(1024)(128)(4,1)} %bitcast.163), calls=%async_computation.14 | async-start | bytes 1048576 | tf_op jit(solution)/shard_map/while
  230.0 16.4 %all-to-all-start.4 = ((bf16[1,6,1,128,640]{4,3,2,0,1:T(8,128)(2,1)}), bf16[1,6,1,128,640]{4,3,2,0,1:T(8,128)(2,1)}, u32[]{:S(2)}, u32[]{:S(2)}) async-start(bf16[1,6,1,128,640]{4,3,2,0,1:T(8,128)(2,1)} %copy.141), calls=%async_computation.4 | async-start | bytes 1966080 | tf_op jit(solution)/shard_map/all_to_all | solution.py:88
  246.4 118.0 %all-to-all-start.5 = ((bf16[1,6,1,128,640]{4,3,2,0,1:T(8,128)(2,1)}), bf16[1,6,1,128,640]{4,3,2,0,1:T(8,128)(2,1)}, u32[]{:S(2)}, u32[]{:S(2)}) async-start(bf16[1,6,1,128,640]{4,3,2,0,1:T(8,128)(2,1)} %copy.143), calls=%async_computation.5 | async-start | bytes 1966080 | tf_op jit(solution)/shard_map/all_to_all | solution.py:89
  250.8 137.2 %reduce-scatter.7.cloned.1.call-start = ((), (), s32[]{:S(2)}) async-start(), calls=%async_computation.12 | async-start | bytes 933888
  364.4 20.0 %all-to-all-start.6 = ((bf16[1,6,1,128,640]{4,3,2,0,1:T(8,128)(2,1)}), bf16[1,6,1,128,640]{4,3,2,0,1:T(8,128)(2,1)S(1)}, u32[]{:S(2)}, u32[]{:S(2)}) async-start(bf16[1,6,1,128,640]{4,3,2,0,1:T(8,128)(2,1)} %copy.145), calls=%async_computation.6 | async-start | bytes 1966080 | tf_op jit(solution)/shard_map/all_to_all | solution.py:92
Sparse Core Ops, SparseCore 0:
  17.8 62.9 all-gather.2
  225.8 131.8 reduce-scatter.4
  360.1 18.3 reduce-scatter.6
where the time goes:
time: 398 us; the launch traced here: 396 us
  waiting for transfers between devices  170 us (43%)
  local copies, waits for them, and re-layouts  89.2 us (22%)
  matrix products  62.3 us (16%)
  starting transfers between devices  29.9 us (8%)
  blocking collectives  25.4 us (6%)
  between operations  14 us (4%)
  other arithmetic  5.81 us (1%)
    reduce_scatter x1, waiting for transfers between devices, body(): lax.psum_scatter(lax.dot_general(flat_att, flat_out, (((0,), (0,)), ((),...  107 us
    dynamic_slice x20, local copies, waits for them, and re-layouts, attend(): lax.map(pair_backward, (to_pairs(q_part), to_pairs(k_part), to_pairs(v_pa...  19.6 us
    unnamed x14, local copies, waits for them, and re-layouts  19.1 us
    sub x5, matrix products, pair_backward(): expd = jnp.exp(scores - top)  18.3 us
    all_gather x1, waiting for transfers between devices, body(): lax.all_gather(full_cols, ('band', 'obj'), axis=0, tiled=True)  16.8 us
    all_to_all x1, blocking collectives, body(): lax.all_to_all(head_att, 'cam', split_axis=1, concat_axis=4, tiled=True)  16.3 us
    dot_general x5, matrix products, pair_backward(): jnp.einsum('ghqk,gkhe->gqhe', probs_b, v_heads, preferred_element_type=jn...  15.8 us
    all_to_all x1, waiting for transfers between devices, body(): lax.all_to_all(keys, 'cam', split_axis=4, concat_axis=1, tiled=True)  12.7 us
  transfers between devices with their start and end apart: 10, of which 7 were waited for; matrix products, arithmetic and copies ran while one was open for 14% of the time, Pallas kernels for 0%

commit v1 on v0

v1 whole, which is shorter than its diff:
```python
import jax
import jax.numpy as jnp
from jax import lax
from jax.experimental import pallas as pl
from jax.experimental.pallas import tpu as pltpu
from jax.sharding import PartitionSpec as P

BF16, F32 = jnp.bfloat16, jnp.float32
HEAD = 64
PAIR = 2 * HEAD
SCALE = HEAD**-0.5
LOG2E = 1.4426950408889634
NT = (((1,), (1,)), ((), ()))
PARAMS = pltpu.CompilerParams(vmem_limit_bytes=48 * 2**20)


def mm(a, b):
    return jnp.dot(a, b, preferred_element_type=F32)


def nt(a, b):
    return lax.dot_general(a, b, NT, preferred_element_type=F32)


def stack_heads(x):
    lane = lax.broadcasted_iota(jnp.int32, x.shape, 1)
    zero = jnp.zeros_like(x)
    return jnp.concatenate([jnp.where(lane < HEAD, x, zero), jnp.where(lane < HEAD, zero, x)], 0)


def spread_heads(x):
    zero = jnp.zeros((HEAD, x.shape[1]), x.dtype)
    return jnp.concatenate(
        [jnp.concatenate([x[:HEAD], zero], 0), jnp.concatenate([zero, x[HEAD:]], 0)], 1
    )


def own_heads(x):
    n = x.shape[1] // 2
    return jnp.concatenate([x[:HEAD, :n], x[HEAD:, n:]], 0)


def pack_kernel(k_ref, v_ref, out_ref):
    n = k_ref.shape[0]
    out_ref[:n] = k_ref[...]
    out_ref[n:] = v_ref[...]


def pack(k, v, first, pairs):
    n = k.shape[0]
    return pl.pallas_call(
        pack_kernel,
        grid=(pairs,),
        in_specs=[pl.BlockSpec((n, PAIR), lambda i: (0, first + i))] * 2,
        out_specs=pl.BlockSpec((2 * n, PAIR), lambda i: (0, i)),
        out_shape=jax.ShapeDtypeStruct((2 * n, pairs * PAIR), BF16),
        compiler_params=PARAMS,
        name="pack",
    )(k, v)


def attend_kernel(q_ref, k_ref, v_ref, kv_ref, *refs):
    p_ref, att_ref = refs[-2:]
    n = q_ref.shape[0]
    k = jnp.concatenate([k_ref[...], kv_ref[:n]], 0)
    v = jnp.concatenate([v_ref[...], kv_ref[n:]], 0)
    s = nt(k, stack_heads(q_ref[...]))
    top = jnp.max(s, axis=0, keepdims=True)
    e = jnp.exp2((s - top) * (SCALE * LOG2E))
    p = e * (1.0 / jnp.sum(e, axis=0, keepdims=True))
    p_ref[0] = p
    att_ref[...] = own_heads(mm(v.T, p.astype(BF16))).astype(BF16)


def attend(q, k, v, kv, att, first, pairs):
    n, width = q.shape
    ins = [q, k, v, kv] + ([] if att is None else [att])
    specs = [pl.BlockSpec((n, PAIR), lambda i: (0, first + i))] * 3
    specs += [pl.BlockSpec((2 * n, PAIR), lambda i: (0, i))]
    specs += [pl.BlockSpec(memory_space=pl.ANY)] * (len(ins) - 4)
    return pl.pallas_call(
        attend_kernel,
        grid=(pairs,),
        in_specs=specs,
        out_specs=[
            pl.BlockSpec((1, 2 * n, 2 * n), lambda i: (i, 0, 0)),
            pl.BlockSpec((PAIR, n), lambda i: (first + i, 0)),
        ],
        out_shape=[
            jax.ShapeDtypeStruct((pairs, 2 * n, 2 * n), F32),
            jax.ShapeDtypeStruct((width, n), BF16),
        ],
        input_output_aliases={} if att is None else {4: 1},
        compiler_params=PARAMS,
        name="attend",
    )(*ins)


def back_kernel(p_ref, q_ref, k_ref, v_ref, kv_ref, d_ref, *refs):
    dq_ref, dk_ref, dv_ref, far_ref = refs[-4:]
    n = q_ref.shape[0]
    k = jnp.concatenate([k_ref[...], kv_ref[:n]], 0)
    v = jnp.concatenate([v_ref[...], kv_ref[n:]], 0)
    q = stack_heads(q_ref[...])
    d = spread_heads(d_ref[...])
    p = p_ref[0]
    dp = mm(v, d)
    delta = jnp.sum(p * dp, axis=0, keepdims=True)
    ds = (p * (dp - delta)).astype(BF16)
    dv = nt(p.astype(BF16), d)
    dk = mm(ds, q) * SCALE
    dq = own_heads(mm(k.T, ds)) * SCALE
    dq_ref[...] = dq.T.astype(BF16)
    dk_ref[...] = dk[:n]
    dv_ref[...] = dv[:n]
    far_ref[:n] = dk[n:].astype(BF16)
    far_ref[n:] = dv[n:].astype(BF16)


def back(p, q, k, v, kv, d, dq, first, pairs):
    n, width = q.shape
    ins = [p, q, k, v, kv, d] + ([] if dq is None else [dq])
    col = pl.BlockSpec((n, PAIR), lambda i: (0, first + i))
    own = pl.BlockSpec((n, PAIR), lambda i: (0, i))
    both = pl.BlockSpec((2 * n, PAIR), lambda i: (0, i))
    specs = [pl.BlockSpec((1, 2 * n, 2 * n), lambda i: (i, 0, 0)), col, col, col, both]
    specs += [pl.BlockSpec((PAIR, n), lambda i: (first + i, 0))]
    specs += [pl.BlockSpec(memory_space=pl.ANY)] * (len(ins) - 6)
    return pl.pallas_call(
        back_kernel,
        grid=(pairs,),
        in_specs=specs,
        out_specs=[col, own, own, both],
        out_shape=[
            jax.ShapeDtypeStruct((n, width), BF16),
            jax.ShapeDtypeStruct((n, pairs * PAIR), F32),
            jax.ShapeDtypeStruct((n, pairs * PAIR), F32),
            jax.ShapeDtypeStruct((2 * n, pairs * PAIR), BF16),
        ],
        input_output_aliases={} if dq is None else {6: 0},
        compiler_params=PARAMS,
        name="back",
    )(*ins)


def finish_kernel(dk_ref, dv_ref, far_ref, *refs):
    gk_ref, gv_ref = refs[-2:]
    n = dk_ref.shape[0]
    gk_ref[...] = (dk_ref[...] + far_ref[:n].astype(F32)).astype(BF16)
    gv_ref[...] = (dv_ref[...] + far_ref[n:].astype(F32)).astype(BF16)


def finish(dk, dv, far, grads, first, pairs, width):
    n = dk.shape[0]
    own = pl.BlockSpec((n, PAIR), lambda i: (0, i))
    specs = [own, own, pl.BlockSpec((2 * n, PAIR), lambda i: (0, i))]
    specs += [pl.BlockSpec(memory_space=pl.ANY)] * len(grads)
    return pl.pallas_call(
        finish_kernel,
        grid=(pairs,),
        in_specs=specs,
        out_specs=[pl.BlockSpec((n, PAIR), lambda i: (0, first + i))] * 2,
        out_shape=[jax.ShapeDtypeStruct((n, width), BF16)] * 2,
        input_output_aliases={3: 0, 4: 1} if grads else {},
        compiler_params=PARAMS,
        name="finish",
    )(dk, dv, far, *grads)


def project_kernel(slot_ref, w0, w1, w2, w3, own_ref, other_ref, out_own, out_other):
    rows = w0.shape[0]
    w = jnp.concatenate([w0[...], w1[...], w2[...], w3[...]], 0)
    for d_ref, out_ref in ((own_ref, out_own), (other_ref, out_other)):
        res = nt(w, d_ref[...]).astype(BF16)
        for j in range(4):
            out_ref[slot_ref[j]] = res[j * rows : (j + 1) * rows]


def project(slots, blocks, own, other):
    rows, depth = blocks[0].shape
    n = own.shape[0]
    whole = pl.BlockSpec(memory_space=pltpu.VMEM)
    return pl.pallas_call(
        project_kernel,
        in_specs=[pl.BlockSpec(memory_space=pltpu.SMEM)] + [whole] * 6,
        out_specs=[whole] * 2,
        out_shape=[jax.ShapeDtypeStruct((4, rows, n), BF16)] * 2,
        compiler_params=PARAMS,
        name="project",
    )(slots, *blocks, own, other)


def outer_kernel(slot_ref, a_own, a_other, d_own, d_other, o0, o1, o2, o3):
    rows = a_own.shape[1]
    left = [
        jnp.concatenate([ref[slot_ref[j]] for j in range(4)], 0) for ref in (a_own, a_other)
    ]
    res = (mm(left[0], d_own[...]) + mm(left[1], d_other[...])).astype(BF16)
    for j, ref in enumerate((o0, o1, o2, o3)):
        ref[...] = res[j * rows : (j + 1) * rows]


def outer(slots, a_own, a_other, d_own, d_other):
    rows, depth = a_own.shape[1], d_own.shape[1]
    whole = pl.BlockSpec(memory_space=pltpu.VMEM)
    return pl.pallas_call(
        outer_kernel,
        in_specs=[pl.BlockSpec(memory_space=pltpu.SMEM)] + [whole] * 4,
        out_specs=[whole] * 4,
        out_shape=[jax.ShapeDtypeStruct((rows, depth), BF16)] * 4,
        compiler_params=PARAMS,
        name="outer",
    )(slots, a_own, a_other, d_own, d_other)


def swap(x, axis, bit=1):
    size = lax.axis_size(axis)
    return lax.ppermute(x, axis, [(i, i ^ bit) for i in range(size)])


def shift(x, axis, step):
    size = lax.axis_size(axis)
    return lax.ppermute(x, axis, [(i, (i + step) % size) for i in range(size)])


def ordered(mine, theirs, flag, axis):
    return jnp.where(
        flag == 0,
        jnp.concatenate([mine, theirs], axis),
        jnp.concatenate([theirs, mine], axis),
    )


ORDER = (2, 1, 3, 0)


def body(queries, keys, values, d_out, w_out):
    shape = queries.shape
    width, model_width = shape[4], d_out.shape[4]
    n = shape[0] * shape[1] * shape[2] * shape[3]
    q, k, v = (x.reshape(n, width) for x in (queries, keys, values))
    flat = d_out.reshape(n, model_width)
    cams, bands, objs = (lax.axis_size(a) for a in ("cam", "band", "obj"))
    total = n * cams * bands * objs
    cam, band, obj = (lax.axis_index(a) for a in ("cam", "band", "obj"))
    core, line = obj % 2, obj // 2
    blocked = bands == 4 and objs == 4
    pairs = width // PAIR
    chunks = [(i, min(2, pairs - i)) for i in range(0, pairs, 2)]

    w_cols = ordered(w_out, swap(w_out, "cam"), cam, 1)
    sent = [swap(pack(k, v, first, count), "cam") for first, count in chunks]
    if blocked:
        flat_other = swap(flat, "obj")
        held = [shift(w_cols, "band", s) for s in ORDER[:3]] + [w_cols]
        passed = [swap(w, "obj", 2) for w in held]
        into = jnp.stack([(band - s) % 4 for s in ORDER]).astype(jnp.int32)

    att, probs = None, []
    for (first, count), kv in zip(chunks, sent):
        p, att = attend(q, k, v, kv, att, first, count)
        probs.append(p)

    if blocked:
        mine_o, mine_x = project(into, held, flat, flat_other)
        far_o, far_x = project(into, passed, flat, flat_other)
        got = swap(jnp.stack([mine_x, far_x], 1), "obj")
        got = got.reshape(4, 2, 1, -1, n)
        both = jnp.stack([mine_o, far_o], 1).reshape(4, 2, 1, -1, n)
        both = ordered(both, got, core, 2)
        both = jnp.where(line == 0, both, both[:, ::-1])
        d_att = both.reshape(width, n)
    else:
        full = lax.all_gather(w_cols, ("band", "obj"), axis=0, tiled=True)
        d_att = nt(full, flat).astype(BF16)

    dq, parts = None, []
    for (first, count), kv, p in zip(chunks, sent, probs):
        dq, dk, dv, far = back(p, q, k, v, kv, d_att, dq, first, count)
        parts.append((dk, dv, swap(far, "cam")))

    if blocked:
        rows = w_out.shape[0]
        blocks = att.reshape(bands * 2, 2, rows, n)
        a_own = lax.dynamic_index_in_dim(blocks, core, 1, keepdims=False)
        a_other = swap(lax.dynamic_index_in_dim(blocks, 1 - core, 1, keepdims=False), "obj")
        out_of = jnp.stack([(band + s) % 4 for s in ORDER]).astype(jnp.int32) * 2
        away = outer(out_of + 1 - line, a_own, a_other, flat, flat_other)
        stay = outer(out_of + line, a_own, a_other, flat, flat_other)
        sums = [a.astype(F32) + swap(b, "obj", 2).astype(F32) for a, b in zip(stay, away)]
        total_rows = sums[3]
        for s, x in zip(ORDER[:3], sums):
            total_rows = total_rows + shift(x.astype(BF16), "band", s).astype(F32)
    else:
        total_rows = lax.psum_scatter(mm(att, flat), ("band", "obj"), scatter_dimension=0, tiled=True)
    half = w_out.shape[1]
    left, right = total_rows[:, :half], total_rows[:, half:]
    mine = jnp.where(cam == 0, left, right)
    theirs = jnp.where(cam == 0, right, left).astype(BF16)
    grad_wo = (mine + swap(theirs, "cam").astype(F32)) * float(total) ** (-0.5)

    grads = []
    for (first, count), (dk, dv, far) in zip(chunks, parts):
        grads = finish(dk, dv, far, grads, first, count, width)
    return (dq.reshape(shape), grads[0].reshape(shape), grads[1].reshape(shape), grad_wo)


def solution(mesh):
    token = P("obj", "cam", "band", None, None)
    weight = P(("band", "obj"), "cam")
    return jax.shard_map(
        body,
        mesh=mesh,
        in_specs=(token, token, token, token, weight),
        out_specs=(token, token, token, weight),
        check_vma=False,
    )
```

time: 398 us -> 223 us (0.56)
  local copies, waits for them, and re-layouts: 89.2 us -> 10.4 us
  Pallas kernels: 0 us -> 72.6 us
  waiting for transfers between devices: 170 us -> 98.8 us
  matrix products: 62.3 us -> 0 us
  blocking collectives: 25.4 us -> 0 us
  between operations: 14 us -> 0.9 us
  starting transfers between devices: 29.9 us -> 34 us
    reduce_scatter x1 -> x0, waiting for transfers between devices: 107 us -> none  [body(): lax.psum_scatter(lax.dot_general(flat_att, flat_out, (((0,), (0,)), ((),...]
    ppermute x0 -> x29, waiting for transfers between devices: none -> 98.8 us  [the longest x23 68.7 us: swap(): return lax.ppermute(x, axis, [(i, i ^ bit) for i in range(size)])]
    pallas_call x0 -> x24, Pallas kernels: none -> 72.6 us  [the longest x5 27.5 us: back(): pl.pallas_call(back_kernel, grid=(pairs,), in_specs=specs, out_specs=[col...]
    all_to_all x7 -> x0, waiting for transfers between devices: 46 us -> none  [the longest x1 12.7 us: body(): lax.all_to_all(keys, 'cam', split_axis=4, concat_axis=1, tiled=True)]
    dot_general x27 -> x0, matrix products: 44 us -> none  [the longest x5 15.8 us: pair_backward(): jnp.einsum('ghqk,gkhe->gqhe', probs_b, v_heads, preferred_element_type=jn...]
    ppermute x0 -> x29, starting transfers between devices: none -> 34 us  [the longest x23 25.8 us: swap(): return lax.ppermute(x, axis, [(i, i ^ bit) for i in range(size)])]
    all_to_all x7 -> x0, starting transfers between devices: 29.6 us -> none  [the longest x1 4.55 us: body(): lax.all_to_all(values, 'cam', split_axis=4, concat_axis=1, tiled=True)]
    dynamic_slice x20 -> x0, local copies, waits for them, and re-layouts: 19.6 us -> none  [attend(): lax.map(pair_backward, (to_pairs(q_part), to_pairs(k_part), to_pairs(v_pa...]
  transfers between devices with their start and end apart: 10 -> 29, of which waited for: 7 -> 15; matrix products, arithmetic and copies ran while one was open for 14% -> 2% of each run, Pallas kernels for 0% -> 33%
where the time goes in v1:
time: 223 us; the launch traced here: 222 us
  waiting for transfers between devices  98.8 us (44%)
  Pallas kernels  72.6 us (33%)
  starting transfers between devices  34 us (15%)
  local copies, waits for them, and re-layouts  10.4 us (5%)
  other arithmetic  5.47 us (2%)
    ppermute x23, waiting for transfers between devices, swap(): return lax.ppermute(x, axis, [(i, i ^ bit) for i in range(size)])  68.7 us
    ppermute x6, waiting for transfers between devices, shift(): return lax.ppermute(x, axis, [(i, (i + step) % size) for i in range(size)])  30.1 us
    pallas_call x5, Pallas kernels, back(): pl.pallas_call(back_kernel, grid=(pairs,), in_specs=specs, out_specs=[col...  27.5 us
    ppermute x23, starting transfers between devices, swap(): return lax.ppermute(x, axis, [(i, i ^ bit) for i in range(size)])  25.8 us
    pallas_call x5, Pallas kernels, attend(): pl.pallas_call(attend_kernel, grid=(pairs,), in_specs=specs, out_specs=[p...  21.9 us
    unnamed x38, local copies, waits for them, and re-layouts  9.43 us
    ppermute x6, starting transfers between devices, shift(): return lax.ppermute(x, axis, [(i, (i + step) % size) for i in range(size)])  8.26 us
    pallas_call x2, Pallas kernels, project(): pl.pallas_call(project_kernel, in_specs=[pl.BlockSpec(memory_space=pltpu....  7.82 us
  transfers between devices with their start and end apart: 29, of which 15 were waited for; matrix products, arithmetic and copies ran while one was open for 2% of the time, Pallas kernels for 33%

profile of v1, /device:TPU:0, one launch (start us, length us, event | category | flops | bytes accessed | tf_op | source)
XLA Modules:
  0.0 222.2 jit_solution(12166032593104165041)
XLA Ops:
  11.3 4.9 %collective-permute-done.3.kv_ref = bf16[768,256]{1,0:T(8,128)(2,1)S(1)} collective-permute-done((bf16[768,256]{1,0:T(8,128)(2,1)S(1)}, bf16[768,256]{1,0:T(8,128)(2,1)S(1)}, u32[]{:S(2)}, u32[]{:S(2)}) %collective-permute-start.3) | collective-permute-done | bytes 393248 | tf_op jit(solution)/shard_map/ppermute | solution.py:218
  18.3 6.4 %collective-permute-done.4.kv_ref = bf16[768,256]{1,0:T(8,128)(2,1)S(1)} collective-permute-done((bf16[768,256]{1,0:T(8,128)(2,1)S(1)}, bf16[768,256]{1,0:T(8,128)(2,1)S(1)}, u32[]{:S(2)}, u32[]{:S(2)}) %collective-permute-start.4) | collective-permute-done | bytes 393248 | tf_op jit(solution)/shard_map/ppermute | solution.py:218
  28.5 3.9 %attend.5 = (f32[2,768,768]{2,1,0:T(8,128)}, bf16[1280,384]{1,0:T(8,128)(2,1)S(1)}) custom-call(bf16[384,1280]{1,0:T(8,128)(2,1)S(1)} %bitcast.67, bf16[384,1280]{1,0:T(8,128)(2,1)S(1)} %bitcast.42, bf16[384,1280]{1,0:T(8,128)(2,1)S(1)} %bitcast.57, bf16[768,256]{1,0:T(8,128)(2,1)S(1)} %copy-done.11), custom_call_target="tpu_custom_call" | custom-call | tf_op jit(solution)/shard_map/attend/pallas_call | solution.py:81
  32.3 3.9 %attend.6 = (f32[2,768,768]{2,1,0:T(8,128)}, bf16[1280,384]{1,0:T(8,128)(2,1)S(1)}) custom-call(bf16[384,1280]{1,0:T(8,128)(2,1)S(1)} %bitcast.68, bf16[384,1280]{1,0:T(8,128)(2,1)S(1)} %bitcast.43, bf16[384,1280]{1,0:T(8,128)(2,1)S(1)} %bitcast.58, bf16[768,256]{1,0:T(8,128)(2,1)S(1)} %collective-permute-done.3.kv_ref, ...), custom_call_target="tpu_custom_call", output_to_operand_aliasing={{1}: (4, {})} | custom-call | tf_op jit(solution)/shard_map/attend/pallas_call | solution.py:81
  36.2 4.7 %attend.7 = (f32[2,768,768]{2,1,0:T(8,128)}, bf16[1280,384]{1,0:T(8,128)(2,1)S(1)}) custom-call(bf16[384,1280]{1,0:T(8,128)(2,1)S(1)} %bitcast.69, bf16[384,1280]{1,0:T(8,128)(2,1)S(1)} %bitcast.44, bf16[384,1280]{1,0:T(8,128)(2,1)S(1)} %bitcast.59, bf16[768,256]{1,0:T(8,128)(2,1)} %collective-permute-done.2.kv_ref, ...), custom_call_target="tpu_custom_call", output_to_operand_aliasing={{1}: (4, {})} | custom-call | tf_op jit(solution)/shard_map/attend/pallas_call | solution.py:81
  41.6 4.7 %attend.8 = (f32[2,768,768]{2,1,0:T(8,128)}, bf16[1280,384]{1,0:T(8,128)(2,1)S(1)}) custom-call(bf16[384,1280]{1,0:T(8,128)(2,1)S(1)} %bitcast.70, bf16[384,1280]{1,0:T(8,128)(2,1)S(1)} %bitcast.45, bf16[384,1280]{1,0:T(8,128)(2,1)S(1)} %bitcast.60, bf16[768,256]{1,0:T(8,128)(2,1)} %collective-permute-done.1.kv_ref, ...), custom_call_target="tpu_custom_call", output_to_operand_aliasing={{1}: (4, {})} | custom-call | tf_op jit(solution)/shard_map/attend/pallas_call | solution.py:81
  50.0 4.7 %attend.9 = (f32[2,768,768]{2,1,0:T(8,128)}, bf16[1280,384]{1,0:T(8,128)(2,1)S(1)}) custom-call(bf16[384,1280]{1,0:T(8,128)(2,1)S(1)} %bitcast.71, bf16[384,1280]{1,0:T(8,128)(2,1)S(1)} %bitcast.46, bf16[384,1280]{1,0:T(8,128)(2,1)S(1)} %bitcast.61, bf16[768,256]{1,0:T(8,128)(2,1)} %collective-permute-done.kv_ref, ...), custom_call_target="tpu_custom_call", output_to_operand_aliasing={{1}: (4, {})} | custom-call | tf_op jit(solution)/shard_map/attend/pallas_call | solution.py:81
  57.8 4.2 %collective-permute-start.8 = (bf16[80,2432]{1,0:T(8,128)(2,1)}, bf16[80,2432]{1,0:T(8,128)(2,1)}, u32[]{:S(2)}, u32[]{:S(2)}) collective-permute-start(bf16[80,2432]{1,0:T(8,128)(2,1)} %maximum_select_fusion.1.w3), channel_id=1, source_target_pairs={{0,12},{4,0},{8,4},{12,8},{1,13},{5,1},{9,5},{13,9},{2,14},{6,2},{... | collective-permute-start | bytes 1167368 | tf_op jit(solution)/shard_map/ppermute | solution.py:223
  63.0 8.7 %collective-permute-done.8.w2 = bf16[80,2432]{1,0:T(8,128)(2,1)} collective-permute-done((bf16[80,2432]{1,0:T(8,128)(2,1)}, bf16[80,2432]{1,0:T(8,128)(2,1)}, u32[]{:S(2)}, u32[]{:S(2)}) %collective-permute-start.8) | collective-permute-done | bytes 389152 | tf_op jit(solution)/shard_map/ppermute | solution.py:223
  73.2 7.8 %collective-permute-done.7.w1 = bf16[80,2432]{1,0:T(8,128)(2,1)} collective-permute-done((bf16[80,2432]{1,0:T(8,128)(2,1)}, bf16[80,2432]{1,0:T(8,128)(2,1)}, u32[]{:S(2)}, u32[]{:S(2)}) %collective-permute-start.7) | collective-permute-done | bytes 389152 | tf_op jit(solution)/shard_map/ppermute | solution.py:223
  82.5 13.7 %collective-permute-done.6.w0 = bf16[80,2432]{1,0:T(8,128)(2,1)} collective-permute-done((bf16[80,2432]{1,0:T(8,128)(2,1)}, bf16[80,2432]{1,0:T(8,128)(2,1)}, u32[]{:S(2)}, u32[]{:S(2)}) %collective-permute-start.6) | collective-permute-done | bytes 389152 | tf_op jit(solution)/shard_map/ppermute | solution.py:223
  99.8 4.2 %outer.3 = (bf16[80,2432]{1,0:T(8,128)(2,1)}, bf16[80,2432]{1,0:T(8,128)(2,1)S(1)}, bf16[80,2432]{1,0:T(8,128)(2,1)S(1)}, bf16[80,2432]{1,0:T(8,128)(2,1)S(1)}) custom-call(s32[4]{0:T(128)S(1)} %add_subtract_fusion.slot_ref, bf16[8,80,384]{2,1,0:T(8,128)(2,1)S(1)} %get-tuple-element.115.a_own, bf16[8,80,384]{2,1,0:T(8,128)(2,1)} %collective-permute-done.20.a_other, ...), custom_call_target="tpu_custom_call" | custom-call | tf_op jit(solution)/shard_map/outer/pallas_call | solution.py:206
  109.4 4.0 %project.2 = (bf16[4,80,384]{2,1,0:T(8,128)(2,1)S(1)}, bf16[4,80,384]{2,1,0:T(8,128)(2,1)S(1)}) custom-call(s32[4]{0:T(128)S(1)} %add_add_fusion.slot_ref, bf16[80,2432]{1,0:T(8,128)(2,1)} %collective-permute-done.6.w0, bf16[80,2432]{1,0:T(8,128)(2,1)} %collective-permute-done.7.w1, bf16[80,2432]{1,0:T(8,128)(2,1)} %collective-permute-done.8.w2, ...), custom_call_target="tpu_custom_call" | custom-call | tf_op jit(solution)/shard_map/project/pallas_call | solution.py:183
  129.2 11.8 %collective-permute-done.24 = bf16[80,2432]{1,0:T(8,128)(2,1)S(1)} collective-permute-done((bf16[80,2432]{1,0:T(8,128)(2,1)S(1)}, bf16[80,2432]{1,0:T(8,128)(2,1)S(1)}, u32[]{:S(2)}, u32[]{:S(2)}) %collective-permute-start.24) | collective-permute-done | bytes 389152 | tf_op jit(solution)/shard_map/ppermute | solution.py:218
  141.2 7.7 %collective-permute-done.26 = bf16[80,2432]{1,0:T(8,128)(2,1)S(1)} collective-permute-done((bf16[80,2432]{1,0:T(8,128)(2,1)S(1)}, bf16[80,2432]{1,0:T(8,128)(2,1)S(1)}, u32[]{:S(2)}, u32[]{:S(2)}) %collective-permute-start.26) | collective-permute-done | bytes 389152 | tf_op jit(solution)/shard_map/ppermute | solution.py:218
  152.4 5.5 %back.5 = (bf16[384,1280]{1,0:T(8,128)(2,1)}, f32[384,256]{1,0:T(8,128)S(1)}, f32[384,256]{1,0:T(8,128)S(1)}, bf16[768,256]{1,0:T(8,128)(2,1)S(1)}) custom-call(f32[2,768,768]{2,1,0:T(8,128)} %get-tuple-element.68.p_ref, bf16[384,1280]{1,0:T(8,128)(2,1)S(1)} %bitcast.72, bf16[384,1280]{1,0:T(8,128)(2,1)S(1)} %bitcast.47, bf16[384,1280]{1,0:T(8,128)(2,1)S(1)} %bitcast.62, ...), custom_call_target="tpu_custom_call" | custom-call | tf_op jit(solution)/shard_map/back/pallas_call | solution.py:129
  159.5 5.5 %back.6 = (bf16[384,1280]{1,0:T(8,128)(2,1)}, f32[384,256]{1,0:T(8,128)S(1)}, f32[384,256]{1,0:T(8,128)S(1)}, bf16[768,256]{1,0:T(8,128)(2,1)S(1)}) custom-call(f32[2,768,768]{2,1,0:T(8,128)} %get-tuple-element.67.p_ref, bf16[384,1280]{1,0:T(8,128)(2,1)S(1)} %bitcast.73, bf16[384,1280]{1,0:T(8,128)(2,1)S(1)} %bitcast.48, ...), custom_call_target="tpu_custom_call", output_to_operand_aliasing={{0}: (6, {})} | custom-call | tf_op jit(solution)/shard_map/back/pallas_call | solution.py:129
  165.0 5.5 %back.7 = (bf16[384,1280]{1,0:T(8,128)(2,1)}, f32[384,256]{1,0:T(8,128)S(1)}, f32[384,256]{1,0:T(8,128)S(1)}, bf16[768,256]{1,0:T(8,128)(2,1)S(1)}) custom-call(f32[2,768,768]{2,1,0:T(8,128)} %get-tuple-element.66.p_ref, bf16[384,1280]{1,0:T(8,128)(2,1)S(1)} %bitcast.74, bf16[384,1280]{1,0:T(8,128)(2,1)S(1)} %bitcast.49, ...), custom_call_target="tpu_custom_call", output_to_operand_aliasing={{0}: (6, {})} | custom-call | tf_op jit(solution)/shard_map/back/pallas_call | solution.py:129
  170.5 5.5 %back.8 = (bf16[384,1280]{1,0:T(8,128)(2,1)}, f32[384,256]{1,0:T(8,128)S(1)}, f32[384,256]{1,0:T(8,128)S(1)}, bf16[768,256]{1,0:T(8,128)(2,1)S(1)}) custom-call(f32[2,768,768]{2,1,0:T(8,128)} %get-tuple-element.65.p_ref, bf16[384,1280]{1,0:T(8,128)(2,1)S(1)} %bitcast.75, bf16[384,1280]{1,0:T(8,128)(2,1)S(1)} %bitcast.50, ...), custom_call_target="tpu_custom_call", output_to_operand_aliasing={{0}: (6, {})} | custom-call | tf_op jit(solution)/shard_map/back/pallas_call | solution.py:129
  176.0 5.5 %back.9 = (bf16[384,1280]{1,0:T(8,128)(2,1)}, f32[384,256]{1,0:T(8,128)S(1)}, f32[384,256]{1,0:T(8,128)S(1)}, bf16[768,256]{1,0:T(8,128)(2,1)S(1)}) custom-call(f32[2,768,768]{2,1,0:T(8,128)} %get-tuple-element.60.p_ref, bf16[384,1280]{1,0:T(8,128)(2,1)S(1)} %bitcast.76, bf16[384,1280]{1,0:T(8,128)(2,1)S(1)} %bitcast.51, ...), custom_call_target="tpu_custom_call", output_to_operand_aliasing={{0}: (6, {})} | custom-call | tf_op jit(solution)/shard_map/back/pallas_call | solution.py:129
  187.5 6.1 %collective-permute-done.18.far_ref = bf16[768,256]{1,0:T(8,128)(2,1)S(1)} collective-permute-done((bf16[768,256]{1,0:T(8,128)(2,1)S(1)}, bf16[768,256]{1,0:T(8,128)(2,1)S(1)}, u32[]{:S(2)}, u32[]{:S(2)}) %collective-permute-start.18) | collective-permute-done | bytes 393248 | tf_op jit(solution)/shard_map/ppermute | solution.py:218
  194.4 7.5 %collective-permute-done.17.far_ref = bf16[768,256]{1,0:T(8,128)(2,1)S(1)} collective-permute-done((bf16[768,256]{1,0:T(8,128)(2,1)S(1)}, bf16[768,256]{1,0:T(8,128)(2,1)S(1)}, u32[]{:S(2)}, u32[]{:S(2)}) %collective-permute-start.17) | collective-permute-done | bytes 393248 | tf_op jit(solution)/shard_map/ppermute | solution.py:218
  202.9 7.5 %collective-permute-done.16.far_ref = bf16[768,256]{1,0:T(8,128)(2,1)S(1)} collective-permute-done((bf16[768,256]{1,0:T(8,128)(2,1)S(1)}, bf16[768,256]{1,0:T(8,128)(2,1)S(1)}, u32[]{:S(2)}, u32[]{:S(2)}) %collective-permute-start.16) | collective-permute-done | bytes 393248 | tf_op jit(solution)/shard_map/ppermute | solution.py:218
  211.3 7.5 %collective-permute-done.15.far_ref = bf16[768,256]{1,0:T(8,128)(2,1)S(1)} collective-permute-done((bf16[768,256]{1,0:T(8,128)(2,1)S(1)}, bf16[768,256]{1,0:T(8,128)(2,1)S(1)}, u32[]{:S(2)}, u32[]{:S(2)}) %collective-permute-start.15) | collective-permute-done | bytes 393248 | tf_op jit(solution)/shard_map/ppermute | solution.py:218
  (112 shorter events, 70.0 us)
Async XLA Ops:
  6.3 92.0 %collective-permute-start.9 = (bf16[384,2432]{1,0:T(8,128)(2,1)}, bf16[384,2432]{1,0:T(8,128)(2,1)}, u32[]{:S(2)}, u32[]{:S(2)}) collective-permute-start(bf16[384,2432]{1,0:T(8,128)(2,1)} %bitcast.82), channel_id=1, source_target_pairs={{0,1},{1,0},{2,3},{3,2},{4,5},{5,4},{6,7},{7,6},{8,9},{9,8},{10,11... | collective-permute-start | bytes 5603336 | tf_op jit(solution)/shard_map/ppermute | solution.py:218
  7.6 28.7 %collective-permute-start.2 = (bf16[768,256]{1,0:T(8,128)(2,1)}, bf16[768,256]{1,0:T(8,128)(2,1)}, u32[]{:S(2)}, u32[]{:S(2)}) collective-permute-start(bf16[768,256]{1,0:T(8,128)(2,1)} %pack.7), channel_id=1, source_target_pairs={{0,16},{16,0},{1,17},{17,1},{2,18},{18,2},{3,19},{19,3},{4,20},{20... | collective-permute-start | bytes 1179656 | tf_op jit(solution)/shard_map/ppermute | solution.py:218
  10.3 31.3 %collective-permute-start.1 = (bf16[768,256]{1,0:T(8,128)(2,1)}, bf16[768,256]{1,0:T(8,128)(2,1)}, u32[]{:S(2)}, u32[]{:S(2)}) collective-permute-start(bf16[768,256]{1,0:T(8,128)(2,1)} %pack.6), channel_id=1, source_target_pairs={{0,16},{16,0},{1,17},{17,1},{2,18},{18,2},{3,19},{19,3},{4,20},{20... | collective-permute-start | bytes 1179656 | tf_op jit(solution)/shard_map/ppermute | solution.py:218
  16.2 33.8 %collective-permute-start = (bf16[768,256]{1,0:T(8,128)(2,1)}, bf16[768,256]{1,0:T(8,128)(2,1)}, u32[]{:S(2)}, u32[]{:S(2)}) collective-permute-start(bf16[768,256]{1,0:T(8,128)(2,1)} %pack.5), channel_id=1, source_target_pairs={{0,16},{16,0},{1,17},{17,1},{2,18},{18,2},{3,19},{19,3},{4,20},{20... | collective-permute-start | bytes 1179656 | tf_op jit(solution)/shard_map/ppermute | solution.py:218
  25.4 30.3 %collective-permute-start.5 = (bf16[80,1216]{1,0:T(8,128)(2,1)}, bf16[80,1216]{1,0:T(8,128)(2,1)}, u32[]{:S(2)}, u32[]{:S(2)}) collective-permute-start(bf16[80,1216]{1,0:T(8,128)(2,1)} %param.9), channel_id=1, source_target_pairs={{0,16},{16,0},{1,17},{17,1},{2,18},{18,2},{3,19},{19,3},{4,20},{20... | collective-permute-start | bytes 583688 | tf_op jit(solution)/shard_map/ppermute | solution.py:218
  55.7 42.1 %collective-permute-start.20 = (bf16[8,80,384]{2,1,0:T(8,128)(2,1)}, bf16[8,80,384]{2,1,0:T(8,128)(2,1)}, u32[]{:S(2)}, u32[]{:S(2)}) collective-permute-start(bf16[8,80,384]{2,1,0:T(8,128)(2,1)} %get-tuple-element.114), channel_id=1, source_target_pairs={{0,1},{1,0},{2,3},{3,2},{4,5},{5,4},{6,7},{7,6},{8,9},{9,8},{10,11... | collective-permute-start | bytes 1474568 | tf_op jit(solution)/shard_map/ppermute | solution.py:218
  62.0 19.0 %collective-permute-start.7 = (bf16[80,2432]{1,0:T(8,128)(2,1)}, bf16[80,2432]{1,0:T(8,128)(2,1)}, u32[]{:S(2)}, u32[]{:S(2)}) collective-permute-start(bf16[80,2432]{1,0:T(8,128)(2,1)} %maximum_select_fusion.1.w3), channel_id=1, source_target_pairs={{0,4},{4,8},{8,12},{12,0},{1,5},{5,9},{9,13},{13,1},{2,6},{6,10},{... | collective-permute-start | bytes 1167368 | tf_op jit(solution)/shard_map/ppermute | solution.py:223
  62.0 34.2 %collective-permute-start.6 = (bf16[80,2432]{1,0:T(8,128)(2,1)}, bf16[80,2432]{1,0:T(8,128)(2,1)}, u32[]{:S(2)}, u32[]{:S(2)}) collective-permute-start(bf16[80,2432]{1,0:T(8,128)(2,1)} %maximum_select_fusion.1.w3), channel_id=1, source_target_pairs={{0,8},{4,12},{8,0},{12,4},{1,9},{5,13},{9,1},{13,5},{2,10},{6,14},... | collective-permute-start | bytes 1167368 | tf_op jit(solution)/shard_map/ppermute | solution.py:223
  71.7 41.7 %collective-permute-start.13 = (bf16[80,2432]{1,0:T(8,128)(2,1)}, bf16[80,2432]{1,0:T(8,128)(2,1)}, u32[]{:S(2)}, u32[]{:S(2)}) collective-permute-start(bf16[80,2432]{1,0:T(8,128)(2,1)} %maximum_select_fusion.1.w3), channel_id=1, source_target_pairs={{0,2},{1,3},{2,0},{3,1},{4,6},{5,7},{6,4},{7,5},{8,10},{9,11},{10,... | collective-permute-start | bytes 1167368 | tf_op jit(solution)/shard_map/ppermute | solution.py:218
  81.0 32.4 %collective-permute-start.12 = (bf16[80,2432]{1,0:T(8,128)(2,1)}, bf16[80,2432]{1,0:T(8,128)(2,1)}, u32[]{:S(2)}, u32[]{:S(2)}) collective-permute-start(bf16[80,2432]{1,0:T(8,128)(2,1)} %collective-permute-done.8.w2), channel_id=1, source_target_pairs={{0,2},{1,3},{2,0},{3,1},{4,6},{5,7},{6,4},{7,5},{8,10},{9,11},{10,... | collective-permute-start | bytes 1167368 | tf_op jit(solution)/shard_map/ppermute | solution.py:218
  97.7 19.1 %collective-permute-start.10 = (bf16[80,2432]{1,0:T(8,128)(2,1)}, bf16[80,2432]{1,0:T(8,128)(2,1)}, u32[]{:S(2)}, u32[]{:S(2)}) collective-permute-start(bf16[80,2432]{1,0:T(8,128)(2,1)} %collective-permute-done.6.w0), channel_id=1, source_target_pairs={{0,2},{1,3},{2,0},{3,1},{4,6},{5,7},{6,4},{7,5},{8,10},{9,11},{10,... | collective-permute-start | bytes 1167368 | tf_op jit(solution)/shard_map/ppermute | solution.py:218
  106.3 21.7 %collective-permute-start.22 = (bf16[80,2432]{1,0:T(8,128)(2,1)}, bf16[80,2432]{1,0:T(8,128)(2,1)}, u32[]{:S(2)}, u32[]{:S(2)}) collective-permute-start(bf16[80,2432]{1,0:T(8,128)(2,1)} %get-tuple-element.103), channel_id=1, source_target_pairs={{0,2},{1,3},{2,0},{3,1},{4,6},{5,7},{6,4},{7,5},{8,10},{9,11},{10,... | collective-permute-start | bytes 1167368 | tf_op jit(solution)/shard_map/ppermute | solution.py:218
  120.7 31.3 %collective-permute-start.14 = (bf16[4,2,80,384]{3,2,0,1:T(8,128)(2,1)S(1)}, bf16[4,2,80,384]{3,2,0,1:T(8,128)(2,1)S(1)}, u32[]{:S(2)}, u32[]{:S(2)}) collective-permute-start(bf16[4,2,80,384]{3,2,0,1:T(8,128)(2,1)S(1)} %pad_maximum_fusion), channel_id=1, source_target_pairs={{0,1},{1,0},{2,3},{3,2},{4,5},{5,4},{6,7},{7,6},{8,9},{9,8},{10,11... | collective-permute-start | bytes 1474568 | tf_op jit(solution)/shard_map/ppermute | solution.py:218
  120.8 60.7 %collective-permute-start.21 = (bf16[80,2432]{1,0:T(8,128)(2,1)S(1)}, bf16[80,2432]{1,0:T(8,128)(2,1)S(1)}, u32[]{:S(2)}, u32[]{:S(2)}) collective-permute-start(bf16[80,2432]{1,0:T(8,128)(2,1)S(1)} %copy-done.14), channel_id=1, source_target_pairs={{0,2},{1,3},{2,0},{3,1},{4,6},{5,7},{6,4},{7,5},{8,10},{9,11},{10,... | collective-permute-start | bytes 1167368 | tf_op jit(solution)/shard_map/ppermute | solution.py:218
  122.4 18.6 %collective-permute-start.24 = (bf16[80,2432]{1,0:T(8,128)(2,1)S(1)}, bf16[80,2432]{1,0:T(8,128)(2,1)S(1)}, u32[]{:S(2)}, u32[]{:S(2)}) collective-permute-start(bf16[80,2432]{1,0:T(8,128)(2,1)S(1)} %copy-done.18), channel_id=1, source_target_pairs={{0,2},{1,3},{2,0},{3,1},{4,6},{5,7},{6,4},{7,5},{8,10},{9,11},{10,... | collective-permute-start | bytes 1167368 | tf_op jit(solution)/shard_map/ppermute | solution.py:218
  122.9 26.0 %collective-permute-start.26 = (bf16[80,2432]{1,0:T(8,128)(2,1)S(1)}, bf16[80,2432]{1,0:T(8,128)(2,1)S(1)}, u32[]{:S(2)}, u32[]{:S(2)}) collective-permute-start(bf16[80,2432]{1,0:T(8,128)(2,1)S(1)} %copy-done.16), channel_id=1, source_target_pairs={{0,2},{1,3},{2,0},{3,1},{4,6},{5,7},{6,4},{7,5},{8,10},{9,11},{10,... | collective-permute-start | bytes 1167368 | tf_op jit(solution)/shard_map/ppermute | solution.py:218
  129.2 52.8 %collective-permute-start.23 = (bf16[80,2432]{1,0:T(8,128)(2,1)S(1)}, bf16[80,2432]{1,0:T(8,128)(2,1)S(1)}, u32[]{:S(2)}, u32[]{:S(2)}) collective-permute-start(bf16[80,2432]{1,0:T(8,128)(2,1)S(1)} %add_convert_fusion.2), channel_id=1, source_target_pairs={{0,8},{4,12},{8,0},{12,4},{1,9},{5,13},{9,1},{13,5},{2,10},{6,14},... | collective-permute-start | bytes 1167368 | tf_op jit(solution)/shard_map/ppermute | solution.py:223
  141.1 42.4 %collective-permute-start.25 = (bf16[80,2432]{1,0:T(8,128)(2,1)S(1)}, bf16[80,2432]{1,0:T(8,128)(2,1)S(1)}, u32[]{:S(2)}, u32[]{:S(2)}) collective-permute-start(bf16[80,2432]{1,0:T(8,128)(2,1)S(1)} %add_convert_fusion.1), channel_id=1, source_target_pairs={{0,4},{4,8},{8,12},{12,0},{1,5},{5,9},{9,13},{13,1},{2,6},{6,10},{... | collective-permute-start | bytes 1167368 | tf_op jit(solution)/shard_map/ppermute | solution.py:223
  149.0 35.1 %collective-permute-start.27 = (bf16[80,2432]{1,0:T(8,128)(2,1)S(1)}, bf16[80,2432]{1,0:T(8,128)(2,1)S(1)}, u32[]{:S(2)}, u32[]{:S(2)}) collective-permute-start(bf16[80,2432]{1,0:T(8,128)(2,1)S(1)} %add_convert_fusion), channel_id=1, source_target_pairs={{0,12},{4,0},{8,4},{12,8},{1,13},{5,1},{9,5},{13,9},{2,14},{6,2},{... | collective-permute-start | bytes 1167368 | tf_op jit(solution)/shard_map/ppermute | solution.py:223
  158.0 28.0 %collective-permute-start.19 = (bf16[768,256]{1,0:T(8,128)(2,1)S(1)}, bf16[768,256]{1,0:T(8,128)(2,1)S(1)}, u32[]{:S(2)}, u32[]{:S(2)}) collective-permute-start(bf16[768,256]{1,0:T(8,128)(2,1)S(1)} %get-tuple-element.88), channel_id=1, source_target_pairs={{0,16},{16,0},{1,17},{17,1},{2,18},{18,2},{3,19},{19,3},{4,20},{20... | collective-permute-start | bytes 1179656 | tf_op jit(solution)/shard_map/ppermute | solution.py:218
  182.0 19.9 %collective-permute-start.17 = (bf16[768,256]{1,0:T(8,128)(2,1)S(1)}, bf16[768,256]{1,0:T(8,128)(2,1)S(1)}, u32[]{:S(2)}, u32[]{:S(2)}) collective-permute-start(bf16[768,256]{1,0:T(8,128)(2,1)S(1)} %get-tuple-element.82), channel_id=1, source_target_pairs={{0,16},{16,0},{1,17},{17,1},{2,18},{18,2},{3,19},{19,3},{4,20},{20... | collective-permute-start | bytes 1179656 | tf_op jit(solution)/shard_map/ppermute | solution.py:218
  183.5 26.9 %collective-permute-start.16 = (bf16[768,256]{1,0:T(8,128)(2,1)S(1)}, bf16[768,256]{1,0:T(8,128)(2,1)S(1)}, u32[]{:S(2)}, u32[]{:S(2)}) collective-permute-start(bf16[768,256]{1,0:T(8,128)(2,1)S(1)} %get-tuple-element.79), channel_id=1, source_target_pairs={{0,16},{16,0},{1,17},{17,1},{2,18},{18,2},{3,19},{19,3},{4,20},{20... | collective-permute-start | bytes 1179656 | tf_op jit(solution)/shard_map/ppermute | solution.py:218
  184.0 34.8 %collective-permute-start.15 = (bf16[768,256]{1,0:T(8,128)(2,1)S(1)}, bf16[768,256]{1,0:T(8,128)(2,1)S(1)}, u32[]{:S(2)}, u32[]{:S(2)}) collective-permute-start(bf16[768,256]{1,0:T(8,128)(2,1)S(1)} %get-tuple-element.76), channel_id=1, source_target_pairs={{0,16},{16,0},{1,17},{17,1},{2,18},{18,2},{3,19},{19,3},{4,20},{20... | collective-permute-start | bytes 1179656 | tf_op jit(solution)/shard_map/ppermute | solution.py:218
  185.9 35.3 %collective-permute-start.28 = (bf16[80,1216]{1,0:T(8,128)(2,1)S(1)}, bf16[80,1216]{1,0:T(8,128)(2,1)S(1)}, u32[]{:S(2)}, u32[]{:S(2)}) collective-permute-start(bf16[80,1216]{1,0:T(8,128)(2,1)S(1)} %select_convert_fusion), channel_id=1, source_target_pairs={{0,16},{16,0},{1,17},{17,1},{2,18},{18,2},{3,19},{19,3},{4,20},{20... | collective-permute-start | bytes 583688 | tf_op jit(solution)/shard_map/ppermute | solution.py:218
  (24 other events, 248.5 us)

commit v2 on v1

v2 whole, which is shorter than its diff:
```python
import jax
import jax.numpy as jnp
from jax import lax
from jax.experimental import pallas as pl
from jax.experimental.pallas import tpu as pltpu
from jax.sharding import PartitionSpec as P

BF16, F32 = jnp.bfloat16, jnp.float32
HEAD = 64
PAIR = 2 * HEAD
SCALE = HEAD**-0.5
LOG2E = 1.4426950408889634
NT = (((1,), (1,)), ((), ()))
ANY = pl.BlockSpec(memory_space=pl.ANY)
VMEM = pl.BlockSpec(memory_space=pltpu.VMEM)
SMEM = pl.BlockSpec(memory_space=pltpu.SMEM)
TOKEN = (8, 128)
BIG = 60
FLOPS_PER_US = 1150e6 * 0.5
CHUNKS = (4, 4, 2)
PARTS = 2


def mm(a, b):
    return jnp.dot(a, b, preferred_element_type=F32)


def nt(a, b):
    return lax.dot_general(a, b, NT, preferred_element_type=F32)


def run(kernel, name, ins, in_specs, outs, out_specs, grid=(), after=(), alias=(), scratch=(), us=1, vmem=24, slots=None):
    hold = [*alias, *after]
    n_slots, n_in, n_hold, n_out = int(slots is not None), len(ins), len(hold), len(outs)

    def wrapped(*refs):
        last = n_slots + n_in + n_hold + n_out
        kernel(*refs[: n_slots + n_in], *refs[last - n_out : last], *refs[last + 1 :])
        refs[last][...] = jnp.zeros(TOKEN, F32)

    token_spec = pl.BlockSpec(TOKEN, lambda *_: (0, 0)) if grid else VMEM
    *results, token = pl.pallas_call(
        wrapped,
        grid_spec=pltpu.PrefetchScalarGridSpec(
            num_scalar_prefetch=n_slots,
            grid=grid,
            in_specs=[*in_specs, *[ANY] * n_hold],
            out_specs=[*out_specs, token_spec],
            scratch_shapes=list(scratch),
        ),
        out_shape=[*[jax.ShapeDtypeStruct(s, t) for s, t in outs], jax.ShapeDtypeStruct(TOKEN, F32)],
        input_output_aliases={n_slots + n_in + i: i for i in range(len(alias))},
        compiler_params=pltpu.CompilerParams(vmem_limit_bytes=vmem * 2**20),
        cost_estimate=pl.CostEstimate(flops=int(us * FLOPS_PER_US), transcendentals=0, bytes_accessed=0),
        name=name,
    )(*([] if slots is None else [slots]), *ins, *hold)
    return results, token


def whole(x):
    shape = x if isinstance(x, tuple) else x.shape
    return pl.BlockSpec(shape, lambda *_: (0,) * len(shape))


def stack_heads(x):
    lane = lax.broadcasted_iota(jnp.int32, x.shape, 1)
    zero = jnp.zeros_like(x)
    return jnp.concatenate([jnp.where(lane < HEAD, x, zero), jnp.where(lane < HEAD, zero, x)], 0)


def spread_heads(x):
    zero = jnp.zeros((HEAD, x.shape[1]), x.dtype)
    return jnp.concatenate(
        [jnp.concatenate([x[:HEAD], zero], 0), jnp.concatenate([zero, x[HEAD:]], 0)], 1
    )


def own_heads(x):
    n = x.shape[1] // 2
    return jnp.concatenate([x[:HEAD, :n], x[HEAD:, n:]], 0)


def column(n, first):
    return pl.BlockSpec((n, PAIR), lambda i: (0, first + i))


def pack_kernel(k_ref, v_ref, out_ref):
    n = k_ref.shape[0]
    out_ref[:n] = k_ref[...]
    out_ref[n:] = v_ref[...]


def pack(k, v, first, pairs, after):
    n = k.shape[0]
    (out,), token = run(
        pack_kernel, "pack", [k, v], [column(n, first)] * 2,
        [((2 * n, pairs * PAIR), BF16)], [column(2 * n, 0)], (pairs,), after, us=pairs * 0.4,
    )
    return out, token


def attend_kernel(q_ref, k_ref, v_ref, kv_ref, att_ref, p_ref, stat_ref, far_ref):
    n = q_ref.shape[0]
    k = jnp.concatenate([k_ref[...], kv_ref[:n]], 0)
    v = jnp.concatenate([v_ref[...], kv_ref[n:]], 0)
    s = nt(k, stack_heads(q_ref[...]))
    top = jnp.max(s, axis=0, keepdims=True)
    e = jnp.exp2((s - top) * (SCALE * LOG2E))
    p_ref[0] = e
    inverse = 1.0 / jnp.sum(e, axis=0, keepdims=True)
    stat_ref[0] = jnp.concatenate([top, inverse], 0)
    att_ref[...] = own_heads(mm(v.T, e.astype(BF16)) * inverse).astype(BF16)
    far_ref[...] = kv_ref[...]


def attend(q, k, v, kv, state, first, pairs, after):
    n, width = q.shape
    count = width // PAIR
    at = lambda *block: pl.BlockSpec((1, *block), lambda i: (first + i, 0, 0))
    return run(
        attend_kernel, "attend",
        [q, k, v, kv], [column(n, first)] * 3 + [column(2 * n, 0)],
        [
            ((width, n), BF16), ((count, 2 * n, 2 * n), F32),
            ((count, 2, 2 * n), F32), ((2 * n, width), BF16),
        ],
        [pl.BlockSpec((PAIR, n), lambda i: (first + i, 0)), at(2 * n, 2 * n), at(2, 2 * n), column(2 * n, first)],
        (pairs,), after, state, us=1.9 * pairs, vmem=BIG,
    )


def back_kernel(p_ref, stat_ref, q_ref, k_ref, v_ref, kv_ref, d_ref, dq_ref, dk_ref, dv_ref, out_ref):
    n = q_ref.shape[0]
    k = jnp.concatenate([k_ref[...], kv_ref[:n]], 0)
    v = jnp.concatenate([v_ref[...], kv_ref[n:]], 0)
    q = stack_heads(q_ref[...])
    d = spread_heads(d_ref[...])
    p = p_ref[0] * stat_ref[0, 1:]
    dp = mm(v, d)
    delta = jnp.sum(p * dp, axis=0, keepdims=True)
    ds = (p * (dp - delta)).astype(BF16)
    dv_ref[...] = nt(p[:n].astype(BF16), d)
    dk_ref[...] = mm(ds[:n], q)
    dq_ref[...] = (own_heads(mm(k.T, ds)) * SCALE).T.astype(BF16)
    out_ref[0] = jnp.concatenate([stat_ref[0], delta], 0)


def back(state, q, k, v, d, done, first, pairs, after):
    n, width = q.shape
    _, p, stat, kv = state
    at = lambda *block: pl.BlockSpec((1, *block), lambda i: (first + i, 0, 0))
    return run(
        back_kernel, "back",
        [p, stat, q, k, v, kv, d],
        [at(2 * n, 2 * n), at(2, 2 * n)]
        + [column(n, first)] * 3
        + [column(2 * n, first), pl.BlockSpec((PAIR, n), lambda i: (first + i, 0))],
        [((n, width), BF16)] + [((n, width), F32)] * 2 + [((width // PAIR, 3, 2 * n), F32)],
        [column(n, first)] * 3 + [at(3, 2 * n)],
        (pairs,), after, done, us=2 * pairs, vmem=BIG,
    )


def cross_kernel(q_ref, k_ref, v_ref, d_ref, stat_ref, dk_ref, dv_ref, gk_ref, gv_ref):
    q = stack_heads(q_ref[...])
    d = spread_heads(d_ref[...])
    top, inverse, delta = (stat_ref[0, i : i + 1] for i in range(3))
    p = jnp.exp2((nt(k_ref[...], q) - top) * (SCALE * LOG2E)) * inverse
    ds = (p * (mm(v_ref[...], d) - delta)).astype(BF16)
    gv_ref[...] = (nt(p.astype(BF16), d) + dv_ref[...]).astype(BF16)
    gk_ref[...] = ((mm(ds, q) + dk_ref[...]) * SCALE).astype(BF16)


def cross(q, k, v, d, share, after):
    n, width = q.shape
    pairs = width // PAIR
    dk, dv, stat = share
    return run(
        cross_kernel, "cross",
        [q, k, v, d, stat, dk, dv],
        [column(n, 0)] * 3
        + [pl.BlockSpec((PAIR, n), lambda i: (i, 0)), pl.BlockSpec((1, 3, 2 * n), lambda i: (i, 0, 0))]
        + [column(n, 0)] * 2,
        [((n, width), BF16)] * 2, [column(n, 0)] * 2, (pairs,), after, us=1.5 * pairs,
    )


def join(cam, mine, far, after):
    rows, half = mine.shape

    def kernel(cam_ref, mine_ref, far_ref, out_ref):
        for c, (left, right) in enumerate(((mine_ref, far_ref), (far_ref, mine_ref))):

            @pl.when(cam_ref[0] == c)
            def _():
                out_ref[:, :half] = left[...]
                out_ref[:, half:] = right[...]

    (out,), token = run(
        kernel, "join", [cam.reshape(1), mine, far], [SMEM, whole(mine), whole(far)],
        [((rows, 2 * half), BF16)], [whole((rows, 2 * half))], (1,), after,
    )
    return out, token


def copy_kernel(x_ref, out_ref):
    out_ref[...] = x_ref[...]


def copy(x, after):
    rows, width = x.shape
    steps = 4 if rows % 64 == 0 else 1
    block = pl.BlockSpec((rows // steps, width), lambda i: (i, 0))
    (out,), token = run(
        copy_kernel, "copy", [x], [block], [(x.shape, x.dtype)], [block], (steps,), after, us=1
    )
    return out, token


def project(slots, w, own, other, after):
    rows, depth = w[0].shape
    n, count = own.shape[0], len(w)

    def kernel(slot_ref, *refs):
        left = jnp.concatenate([r[...] for r in refs[:count]], 0)
        for ref, out in zip(refs[count : count + 2], refs[count + 2 :]):
            res = nt(left, ref[...]).astype(BF16)
            for j in range(count):
                out[slot_ref[j]] = res[j * rows : (j + 1) * rows]

    tokens = pl.BlockSpec((PAIR, depth), lambda i, _: (i, 0))
    return run(
        kernel, "project", [*w, own, other],
        [pl.BlockSpec((rows, depth), lambda i, _: (0, 0))] * count + [tokens] * 2,
        [((count, rows, n), BF16)] * 2, [pl.BlockSpec((count, rows, PAIR), lambda i, _: (0, 0, i))] * 2,
        (n // PAIR,), after, slots=slots, us=6,
    )


def weave(core, mine, theirs, sizes, after):
    count, rows, n = mine.shape

    def kernel(core_ref, mine_ref, theirs_ref, *outs):
        for c, (even, odd) in enumerate(((mine_ref, theirs_ref), (theirs_ref, mine_ref))):

            @pl.when(core_ref[0] == c)
            def _():
                first = 0
                for out in outs:
                    last = first + out.shape[0]
                    row = first
                    while row < last:
                        block, offset = row // rows, row % rows
                        size = min(rows - offset, last - row)
                        src = (even, odd)[block % 2]
                        out[row - first : row - first + size] = src[block // 2, offset : offset + size]
                        row += size
                    first = last

    return run(
        kernel, "weave", [core.reshape(1), mine, theirs], [SMEM, whole(mine), whole(theirs)],
        [((s * PAIR, n), BF16) for s in sizes], [whole((s * PAIR, n)) for s in sizes], (1,), after, us=2,
    )


def outer(slots, a_own, a_other, own, other, groups, after):
    _, rows, n = a_own.shape
    depth = own.shape[1]
    count, tile = sum(groups), 5 * PAIR

    def kernel(slot_ref, *refs):
        mine, theirs, (own_ref, other_ref), outs = refs[:count], refs[count : 2 * count], refs[2 * count : 2 * count + 2], refs[2 * count + 2 :]
        left = [jnp.concatenate([r[0] for r in part], 0) for part in (mine, theirs)]
        res = (mm(left[0], own_ref[...]) + mm(left[1], other_ref[...])).astype(BF16)
        first = 0
        for out in outs:
            for j in range(out.shape[0]):
                out[j] = res[(first + j) * rows : (first + j + 1) * rows]
            first += out.shape[0]

    blocks = [pl.BlockSpec((1, rows, n), lambda i, slot, j=j: (slot[j], 0, 0)) for j in range(count)]
    return run(
        kernel, "outer", [a_own] * count + [a_other] * count + [own, other],
        blocks * 2 + [pl.BlockSpec((n, tile), lambda i, _: (0, i))] * 2,
        [((g, rows, depth), BF16) for g in groups],
        [pl.BlockSpec((g, rows, tile), lambda i, _: (0, 0, i)) for g in groups],
        (pl.cdiv(depth, tile),), after, slots=slots, us=6,
    )


def add_kernel(x_ref, y_ref, *outs):
    for j, out in enumerate(outs):
        out[...] = (x_ref[j].astype(F32) + y_ref[j].astype(F32)).astype(out.dtype)


def add(x, y, dtype, after):
    count, *block = x.shape
    return run(
        add_kernel, "add", [x, y], [whole(x), whole(y)], [(tuple(block), dtype)] * count,
        [whole(tuple(block))] * count, (1,), after,
    )


def total_of(cam, parts, after):
    rows, width = parts[0].shape
    half = width // 2

    def kernel(cam_ref, *refs):
        *refs, mine, theirs = refs
        total = refs[0][...].astype(F32)
        for ref in refs[1:]:
            total += ref[...].astype(F32)
        left, right = total[:, :half], total[:, half:]
        for c, (x, y) in enumerate(((left, right), (right, left))):

            @pl.when(cam_ref[0] == c)
            def _():
                mine[...] = x
                theirs[...] = y.astype(BF16)

    return run(
        kernel, "total", [cam.reshape(1), *parts], [SMEM] + [whole(x) for x in parts],
        [((rows, half), F32), ((rows, half), BF16)], [whole((rows, half))] * 2, (1,), after,
    )


def last_sum(mine, theirs, scale, after):
    def kernel(x_ref, y_ref, out_ref):
        out_ref[...] = (x_ref[...] + y_ref[...].astype(F32)) * scale

    (out,), _ = run(
        kernel, "scale", [mine, theirs], [whole(mine)] * 2, [(mine.shape, F32)], [whole(mine)], (1,), after,
    )
    return out


def swap(x, axis, bit=1):
    size = lax.axis_size(axis)
    return lax.ppermute(x, axis, [(i, i ^ bit) for i in range(size)])


def shift(x, axis, step):
    size = lax.axis_size(axis)
    return lax.ppermute(x, axis, [(i, (i + step) % size) for i in range(size)])


def ordered(mine, theirs, flag, axis):
    return jnp.where(
        flag == 0,
        jnp.concatenate([mine, theirs], axis),
        jnp.concatenate([theirs, mine], axis),
    )


ORDER = (2, 1, 3, 0)


def body(queries, keys, values, d_out, w_out):
    shape = queries.shape
    width, model_width = shape[4], d_out.shape[4]
    n = shape[0] * shape[1] * shape[2] * shape[3]
    q, k, v = (x.reshape(n, width) for x in (queries, keys, values))
    flat = d_out.reshape(n, model_width)
    cams, bands, objs = (lax.axis_size(a) for a in ("cam", "band", "obj"))
    total = n * cams * bands * objs
    cam, band, obj = (lax.axis_index(a) for a in ("cam", "band", "obj"))
    core, line = obj % 2, obj // 2
    rows, half = w_out.shape
    blocked = bands == 4 and objs == 4
    sizes = CHUNKS if sum(CHUNKS) * PAIR == width else (1,) * (width // PAIR)
    chunks = [(sum(sizes[:i]), c) for i, c in enumerate(sizes)]

    scale = float(total) ** (-0.5)
    w_far = swap(w_out, "cam")
    sent, token = [], ()

    def send(i, after):
        packed, token = pack(k, v, *chunks[i], after)
        sent.append(swap(packed, "cam"))
        return (token,)

    def forward(i, state, after):
        state, token = attend(q, k, v, sent[i], state, *chunks[i], after)
        return state, (token,)

    def backward(i, dq, after):
        (dq, *share), token = back(state, q, k, v, d_att, dq, *parts[i], after)
        return (dq, *share), (token,)

    pairs = width // PAIR
    cuts = [pairs * i // PARTS for i in range(PARTS + 1)]
    parts = [(a, b - a) for a, b in zip(cuts, cuts[1:])]
    state, dq = (), ()
    if blocked and len(chunks) == 3 and PARTS == 2:
        flat_other = swap(flat, "obj")
        into = [2 * ((band - s) % 4) + line for s in ORDER] + [2 * ((band - s) % 4) + 1 - line for s in ORDER]
        into = jnp.stack(into).astype(jnp.int32)
        out_of = [4 * ((band + s) % 4) + 2 * (1 - line) + core for s in ORDER]
        out_of += [4 * ((band + s) % 4) + 2 * line + core for s in ORDER]
        out_of = jnp.stack(out_of).astype(jnp.int32)

        w_cols, token = join(cam, w_out, w_far, (flat_other,))
        after = send(0, (token,))
        held = [shift(w_cols, "band", s) for s in ORDER[:3]]
        passed = [None, None, None, swap(w_cols, "obj", 2)]

        def forward_w(j, after):
            x, token = copy(held[j], after)
            passed[j] = swap(x, "obj", 2)
            return (token,)

        after = send(1, (*after, passed[3]))
        state, after = forward(0, state, after)
        after = forward_w(0, after)
        after = send(2, after)
        after = forward_w(1, after)
        state, after = forward(1, state, (*after, passed[0]))
        x, token = copy(q, after)
        q_far = swap(x, "cam")
        after = forward_w(2, (token,))
        state, after = forward(2, state, (*after, passed[1]))

        a_own = state[0].reshape(bands * objs, rows, n)
        a_other = swap(a_own, "obj")
        (*away, stay), token = outer(out_of, a_own, a_other, flat, flat_other, (1, 2, 1, 4), after)
        away = [swap(x, "obj", 2) for x in away]
        (mine, theirs), token = project(into, [*held, w_cols, *passed], flat, flat_other, (token,))
        theirs = swap(theirs, "obj")
        (d_att,), token = weave(core, mine, theirs, [pairs], (token,))
        d_far = swap(d_att, "cam")
        (x,), token = add(stay[:1], away[0], BF16, (token, q_far))
        sums = [shift(x, "band", ORDER[0])]
        dq, after = backward(0, dq, (token,))
        (x, y), token = add(stay[1:3], away[1], BF16, after)
        sums += [shift(x, "band", ORDER[1]), shift(y, "band", ORDER[2])]
        (base,), token = add(stay[3:], away[2], F32, (token,))
        (dq, *share), after = backward(1, dq, (token,))
        share[2] = swap(share[2], "cam")
        (*grads,), token = cross(q_far, k, v, d_far, share, (*after, sums[0]))
        (mine, theirs), token = total_of(cam, [base, *sums], (token,))
        theirs = swap(theirs, "cam")
    else:
        after, q_far = (), swap(q, "cam")
        for i in range(len(chunks)):
            after = send(i, after)
        for i in range(len(chunks)):
            state, after = forward(i, state, after)
        full = lax.all_gather(ordered(w_out, w_far, cam, 1), ("band", "obj"), axis=0, tiled=True)
        d_att = nt(full, flat).astype(BF16)
        d_far = swap(d_att, "cam")
        for i in range(PARTS):
            dq, after = backward(i, dq, after)
        dq, *share = dq
        share[2] = swap(share[2], "cam")
        (*grads,), token = cross(q_far, k, v, d_far, share, after)
        sums = lax.psum_scatter(mm(state[0], flat), ("band", "obj"), scatter_dimension=0, tiled=True)
        mine = jnp.where(cam == 0, sums[:, :half], sums[:, half:])
        theirs = jnp.where(cam == 0, sums[:, half:], sums[:, :half])
        theirs = swap(theirs.astype(BF16), "cam")
    grad_wo = last_sum(mine, theirs, scale, (token,))
    return (dq.reshape(shape), grads[0].reshape(shape), grads[1].reshape(shape), grad_wo)


def solution(mesh):
    token = P("obj", "cam", "band", None, None)
    weight = P(("band", "obj"), "cam")
    return jax.shard_map(
        body,
        mesh=mesh,
        in_specs=(token, token, token, token, weight),
        out_specs=(token, token, token, weight),
        check_vma=False,
    )
```

time: 223 us -> 171 us (0.77)
  waiting for transfers between devices: 98.8 us -> 50.7 us
  starting transfers between devices: 34 us -> 28.2 us
  other arithmetic: 5.47 us -> 0 us
  local copies, waits for them, and re-layouts: 10.4 us -> 14.8 us
  Pallas kernels: 72.6 us -> 75 us
    ppermute x6, waiting for transfers between devices: 30.1 us -> 2.28 us  [shift(): return lax.ppermute(x, axis, [(i, (i + step) % size) for i in range(size)])]
    ppermute x23 -> x18, waiting for transfers between devices: 68.7 us -> 48.4 us  [swap(): return lax.ppermute(x, axis, [(i, i ^ bit) for i in range(size)])]
    ppermute x23 -> x18, starting transfers between devices: 25.8 us -> 16.3 us  [swap(): return lax.ppermute(x, axis, [(i, i ^ bit) for i in range(size)])]
    unnamed x38 -> x76, local copies, waits for them, and re-layouts: 9.43 us -> 14.5 us
    ppermute x6, starting transfers between devices: 8.26 us -> 11.9 us  [shift(): return lax.ppermute(x, axis, [(i, (i + step) % size) for i in range(size)])]
    select_n x3 -> x0, other arithmetic: 2.54 us -> none  [the longest x2 2.36 us: ordered(): jnp.where(flag == 0, jnp.concatenate([mine, theirs], axis), jnp.concatena...]
    pallas_call x24 -> x22, Pallas kernels: 72.6 us -> 75 us  [run(): pl.pallas_call(wrapped, grid_spec=pltpu.PrefetchScalarGridSpec(num_scalar...]
  transfers between devices with their start and end apart: 29 -> 24, of which waited for: 15 -> 12; matrix products, arithmetic and copies ran while one was open for 2% -> 0% of each run, Pallas kernels for 33% -> 39%
where the time goes in v2:
time: 171 us; the launch traced here: 170 us
  Pallas kernels  75 us (44%)
  waiting for transfers between devices  50.7 us (30%)
  starting transfers between devices  28.2 us (16%)
  local copies, waits for them, and re-layouts  14.8 us (9%)
    pallas_call x22, Pallas kernels, run(): pl.pallas_call(wrapped, grid_spec=pltpu.PrefetchScalarGridSpec(num_scalar...  75 us
    ppermute x18, waiting for transfers between devices, swap(): return lax.ppermute(x, axis, [(i, i ^ bit) for i in range(size)])  48.4 us
    ppermute x18, starting transfers between devices, swap(): return lax.ppermute(x, axis, [(i, i ^ bit) for i in range(size)])  16.3 us
    unnamed x76, local copies, waits for them, and re-layouts  14.5 us
    ppermute x6, starting transfers between devices, shift(): return lax.ppermute(x, axis, [(i, (i + step) % size) for i in range(size)])  11.9 us
  transfers between devices with their start and end apart: 24, of which 12 were waited for; matrix products, arithmetic and copies ran while one was open for 0% of the time, Pallas kernels for 39%

profile of v2, /device:TPU:0, one launch (start us, length us, event | category | flops | bytes accessed | tf_op | source)
XLA Modules:
  0.0 169.6 jit_solution(2352743140078925910)
XLA Ops:
  1.2 2.6 %collective-permute-start = (bf16[80,1216]{1,0:T(8,128)(2,1)}, bf16[80,1216]{1,0:T(8,128)(2,1)S(1)}, u32[]{:S(2)}, u32[]{:S(2)}) collective-permute-start(bf16[80,1216]{1,0:T(8,128)(2,1)} %refs_1_.1), channel_id=1, source_target_pairs={{0,16},{16,0},{1,17},{17,1},{2,18},{18,2},{3,19},{19,3},{4,20},{20... | collective-permute-start | bytes 583688 | tf_op jit(solution)/shard_map/ppermute | solution.py:339
  3.7 5.9 %collective-permute-done.refs_2_ = bf16[80,1216]{1,0:T(8,128)(2,1)S(1)} collective-permute-done((bf16[80,1216]{1,0:T(8,128)(2,1)}, bf16[80,1216]{1,0:T(8,128)(2,1)S(1)}, u32[]{:S(2)}, u32[]{:S(2)}) %collective-permute-start) | collective-permute-done | bytes 194592 | tf_op jit(solution)/shard_map/ppermute | solution.py:339
  11.9 1.8 %collective-permute-start.3 = (bf16[768,512]{1,0:T(8,128)(2,1)S(1)}, bf16[768,512]{1,0:T(8,128)(2,1)S(1)}, u32[]{:S(2)}, u32[]{:S(2)}) collective-permute-start(bf16[768,512]{1,0:T(8,128)(2,1)S(1)} %get-tuple-element.71), channel_id=1, source_target_pairs={{0,16},{16,0},{1,17},{17,1},{2,18},{18,2},{3,19},{19,3},{4,20},{20... | collective-permute-start | bytes 2359304 | tf_op jit(solution)/shard_map/ppermute | solution.py:339
  15.2 2.6 %collective-permute-start.2 = (bf16[80,2432]{1,0:T(8,128)(2,1)}, bf16[80,2432]{1,0:T(8,128)(2,1)S(1)}, u32[]{:S(2)}, u32[]{:S(2)}) collective-permute-start(bf16[80,2432]{1,0:T(8,128)(2,1)} %get-tuple-element.69.refs_4_), channel_id=1, source_target_pairs={{0,8},{4,12},{8,0},{12,4},{1,9},{5,13},{9,1},{13,5},{2,10},{6,14},... | collective-permute-start | bytes 1167368 | tf_op jit(solution)/shard_map/ppermute | solution.py:344
  19.4 4.8 %collective-permute-done.4.refs_3_.refs_8_ = bf16[80,2432]{1,0:T(8,128)(2,1)S(1)} collective-permute-done((bf16[80,2432]{1,0:T(8,128)(2,1)}, bf16[80,2432]{1,0:T(8,128)(2,1)S(1)}, u32[]{:S(2)}, u32[]{:S(2)}) %collective-permute-start.4) | collective-permute-done | bytes 389152 | tf_op jit(solution)/shard_map/ppermute | solution.py:339
  25.2 7.2 %collective-permute-done.3.refs_3_ = bf16[768,512]{1,0:T(8,128)(2,1)S(1)} collective-permute-done((bf16[768,512]{1,0:T(8,128)(2,1)S(1)}, bf16[768,512]{1,0:T(8,128)(2,1)S(1)}, u32[]{:S(2)}, u32[]{:S(2)}) %collective-permute-start.3) | collective-permute-done | bytes 786464 | tf_op jit(solution)/shard_map/ppermute | solution.py:339
  33.2 7.5 %attend.3 = (bf16[1280,384]{1,0:T(8,128)(2,1)}, f32[10,768,768]{2,1,0:T(8,128)}, f32[10,2,768]{2,1,0:T(2,128)}, bf16[768,1280]{1,0:T(8,128)(2,1)}, f32[8,128]{1,0:T(8,128)}) custom-call(bf16[384,1280]{1,0:T(8,128)(2,1)} %bitcast.59, bf16[384,1280]{1,0:T(8,128)(2,1)} %bitcast.41, bf16[384,1280]{1,0:T(8,128)(2,1)} %bitcast.50, bf16[768,512]{1,0:T(8,128)(2,1)} %copy-done.37, ...), custom_call_target="tpu_custom_call" | custom-call | flops 4369999872 | tf_op jit(solution)/shard_map/attend/pallas_call | solution.py:42
  40.8 2.3 %collective-permute-done.2.refs_0_.refs_1_ = bf16[80,2432]{1,0:T(8,128)(2,1)S(1)} collective-permute-done((bf16[80,2432]{1,0:T(8,128)(2,1)}, bf16[80,2432]{1,0:T(8,128)(2,1)S(1)}, u32[]{:S(2)}, u32[]{:S(2)}) %collective-permute-start.2) | collective-permute-done | bytes 389152 | tf_op jit(solution)/shard_map/ppermute | solution.py:344
  44.3 2.8 %collective-permute-start.9 = (bf16[80,2432]{1,0:T(8,128)(2,1)}, bf16[80,2432]{1,0:T(8,128)(2,1)}, u32[]{:S(2)}, u32[]{:S(2)}) collective-permute-start(bf16[80,2432]{1,0:T(8,128)(2,1)} %get-tuple-element.69.refs_4_), channel_id=1, source_target_pairs={{0,12},{4,0},{8,4},{12,8},{1,13},{5,1},{9,5},{13,9},{2,14},{6,2},{... | collective-permute-start | bytes 1167368 | tf_op jit(solution)/shard_map/ppermute | solution.py:344
  50.5 5.3 %collective-permute-done.8.refs_9_.refs_5_ = bf16[80,2432]{1,0:T(8,128)(2,1)S(1)} collective-permute-done((bf16[80,2432]{1,0:T(8,128)(2,1)S(1)}, bf16[80,2432]{1,0:T(8,128)(2,1)S(1)}, u32[]{:S(2)}, u32[]{:S(2)}) %collective-permute-start.8) | collective-permute-done | bytes 389152 | tf_op jit(solution)/shard_map/ppermute | solution.py:339
  56.5 7.6 %attend.4 = (bf16[1280,384]{1,0:T(8,128)(2,1)}, f32[10,768,768]{2,1,0:T(8,128)}, f32[10,2,768]{2,1,0:T(2,128)}, bf16[768,1280]{1,0:T(8,128)(2,1)}, f32[8,128]{1,0:T(8,128)}) custom-call(bf16[384,1280]{1,0:T(8,128)(2,1)} %bitcast.60, bf16[384,1280]{1,0:T(8,128)(2,1)} %bitcast.42, ...), custom_call_target="tpu_custom_call", output_to_operand_aliasing={{0}: (4, {}), {1}: (5, {}), {2}: (6, {}), {3}: (7, {})} | custom-call | flops 4369999872 | tf_op jit(solution)/shard_map/attend/pallas_call | solution.py:42
  65.0 2.1 %copy.43 = (bf16[80,2432]{1,0:T(8,128)(2,1)}, f32[8,128]{1,0:T(8,128)S(1)}) custom-call(bf16[80,2432]{1,0:T(8,128)(2,1)} %collective-permute-done.9.refs_0_.refs_3_, f32[8,128]{1,0:T(8,128)S(1)} %get-tuple-element.90.refs_1_), custom_call_target="tpu_custom_call" | custom-call | flops 575000000 | tf_op jit(solution)/shard_map/copy/pallas_call | solution.py:42
  68.0 4.7 %attend.5 = (bf16[1280,384]{1,0:T(8,128)(2,1)}, f32[10,768,768]{2,1,0:T(8,128)}, f32[10,2,768]{2,1,0:T(2,128)}, bf16[768,1280]{1,0:T(8,128)(2,1)}, f32[8,128]{1,0:T(8,128)}) custom-call(bf16[384,1280]{1,0:T(8,128)(2,1)} %bitcast.61, bf16[384,1280]{1,0:T(8,128)(2,1)} %bitcast.43, ...), custom_call_target="tpu_custom_call", output_to_operand_aliasing={{0}: (4, {}), {1}: (5, {}), {2}: (6, {}), {3}: (7, {})} | custom-call | flops 2184999936 | tf_op jit(solution)/shard_map/attend/pallas_call | solution.py:42
  77.4 7.5 %outer.1 = (bf16[1,80,2432]{2,1,0:T(8,128)(2,1)S(1)}, bf16[2,80,2432]{2,1,0:T(8,128)(2,1)}, bf16[1,80,2432]{2,1,0:T(8,128)(2,1)}, bf16[4,80,2432]{2,1,0:T(8,128)(2,1)S(1)}, f32[8,128]{1,0:T(8,128)S(1)}) custom-call(s32[8]{0:T(128)S(1)} %stack.71.refs_0_, bf16[16,80,384]{2,1,0:T(8,128)(2,1)S(1)} %bitcast.33, bf16[16,80,384]{2,1,0:T(8,128)(2,1)S(1)} %bitcast.34, ...), custom_call_target="tpu_custom_call" | custom-call | flops 3449999872 | tf_op jit(solution)/shard_map/outer/pallas_call | solution.py:42
  85.0 7.5 %project.1 = (bf16[8,80,384]{2,1,0:T(8,128)(2,1)S(1)}, bf16[8,80,384]{2,1,0:T(8,128)(2,1)S(1)}, f32[8,128]{1,0:T(8,128)S(1)}) custom-call(s32[8]{0:T(128)S(1)} %stack.62.refs_0_, bf16[80,2432]{1,0:T(8,128)(2,1)S(1)} %copy-done.28, bf16[80,2432]{1,0:T(8,128)(2,1)} %collective-permute-done.7.refs_0_.refs_2_, ...), custom_call_target="tpu_custom_call" | custom-call | flops 3449999872 | tf_op jit(solution)/shard_map/project/pallas_call | solution.py:42
  95.5 2.0 %collective-permute-done.15.refs_3_.refs_0_ = bf16[384,1280]{1,0:T(8,128)(2,1)S(1)} collective-permute-done((bf16[384,1280]{1,0:T(8,128)(2,1)}, bf16[384,1280]{1,0:T(8,128)(2,1)S(1)}, u32[]{:S(2)}, u32[]{:S(2)}) %collective-permute-start.15) | collective-permute-done | bytes 983072 | tf_op jit(solution)/shard_map/ppermute | solution.py:339
  97.6 7.0 %collective-permute-done.14.refs_1_ = bf16[1,80,2432]{2,1,0:T(8,128)(2,1)S(1)} collective-permute-done((bf16[1,80,2432]{2,1,0:T(8,128)(2,1)S(1)}, bf16[1,80,2432]{2,1,0:T(8,128)(2,1)S(1)}, u32[]{:S(2)}, u32[]{:S(2)}) %collective-permute-start.14) | collective-permute-done | bytes 389152 | tf_op jit(solution)/shard_map/ppermute | solution.py:339
  108.2 10.0 %back.2 = (bf16[384,1280]{1,0:T(8,128)(2,1)}, f32[384,1280]{1,0:T(8,128)}, f32[384,1280]{1,0:T(8,128)}, f32[10,3,768]{2,1,0:T(4,128)}, f32[8,128]{1,0:T(8,128)}) custom-call(f32[10,768,768]{2,1,0:T(8,128)} %get-tuple-element.93.refs_0_, f32[10,2,768]{2,1,0:T(2,128)} %get-tuple-element.94.refs_1_, bf16[384,1280]{1,0:T(8,128)(2,1)} %bitcast.62, ...), custom_call_target="tpu_custom_call" | custom-call | flops 5750000128 | tf_op jit(solution)/shard_map/back/pallas_call | solution.py:42
  118.2 3.0 %collective-permute-done.17.refs_1_ = bf16[2,80,2432]{2,1,0:T(8,128)(2,1)S(1)} collective-permute-done((bf16[2,80,2432]{2,1,0:T(8,128)(2,1)}, bf16[2,80,2432]{2,1,0:T(8,128)(2,1)S(1)}, u32[]{:S(2)}, u32[]{:S(2)}) %collective-permute-start.17) | collective-permute-done | bytes 778272 | tf_op jit(solution)/shard_map/ppermute | solution.py:339
  122.9 6.1 %collective-permute-done.16.refs_1_ = bf16[1,80,2432]{2,1,0:T(8,128)(2,1)S(1)} collective-permute-done((bf16[1,80,2432]{2,1,0:T(8,128)(2,1)}, bf16[1,80,2432]{2,1,0:T(8,128)(2,1)S(1)}, u32[]{:S(2)}, u32[]{:S(2)}) %collective-permute-start.16) | collective-permute-done | bytes 389152 | tf_op jit(solution)/shard_map/ppermute | solution.py:339
  130.6 10.1 %back.3 = (bf16[384,1280]{1,0:T(8,128)(2,1)}, f32[384,1280]{1,0:T(8,128)}, f32[384,1280]{1,0:T(8,128)}, f32[10,3,768]{2,1,0:T(4,128)}, f32[8,128]{1,0:T(8,128)}) custom-call(f32[10,768,768]{2,1,0:T(8,128)} %get-tuple-element.93.refs_0_, ...), custom_call_target="tpu_custom_call", output_to_operand_aliasing={{0}: (7, {}), {1}: (8, {}), {2}: (9, {}), {3}: (10, {})} | custom-call | flops 5750000128 | tf_op jit(solution)/shard_map/back/pallas_call | solution.py:42
  142.0 3.1 %collective-permute-start.22 = (bf16[80,2432]{1,0:T(8,128)(2,1)}, bf16[80,2432]{1,0:T(8,128)(2,1)S(1)}, u32[]{:S(2)}, u32[]{:S(2)}) collective-permute-start(bf16[80,2432]{1,0:T(8,128)(2,1)} %get-tuple-element.128), channel_id=1, source_target_pairs={{0,12},{4,0},{8,4},{12,8},{1,13},{5,1},{9,5},{13,9},{2,14},{6,2},{... | collective-permute-start | bytes 1167368 | tf_op jit(solution)/shard_map/ppermute | solution.py:344
  150.9 10.6 %cross.1 = (bf16[384,1280]{1,0:T(8,128)(2,1)}, bf16[384,1280]{1,0:T(8,128)(2,1)}, f32[8,128]{1,0:T(8,128)S(1)}) custom-call(bf16[384,1280]{1,0:T(8,128)(2,1)S(1)} %copy-done.24, bf16[384,1280]{1,0:T(8,128)(2,1)S(1)} %bitcast.49, bf16[384,1280]{1,0:T(8,128)(2,1)S(1)} %bitcast.58, bf16[1280,384]{1,0:T(8,128)(2,1)} %collective-permute-done.18.refs_3_, ...), custom_call_target="tpu_custom_call" | custom-call | flops 8625000448 | tf_op jit(solution)/shard_map/cross/pallas_call | solution.py:42
  163.8 5.0 %collective-permute-done.23.refs_1_ = bf16[80,1216]{1,0:T(8,128)(2,1)S(1)} collective-permute-done((bf16[80,1216]{1,0:T(8,128)(2,1)S(1)}, bf16[80,1216]{1,0:T(8,128)(2,1)S(1)}, u32[]{:S(2)}, u32[]{:S(2)}) %collective-permute-start.23) | collective-permute-done | bytes 194592 | tf_op jit(solution)/shard_map/ppermute | solution.py:339
  (126 shorter events, 39.6 us)
Async XLA Ops:
  0.7 9.0 %collective-permute-start.1 = (bf16[384,2432]{1,0:T(8,128)(2,1)}, bf16[384,2432]{1,0:T(8,128)(2,1)}, u32[]{:S(2)}, u32[]{:S(2)}) collective-permute-start(bf16[384,2432]{1,0:T(8,128)(2,1)} %bitcast.65), channel_id=1, source_target_pairs={{0,1},{1,0},{2,3},{3,2},{4,5},{5,4},{6,7},{7,6},{8,9},{9,8},{10,11... | collective-permute-start | bytes 5603336 | tf_op jit(solution)/shard_map/ppermute | solution.py:339
  1.2 8.4 %collective-permute-start = (bf16[80,1216]{1,0:T(8,128)(2,1)}, bf16[80,1216]{1,0:T(8,128)(2,1)S(1)}, u32[]{:S(2)}, u32[]{:S(2)}) collective-permute-start(bf16[80,1216]{1,0:T(8,128)(2,1)} %refs_1_.1), channel_id=1, source_target_pairs={{0,16},{16,0},{1,17},{17,1},{2,18},{18,2},{3,19},{19,3},{4,20},{20... | collective-permute-start | bytes 583688 | tf_op jit(solution)/shard_map/ppermute | solution.py:339
  11.9 20.5 %collective-permute-start.3 = (bf16[768,512]{1,0:T(8,128)(2,1)S(1)}, bf16[768,512]{1,0:T(8,128)(2,1)S(1)}, u32[]{:S(2)}, u32[]{:S(2)}) collective-permute-start(bf16[768,512]{1,0:T(8,128)(2,1)S(1)} %get-tuple-element.71), channel_id=1, source_target_pairs={{0,16},{16,0},{1,17},{17,1},{2,18},{18,2},{3,19},{19,3},{4,20},{20... | collective-permute-start | bytes 2359304 | tf_op jit(solution)/shard_map/ppermute | solution.py:339
  13.7 10.5 %collective-permute-start.4 = (bf16[80,2432]{1,0:T(8,128)(2,1)}, bf16[80,2432]{1,0:T(8,128)(2,1)S(1)}, u32[]{:S(2)}, u32[]{:S(2)}) collective-permute-start(bf16[80,2432]{1,0:T(8,128)(2,1)} %get-tuple-element.69.refs_4_), channel_id=1, source_target_pairs={{0,2},{1,3},{2,0},{3,1},{4,6},{5,7},{6,4},{7,5},{8,10},{9,11},{10,... | collective-permute-start | bytes 1167368 | tf_op jit(solution)/shard_map/ppermute | solution.py:339
  15.2 27.8 %collective-permute-start.2 = (bf16[80,2432]{1,0:T(8,128)(2,1)}, bf16[80,2432]{1,0:T(8,128)(2,1)S(1)}, u32[]{:S(2)}, u32[]{:S(2)}) collective-permute-start(bf16[80,2432]{1,0:T(8,128)(2,1)} %get-tuple-element.69.refs_4_), channel_id=1, source_target_pairs={{0,8},{4,12},{8,0},{12,4},{1,9},{5,13},{9,1},{13,5},{2,10},{6,14},... | collective-permute-start | bytes 1167368 | tf_op jit(solution)/shard_map/ppermute | solution.py:344
  17.8 29.6 %collective-permute-start.7 = (bf16[80,2432]{1,0:T(8,128)(2,1)}, bf16[80,2432]{1,0:T(8,128)(2,1)}, u32[]{:S(2)}, u32[]{:S(2)}) collective-permute-start(bf16[80,2432]{1,0:T(8,128)(2,1)} %get-tuple-element.69.refs_4_), channel_id=1, source_target_pairs={{0,4},{4,8},{8,12},{12,0},{1,5},{5,9},{9,13},{13,1},{2,6},{6,10},{... | collective-permute-start | bytes 1167368 | tf_op jit(solution)/shard_map/ppermute | solution.py:344
  24.7 31.1 %collective-permute-start.6 = (bf16[768,512]{1,0:T(8,128)(2,1)S(1)}, bf16[768,512]{1,0:T(8,128)(2,1)}, u32[]{:S(2)}, u32[]{:S(2)}) collective-permute-start(bf16[768,512]{1,0:T(8,128)(2,1)S(1)} %get-tuple-element.77), channel_id=1, source_target_pairs={{0,16},{16,0},{1,17},{17,1},{2,18},{18,2},{3,19},{19,3},{4,20},{20... | collective-permute-start | bytes 2359304 | tf_op jit(solution)/shard_map/ppermute | solution.py:339
  43.7 12.0 %collective-permute-start.8 = (bf16[80,2432]{1,0:T(8,128)(2,1)S(1)}, bf16[80,2432]{1,0:T(8,128)(2,1)S(1)}, u32[]{:S(2)}, u32[]{:S(2)}) collective-permute-start(bf16[80,2432]{1,0:T(8,128)(2,1)S(1)} %get-tuple-element.84), channel_id=1, source_target_pairs={{0,2},{1,3},{2,0},{3,1},{4,6},{5,7},{6,4},{7,5},{8,10},{9,11},{10,... | collective-permute-start | bytes 1167368 | tf_op jit(solution)/shard_map/ppermute | solution.py:339
  44.3 20.6 %collective-permute-start.9 = (bf16[80,2432]{1,0:T(8,128)(2,1)}, bf16[80,2432]{1,0:T(8,128)(2,1)}, u32[]{:S(2)}, u32[]{:S(2)}) collective-permute-start(bf16[80,2432]{1,0:T(8,128)(2,1)} %get-tuple-element.69.refs_4_), channel_id=1, source_target_pairs={{0,12},{4,0},{8,4},{12,8},{1,13},{5,1},{9,5},{13,9},{2,14},{6,2},{... | collective-permute-start | bytes 1167368 | tf_op jit(solution)/shard_map/ppermute | solution.py:344
  48.4 18.7 %collective-permute-start.10 = (bf16[80,2432]{1,0:T(8,128)(2,1)S(1)}, bf16[80,2432]{1,0:T(8,128)(2,1)S(1)}, u32[]{:S(2)}, u32[]{:S(2)}) collective-permute-start(bf16[80,2432]{1,0:T(8,128)(2,1)S(1)} %get-tuple-element.92), channel_id=1, source_target_pairs={{0,2},{1,3},{2,0},{3,1},{4,6},{5,7},{6,4},{7,5},{8,10},{9,11},{10,... | collective-permute-start | bytes 1167368 | tf_op jit(solution)/shard_map/ppermute | solution.py:339
  49.0 18.1 %collective-permute-start.5 = (bf16[768,256]{1,0:T(8,128)(2,1)S(1)}, bf16[768,256]{1,0:T(8,128)(2,1)S(1)}, u32[]{:S(2)}, u32[]{:S(2)}) collective-permute-start(bf16[768,256]{1,0:T(8,128)(2,1)S(1)} %get-tuple-element.76), channel_id=1, source_target_pairs={{0,16},{16,0},{1,17},{17,1},{2,18},{18,2},{3,19},{19,3},{4,20},{20... | collective-permute-start | bytes 1179656 | tf_op jit(solution)/shard_map/ppermute | solution.py:339
  72.7 2.8 %collective-permute-start.12 = (bf16[16,80,384]{2,1,0:T(8,128)(2,1)}, bf16[16,80,384]{2,1,0:T(8,128)(2,1)S(1)}, u32[]{:S(2)}, u32[]{:S(2)}) collective-permute-start(bf16[16,80,384]{2,1,0:T(8,128)(2,1)} %bitcast.32), channel_id=1, source_target_pairs={{0,1},{1,0},{2,3},{3,2},{4,5},{5,4},{6,7},{7,6},{8,9},{9,8},{10,11... | collective-permute-start | bytes 2949128 | tf_op jit(solution)/shard_map/ppermute | solution.py:339
  72.8 12.2 %collective-permute-start.11 = (bf16[80,2432]{1,0:T(8,128)(2,1)}, bf16[80,2432]{1,0:T(8,128)(2,1)S(1)}, u32[]{:S(2)}, u32[]{:S(2)}) collective-permute-start(bf16[80,2432]{1,0:T(8,128)(2,1)} %get-tuple-element.96), channel_id=1, source_target_pairs={{0,2},{1,3},{2,0},{3,1},{4,6},{5,7},{6,4},{7,5},{8,10},{9,11},{10,... | collective-permute-start | bytes 1167368 | tf_op jit(solution)/shard_map/ppermute | solution.py:339
  73.5 24.0 %collective-permute-start.15 = (bf16[384,1280]{1,0:T(8,128)(2,1)}, bf16[384,1280]{1,0:T(8,128)(2,1)S(1)}, u32[]{:S(2)}, u32[]{:S(2)}) collective-permute-start(bf16[384,1280]{1,0:T(8,128)(2,1)} %copy-done.22), channel_id=1, source_target_pairs={{0,16},{16,0},{1,17},{17,1},{2,18},{18,2},{3,19},{19,3},{4,20},{20... | collective-permute-start | bytes 2949128 | tf_op jit(solution)/shard_map/ppermute | solution.py:339
  92.5 2.9 %collective-permute-start.13 = (bf16[8,80,384]{2,1,0:T(8,128)(2,1)S(1)}, bf16[8,80,384]{2,1,0:T(8,128)(2,1)S(1)}, u32[]{:S(2)}, u32[]{:S(2)}) collective-permute-start(bf16[8,80,384]{2,1,0:T(8,128)(2,1)S(1)} %get-tuple-element.101), channel_id=1, source_target_pairs={{0,1},{1,0},{2,3},{3,2},{4,5},{5,4},{6,7},{7,6},{8,9},{9,8},{10,11... | collective-permute-start | bytes 1474568 | tf_op jit(solution)/shard_map/ppermute | solution.py:339
  92.7 11.9 %collective-permute-start.14 = (bf16[1,80,2432]{2,1,0:T(8,128)(2,1)S(1)}, bf16[1,80,2432]{2,1,0:T(8,128)(2,1)S(1)}, u32[]{:S(2)}, u32[]{:S(2)}) collective-permute-start(bf16[1,80,2432]{2,1,0:T(8,128)(2,1)S(1)} %get-tuple-element.105), channel_id=1, source_target_pairs={{0,2},{1,3},{2,0},{3,1},{4,6},{5,7},{6,4},{7,5},{8,10},{9,11},{10,... | collective-permute-start | bytes 1167368 | tf_op jit(solution)/shard_map/ppermute | solution.py:339
  93.2 28.0 %collective-permute-start.17 = (bf16[2,80,2432]{2,1,0:T(8,128)(2,1)}, bf16[2,80,2432]{2,1,0:T(8,128)(2,1)S(1)}, u32[]{:S(2)}, u32[]{:S(2)}) collective-permute-start(bf16[2,80,2432]{2,1,0:T(8,128)(2,1)} %get-tuple-element.114), channel_id=1, source_target_pairs={{0,2},{1,3},{2,0},{3,1},{4,6},{5,7},{6,4},{7,5},{8,10},{9,11},{10,... | collective-permute-start | bytes 2334728 | tf_op jit(solution)/shard_map/ppermute | solution.py:339
  94.8 34.2 %collective-permute-start.16 = (bf16[1,80,2432]{2,1,0:T(8,128)(2,1)}, bf16[1,80,2432]{2,1,0:T(8,128)(2,1)S(1)}, u32[]{:S(2)}, u32[]{:S(2)}) collective-permute-start(bf16[1,80,2432]{2,1,0:T(8,128)(2,1)} %get-tuple-element.113), channel_id=1, source_target_pairs={{0,2},{1,3},{2,0},{3,1},{4,6},{5,7},{6,4},{7,5},{8,10},{9,11},{10,... | collective-permute-start | bytes 1167368 | tf_op jit(solution)/shard_map/ppermute | solution.py:339
  106.0 39.9 %collective-permute-start.20 = (bf16[80,2432]{1,0:T(8,128)(2,1)}, bf16[80,2432]{1,0:T(8,128)(2,1)}, u32[]{:S(2)}, u32[]{:S(2)}) collective-permute-start(bf16[80,2432]{1,0:T(8,128)(2,1)} %get-tuple-element.123), channel_id=1, source_target_pairs={{0,8},{4,12},{8,0},{12,4},{1,9},{5,13},{9,1},{13,5},{2,10},{6,14},... | collective-permute-start | bytes 1167368 | tf_op jit(solution)/shard_map/ppermute | solution.py:344
  107.1 38.7 %collective-permute-start.18 = (bf16[1280,384]{1,0:T(8,128)(2,1)S(1)}, bf16[1280,384]{1,0:T(8,128)(2,1)}, u32[]{:S(2)}, u32[]{:S(2)}) collective-permute-start(bf16[1280,384]{1,0:T(8,128)(2,1)S(1)} %get-tuple-element.103.refs_6_), channel_id=1, source_target_pairs={{0,16},{16,0},{1,17},{17,1},{2,18},{18,2},{3,19},{19,3},{4,20},{20... | collective-permute-start | bytes 2949128 | tf_op jit(solution)/shard_map/ppermute | solution.py:339
  140.7 5.2 %collective-permute-start.19 = (f32[10,3,768]{2,1,0:T(4,128)}, f32[10,3,768]{2,1,0:T(4,128)S(1)}, u32[]{:S(2)}, u32[]{:S(2)}) collective-permute-start(f32[10,3,768]{2,1,0:T(4,128)} %get-tuple-element.119), channel_id=1, source_target_pairs={{0,16},{16,0},{1,17},{17,1},{2,18},{18,2},{3,19},{19,3},{4,20},{20... | collective-permute-start | bytes 276488 | tf_op jit(solution)/shard_map/ppermute | solution.py:339
  141.3 20.2 %collective-permute-start.21 = (bf16[80,2432]{1,0:T(8,128)(2,1)}, bf16[80,2432]{1,0:T(8,128)(2,1)S(1)}, u32[]{:S(2)}, u32[]{:S(2)}) collective-permute-start(bf16[80,2432]{1,0:T(8,128)(2,1)} %get-tuple-element.127), channel_id=1, source_target_pairs={{0,4},{4,8},{8,12},{12,0},{1,5},{5,9},{9,13},{13,1},{2,6},{6,10},{... | collective-permute-start | bytes 1167368 | tf_op jit(solution)/shard_map/ppermute | solution.py:344
  142.0 19.5 %collective-permute-start.22 = (bf16[80,2432]{1,0:T(8,128)(2,1)}, bf16[80,2432]{1,0:T(8,128)(2,1)S(1)}, u32[]{:S(2)}, u32[]{:S(2)}) collective-permute-start(bf16[80,2432]{1,0:T(8,128)(2,1)} %get-tuple-element.128), channel_id=1, source_target_pairs={{0,12},{4,0},{8,4},{12,8},{1,13},{5,1},{9,5},{13,9},{2,14},{6,2},{... | collective-permute-start | bytes 1167368 | tf_op jit(solution)/shard_map/ppermute | solution.py:344
  162.9 5.8 %collective-permute-start.23 = (bf16[80,1216]{1,0:T(8,128)(2,1)S(1)}, bf16[80,1216]{1,0:T(8,128)(2,1)S(1)}, u32[]{:S(2)}, u32[]{:S(2)}) collective-permute-start(bf16[80,1216]{1,0:T(8,128)(2,1)S(1)} %get-tuple-element.131), channel_id=1, source_target_pairs={{0,16},{16,0},{1,17},{17,1},{2,18},{18,2},{3,19},{19,3},{4,20},{20... | collective-permute-start | bytes 583688 | tf_op jit(solution)/shard_map/ppermute | solution.py:339
  (38 other events, 189.2 us)

commit v3 on v2

--- a/solution.py
+++ b/solution.py
@@ -15,10 +15,10 @@
 VMEM = pl.BlockSpec(memory_space=pltpu.VMEM)
 SMEM = pl.BlockSpec(memory_space=pltpu.SMEM)
 TOKEN = (8, 128)
-BIG = 60
+BIG = 36
 FLOPS_PER_US = 1150e6 * 0.5
-CHUNKS = (4, 4, 2)
-PARTS = 2
+CHUNKS = (3, 4, 3)
+PARTS = (6, 3, 1)
 
 
 def mm(a, b):
@@ -94,7 +94,7 @@
     n = k.shape[0]
     (out,), token = run(
         pack_kernel, "pack", [k, v], [column(n, first)] * 2,
-        [((2 * n, pairs * PAIR), BF16)], [column(2 * n, 0)], (pairs,), after, us=pairs * 0.4,
+        [((2 * n, pairs * PAIR), BF16)], [column(2 * n, 0)], (pairs,), after, us=0.1,
     )
     return out, token
 
@@ -171,17 +171,16 @@
     gk_ref[...] = ((mm(ds, q) + dk_ref[...]) * SCALE).astype(BF16)
 
 
-def cross(q, k, v, d, share, after):
+def cross(q, k, v, d, share, grads, first, pairs, after):
     n, width = q.shape
-    pairs = width // PAIR
     dk, dv, stat = share
     return run(
         cross_kernel, "cross",
         [q, k, v, d, stat, dk, dv],
-        [column(n, 0)] * 3
-        + [pl.BlockSpec((PAIR, n), lambda i: (i, 0)), pl.BlockSpec((1, 3, 2 * n), lambda i: (i, 0, 0))]
-        + [column(n, 0)] * 2,
-        [((n, width), BF16)] * 2, [column(n, 0)] * 2, (pairs,), after, us=1.5 * pairs,
+        [column(n, first)] * 3
+        + [pl.BlockSpec((PAIR, n), lambda i: (first + i, 0)), pl.BlockSpec((1, 3, 2 * n), lambda i: (first + i, 0, 0))]
+        + [column(n, first)] * 2,
+        [((n, width), BF16)] * 2, [column(n, first)] * 2, (pairs,), after, grads, us=1.5 * pairs, vmem=BIG,
     )
 
 
@@ -198,69 +197,65 @@
 
     (out,), token = run(
         kernel, "join", [cam.reshape(1), mine, far], [SMEM, whole(mine), whole(far)],
-        [((rows, 2 * half), BF16)], [whole((rows, 2 * half))], (1,), after,
+        [((rows, 2 * half), BF16)], [whole((rows, 2 * half))], (1,), after, us=30,
     )
     return out, token
 
 
-def copy_kernel(x_ref, out_ref):
-    out_ref[...] = x_ref[...]
-
-
-def copy(x, after):
-    rows, width = x.shape
-    steps = 4 if rows % 64 == 0 else 1
-    block = pl.BlockSpec((rows // steps, width), lambda i: (i, 0))
+def copy(parts, after):
+    rows, width = parts[0].shape
+    count = len(parts)
+
+    def kernel(*refs):
+        for i, ref in enumerate(refs[:count]):
+            refs[count][i * rows : (i + 1) * rows] = ref[...]
+
     (out,), token = run(
-        copy_kernel, "copy", [x], [block], [(x.shape, x.dtype)], [block], (steps,), after, us=1
+        kernel, "copy", parts, [whole(x) for x in parts],
+        [((count * rows, width), BF16)], [whole((count * rows, width))], (1,), after, us=1,
     )
     return out, token
 
 
-def project(slots, w, own, other, after):
+def project(w, own, other, after):
     rows, depth = w[0].shape
-    n, count = own.shape[0], len(w)
-
-    def kernel(slot_ref, *refs):
-        left = jnp.concatenate([r[...] for r in refs[:count]], 0)
-        for ref, out in zip(refs[count : count + 2], refs[count + 2 :]):
+    n, parts, count = own.shape[0], len(w), sum(x.shape[0] for x in w) // rows
+
+    def kernel(*refs):
+        left = jnp.concatenate([r[...] for r in refs[:parts]], 0)
+        for ref, out in zip(refs[parts : parts + 2], refs[parts + 2 :]):
             res = nt(left, ref[...]).astype(BF16)
             for j in range(count):
-                out[slot_ref[j]] = res[j * rows : (j + 1) * rows]
-
-    tokens = pl.BlockSpec((PAIR, depth), lambda i, _: (i, 0))
+                out[j] = res[j * rows : (j + 1) * rows]
+
+    tokens = pl.BlockSpec((PAIR, depth), lambda i: (i, 0))
     return run(
         kernel, "project", [*w, own, other],
-        [pl.BlockSpec((rows, depth), lambda i, _: (0, 0))] * count + [tokens] * 2,
-        [((count, rows, n), BF16)] * 2, [pl.BlockSpec((count, rows, PAIR), lambda i, _: (0, 0, i))] * 2,
-        (n // PAIR,), after, slots=slots, us=6,
-    )
-
-
-def weave(core, mine, theirs, sizes, after):
-    count, rows, n = mine.shape
-
-    def kernel(core_ref, mine_ref, theirs_ref, *outs):
-        for c, (even, odd) in enumerate(((mine_ref, theirs_ref), (theirs_ref, mine_ref))):
-
-            @pl.when(core_ref[0] == c)
-            def _():
-                first = 0
-                for out in outs:
-                    last = first + out.shape[0]
-                    row = first
-                    while row < last:
-                        block, offset = row // rows, row % rows
-                        size = min(rows - offset, last - row)
-                        src = (even, odd)[block % 2]
-                        out[row - first : row - first + size] = src[block // 2, offset : offset + size]
-                        row += size
-                    first = last
-
-    return run(
-        kernel, "weave", [core.reshape(1), mine, theirs], [SMEM, whole(mine), whole(theirs)],
-        [((s * PAIR, n), BF16) for s in sizes], [whole((s * PAIR, n)) for s in sizes], (1,), after, us=2,
-    )
+        [whole(x) for x in w] + [tokens] * 2,
+        [((count, rows, n), BF16)] * 2, [pl.BlockSpec((count, rows, PAIR), lambda i: (0, 0, i))] * 2,
+        (n // PAIR,), after, us=count - 1.9,
+    )
+
+
+def weave(core, slots, mine, theirs, after):
+    _, rows, n = mine[0].shape
+    total = 2 * slots.shape[0]
+
+    def kernel(slot_ref, core_ref, *refs):
+        *refs, out = refs
+        for side, which in enumerate((core_ref[0], 1 - core_ref[0])):
+            place = 0
+            for ref in refs[side * len(mine) : (side + 1) * len(mine)]:
+                for j in range(ref.shape[0]):
+                    out[2 * slot_ref[place] + which] = ref[j]
+                    place += 1
+
+    ins = [slots, core.reshape(1), *mine, *theirs]
+    (out,), token = run(
+        kernel, "weave", ins, [SMEM, SMEM] + [whole(x) for x in (*mine, *theirs)],
+        [((total, rows, n), BF16)], [whole((total, rows, n))], (1,), after, us=2,
+    )
+    return out.reshape(total * rows, n), token
 
 
 def outer(slots, a_own, a_other, own, other, groups, after):
@@ -271,7 +266,8 @@
     def kernel(slot_ref, *refs):
         mine, theirs, (own_ref, other_ref), outs = refs[:count], refs[count : 2 * count], refs[2 * count : 2 * count + 2], refs[2 * count + 2 :]
         left = [jnp.concatenate([r[0] for r in part], 0) for part in (mine, theirs)]
-        res = (mm(left[0], own_ref[...]) + mm(left[1], other_ref[...])).astype(BF16)
+        right = jnp.concatenate([own_ref[...], other_ref[...]], 0)
+        res = mm(jnp.concatenate(left, 1), right).astype(BF16)
         first = 0
         for out in outs:
             for j in range(out.shape[0]):
@@ -293,10 +289,10 @@
         out[...] = (x_ref[j].astype(F32) + y_ref[j].astype(F32)).astype(out.dtype)
 
 
-def add(x, y, dtype, after):
+def add(x, y, types, after):
     count, *block = x.shape
     return run(
-        add_kernel, "add", [x, y], [whole(x), whole(y)], [(tuple(block), dtype)] * count,
+        add_kernel, "add", [x, y], [whole(x), whole(y)], [(tuple(block), t) for t in types],
         [whole(tuple(block))] * count, (1,), after,
     )
 
@@ -352,7 +348,8 @@
     )
 
 
-ORDER = (2, 1, 3, 0)
+ORDER = (1, 3, 2)
+LATE = (2, 1, 3, 0)
 
 
 def body(queries, keys, values, d_out, w_out):
@@ -388,57 +385,56 @@
         return (dq, *share), (token,)
 
     pairs = width // PAIR
-    cuts = [pairs * i // PARTS for i in range(PARTS + 1)]
-    parts = [(a, b - a) for a, b in zip(cuts, cuts[1:])]
+    parts = [(sum(PARTS[:i]), c) for i, c in enumerate(PARTS)] if sum(PARTS) == pairs else [(0, pairs)]
     state, dq = (), ()
-    if blocked and len(chunks) == 3 and PARTS == 2:
+    if blocked and len(chunks) == len(parts) == 3:
         flat_other = swap(flat, "obj")
-        into = [2 * ((band - s) % 4) + line for s in ORDER] + [2 * ((band - s) % 4) + 1 - line for s in ORDER]
+        into = [2 * band + line, 2 * band + 1 - line]
+        into += [2 * ((band - s) % 4) + l for l in (line, 1 - line) for s in ORDER]
         into = jnp.stack(into).astype(jnp.int32)
-        out_of = [4 * ((band + s) % 4) + 2 * (1 - line) + core for s in ORDER]
-        out_of += [4 * ((band + s) % 4) + 2 * line + core for s in ORDER]
+        out_of = [4 * ((band + s) % 4) + 2 * l + core for l in (1 - line, line) for s in LATE]
         out_of = jnp.stack(out_of).astype(jnp.int32)
 
-        w_cols, token = join(cam, w_out, w_far, (flat_other,))
-        after = send(0, (token,))
-        held = [shift(w_cols, "band", s) for s in ORDER[:3]]
-        passed = [None, None, None, swap(w_cols, "obj", 2)]
-
-        def forward_w(j, after):
-            x, token = copy(held[j], after)
-            passed[j] = swap(x, "obj", 2)
-            return (token,)
-
-        after = send(1, (*after, passed[3]))
-        state, after = forward(0, state, after)
-        after = forward_w(0, after)
-        after = send(2, after)
-        after = forward_w(1, after)
-        state, after = forward(1, state, (*after, passed[0]))
-        x, token = copy(q, after)
+        after = send(0, ())
+        w_cols, token = join(cam, w_out, w_far, after)
+        held = [shift(w_cols, "band", s) for s in ORDER]
+        y_own = swap(w_cols, "obj", 2)
+        after = send(1, (token, flat_other))
+        (mine_a, theirs_a), token = project([w_cols, y_own], flat, flat_other, after)
+        theirs_a = swap(theirs_a, "obj")
+        state, after = forward(0, state, (token,))
+        x, token = copy(held[:2], after)
+        y_near = swap(x, "obj", 2)
+        after = send(2, (token,))
+        state, after = forward(1, state, after)
+        x, token = copy([q], after)
         q_far = swap(x, "cam")
-        after = forward_w(2, (token,))
-        state, after = forward(2, state, (*after, passed[1]))
+        x, token = copy(held[2:], (token, y_near))
+        y_far = swap(x, "obj", 2)
+        state, after = forward(2, state, (token,))
 
         a_own = state[0].reshape(bands * objs, rows, n)
         a_other = swap(a_own, "obj")
-        (*away, stay), token = outer(out_of, a_own, a_other, flat, flat_other, (1, 2, 1, 4), after)
+        (*away, stay), token = outer(out_of, a_own, a_other, flat, flat_other, (1, 1, 2, 4), after)
         away = [swap(x, "obj", 2) for x in away]
-        (mine, theirs), token = project(into, [*held, w_cols, *passed], flat, flat_other, (token,))
-        theirs = swap(theirs, "obj")
-        (d_att,), token = weave(core, mine, theirs, [pairs], (token,))
+        (mine_b, theirs_b), token = project([*held, y_near, y_far], flat, flat_other, (token,))
+        theirs_b = swap(theirs_b, "obj")
+        (x,), token = add(stay[:1], away[0], (BF16,), (token,))
+        sums = [shift(x, "band", LATE[0])]
+        d_att, token = weave(core, into, [mine_a, mine_b], [theirs_a, theirs_b], (token, q_far))
         d_far = swap(d_att, "cam")
-        (x,), token = add(stay[:1], away[0], BF16, (token, q_far))
-        sums = [shift(x, "band", ORDER[0])]
         dq, after = backward(0, dq, (token,))
-        (x, y), token = add(stay[1:3], away[1], BF16, after)
-        sums += [shift(x, "band", ORDER[1]), shift(y, "band", ORDER[2])]
-        (base,), token = add(stay[3:], away[2], F32, (token,))
-        (dq, *share), after = backward(1, dq, (token,))
+        (x,), token = add(stay[1:2], away[1], (BF16,), after)
+        sums.append(shift(x, "band", LATE[1]))
+        dq, after = backward(1, dq, (token,))
+        (dq, *share), after = backward(2, dq, (*after, sums[0]))
         share[2] = swap(share[2], "cam")
-        (*grads,), token = cross(q_far, k, v, d_far, share, (*after, sums[0]))
+        (x, base), token = add(stay[2:], away[2], (BF16, F32), after)
+        sums.append(shift(x, "band", LATE[2]))
+        grads, token = cross(q_far, k, v, d_far, share, (), 0, pairs // 2, (token, sums[1]))
         (mine, theirs), token = total_of(cam, [base, *sums], (token,))
         theirs = swap(theirs, "cam")
+        grads, token = cross(q_far, k, v, d_far, share, grads, pairs // 2, pairs - pairs // 2, (token,))
     else:
         after, q_far = (), swap(q, "cam")
         for i in range(len(chunks)):
@@ -448,11 +444,11 @@
         full = lax.all_gather(ordered(w_out, w_far, cam, 1), ("band", "obj"), axis=0, tiled=True)
         d_att = nt(full, flat).astype(BF16)
         d_far = swap(d_att, "cam")
-        for i in range(PARTS):
+        for i in range(len(parts)):
             dq, after = backward(i, dq, after)
         dq, *share = dq
         share[2] = swap(share[2], "cam")
-        (*grads,), token = cross(q_far, k, v, d_far, share, after)
+        grads, token = cross(q_far, k, v, d_far, share, (), 0, pairs, after)
         sums = lax.psum_scatter(mm(state[0], flat), ("band", "obj"), scatter_dimension=0, tiled=True)
         mine = jnp.where(cam == 0, sums[:, :half], sums[:, half:])
         theirs = jnp.where(cam == 0, sums[:, half:], sums[:, :half])

time: 171 us -> 133 us (0.78)
  waiting for transfers between devices: 50.7 us -> 25 us
  Pallas kernels: 75 us -> 65.9 us
  local copies, waits for them, and re-layouts: 14.8 us -> 12.8 us
    ppermute x18, waiting for transfers between devices: 48.4 us -> 11.5 us  [swap(): return lax.ppermute(x, axis, [(i, i ^ bit) for i in range(size)])]
    ppermute x6, waiting for transfers between devices: 2.28 us -> 13.5 us  [shift(): return lax.ppermute(x, axis, [(i, (i + step) % size) for i in range(size)])]
    pallas_call x22 -> x24, Pallas kernels: 75 us -> 65.9 us  [run(): pl.pallas_call(wrapped, grid_spec=pltpu.PrefetchScalarGridSpec(num_scalar...]
    ppermute x6, starting transfers between devices: 11.9 us -> 9.69 us  [shift(): return lax.ppermute(x, axis, [(i, (i + step) % size) for i in range(size)])]
    ppermute x18, starting transfers between devices: 16.3 us -> 18.3 us  [swap(): return lax.ppermute(x, axis, [(i, i ^ bit) for i in range(size)])]
    unnamed x76 -> x58, local copies, waits for them, and re-layouts: 14.5 us -> 12.5 us
  transfers between devices with their start and end apart: 24 -> 24, of which waited for: 12 -> 10; matrix products, arithmetic and copies ran while one was open for 0% -> 0% of each run, Pallas kernels for 39% -> 45%
where the time goes in v3:
time: 133 us
  Pallas kernels  65.9 us (50%)
  starting transfers between devices  28 us (21%)
  waiting for transfers between devices  25 us (19%)
  local copies, waits for them, and re-layouts  12.8 us (10%)
    pallas_call x24, Pallas kernels, run(): pl.pallas_call(wrapped, grid_spec=pltpu.PrefetchScalarGridSpec(num_scalar...  65.9 us
    ppermute x18, starting transfers between devices, swap(): return lax.ppermute(x, axis, [(i, i ^ bit) for i in range(size)])  18.3 us
    ppermute x6, waiting for transfers between devices, shift(): return lax.ppermute(x, axis, [(i, (i + step) % size) for i in range(size)])  13.5 us
    unnamed x58, local copies, waits for them, and re-layouts  12.5 us
    ppermute x18, waiting for transfers between devices, swap(): return lax.ppermute(x, axis, [(i, i ^ bit) for i in range(size)])  11.5 us
    ppermute x6, starting transfers between devices, shift(): return lax.ppermute(x, axis, [(i, (i + step) % size) for i in range(size)])  9.69 us
  transfers between devices with their start and end apart: 24, of which 10 were waited for; matrix products, arithmetic and copies ran while one was open for 0% of the time, Pallas kernels for 45%

profile of v3, /device:TPU:0, one launch (start us, length us, event | category | flops | bytes accessed | tf_op | source)
XLA Modules:
  0.0 132.5 jit_solution(10974966670000317992)
XLA Ops:
  0.6 3.0 %collective-permute-start = (bf16[80,1216]{1,0:T(8,128)(2,1)}, bf16[80,1216]{1,0:T(8,128)(2,1)S(1)}, u32[]{:S(2)}, u32[]{:S(2)}) collective-permute-start(bf16[80,1216]{1,0:T(8,128)(2,1)} %refs_1_.1), channel_id=1, source_target_pairs={{0,16},{16,0},{1,17},{17,1},{2,18},{18,2},{3,19},{19,3},{4,20},{20... | collective-permute-start | bytes 583688 | tf_op jit(solution)/shard_map/ppermute | solution.py:335
  11.6 1.8 %collective-permute-start.4 = (bf16[80,2432]{1,0:T(8,128)(2,1)S(1)}, bf16[80,2432]{1,0:T(8,128)(2,1)S(1)}, u32[]{:S(2)}, u32[]{:S(2)}) collective-permute-start(bf16[80,2432]{1,0:T(8,128)(2,1)S(1)} %get-tuple-element.79.refs_0_), channel_id=1, source_target_pairs={{0,2},{1,3},{2,0},{3,1},{4,6},{5,7},{6,4},{7,5},{8,10},{9,11},{10,... | collective-permute-start | bytes 1167368 | tf_op jit(solution)/shard_map/ppermute | solution.py:335
  17.0 2.2 %collective-permute-start.2 = (bf16[80,2432]{1,0:T(8,128)(2,1)S(1)}, bf16[80,2432]{1,0:T(8,128)(2,1)S(1)}, u32[]{:S(2)}, u32[]{:S(2)}) collective-permute-start(bf16[80,2432]{1,0:T(8,128)(2,1)S(1)} %get-tuple-element.79.refs_0_), channel_id=1, source_target_pairs={{0,12},{4,0},{8,4},{12,8},{1,13},{5,1},{9,5},{13,9},{2,14},{6,2},{... | collective-permute-start | bytes 1167368 | tf_op jit(solution)/shard_map/ppermute | solution.py:340
  19.3 2.6 %collective-permute-done.4.refs_1_ = bf16[80,2432]{1,0:T(8,128)(2,1)S(1)} collective-permute-done((bf16[80,2432]{1,0:T(8,128)(2,1)S(1)}, bf16[80,2432]{1,0:T(8,128)(2,1)S(1)}, u32[]{:S(2)}, u32[]{:S(2)}) %collective-permute-start.4) | collective-permute-done | bytes 389152 | tf_op jit(solution)/shard_map/ppermute | solution.py:335
  21.9 1.8 %project.2 = (bf16[2,80,384]{2,1,0:T(8,128)(2,1)S(1)}, bf16[2,80,384]{2,1,0:T(8,128)(2,1)S(1)}, f32[8,128]{1,0:T(8,128)S(1)}) custom-call(bf16[80,2432]{1,0:T(8,128)(2,1)S(1)} %get-tuple-element.79.refs_0_, bf16[80,2432]{1,0:T(8,128)(2,1)S(1)} %collective-permute-done.4.refs_1_, bf16[384,2432]{1,0:T(8,128)(2,1)S(1)} %bitcast.76, ...), custom_call_target="tpu_custom_call" | custom-call | flops 57500000 | tf_op jit(solution)/shard_map/project/pallas_call | solution.py:42
  26.9 4.9 %attend.3 = (bf16[1280,384]{1,0:T(8,128)(2,1)S(1)}, f32[10,768,768]{2,1,0:T(8,128)}, f32[10,2,768]{2,1,0:T(2,128)S(1)}, bf16[768,1280]{1,0:T(8,128)(2,1)S(1)}, f32[8,128]{1,0:T(8,128)S(1)}) custom-call(bf16[384,1280]{1,0:T(8,128)(2,1)S(1)} %bitcast.64, bf16[384,1280]{1,0:T(8,128)(2,1)S(1)} %bitcast.44, bf16[384,1280]{1,0:T(8,128)(2,1)S(1)} %bitcast.55, ...), custom_call_target="tpu_custom_call" | custom-call | flops 3277499904 | tf_op jit(solution)/shard_map/attend/pallas_call | solution.py:42
  31.8 2.8 %collective-permute-done.2.refs_1_ = bf16[80,2432]{1,0:T(8,128)(2,1)S(1)} collective-permute-done((bf16[80,2432]{1,0:T(8,128)(2,1)S(1)}, bf16[80,2432]{1,0:T(8,128)(2,1)S(1)}, u32[]{:S(2)}, u32[]{:S(2)}) %collective-permute-start.2) | collective-permute-done | bytes 389152 | tf_op jit(solution)/shard_map/ppermute | solution.py:340
  34.7 1.9 %collective-permute-start.9 = (bf16[160,2432]{1,0:T(8,128)(2,1)S(1)}, bf16[160,2432]{1,0:T(8,128)(2,1)S(1)}, u32[]{:S(2)}, u32[]{:S(2)}) collective-permute-start(bf16[160,2432]{1,0:T(8,128)(2,1)S(1)} %get-tuple-element.99), channel_id=1, source_target_pairs={{0,2},{1,3},{2,0},{3,1},{4,6},{5,7},{6,4},{7,5},{8,10},{9,11},{10,... | collective-permute-start | bytes 2334728 | tf_op jit(solution)/shard_map/ppermute | solution.py:335
  38.8 1.9 %collective-permute-done.7.refs_3_ = bf16[768,512]{1,0:T(8,128)(2,1)S(1)} collective-permute-done((bf16[768,512]{1,0:T(8,128)(2,1)S(1)}, bf16[768,512]{1,0:T(8,128)(2,1)S(1)}, u32[]{:S(2)}, u32[]{:S(2)}) %collective-permute-start.7) | collective-permute-done | bytes 786464 | tf_op jit(solution)/shard_map/ppermute | solution.py:335
  40.7 6.3 %attend.4 = (bf16[1280,384]{1,0:T(8,128)(2,1)S(1)}, f32[10,768,768]{2,1,0:T(8,128)}, f32[10,2,768]{2,1,0:T(2,128)S(1)}, bf16[768,1280]{1,0:T(8,128)(2,1)S(1)}, f32[8,128]{1,0:T(8,128)S(1)}) custom-call(bf16[384,1280]{1,0:T(8,128)(2,1)S(1)} %bitcast.65, ...), custom_call_target="tpu_custom_call", output_to_operand_aliasing={{0}: (4, {}), {1}: (5, {}), {2}: (6, {}), {3}: (7, {})} | custom-call | flops 4369999872 | tf_op jit(solution)/shard_map/attend/pallas_call | solution.py:42
  47.0 9.3 %collective-permute-done.8.refs_0_.refs_2_ = bf16[80,2432]{1,0:T(8,128)(2,1)S(1)} collective-permute-done((bf16[80,2432]{1,0:T(8,128)(2,1)S(1)}, bf16[80,2432]{1,0:T(8,128)(2,1)S(1)}, u32[]{:S(2)}, u32[]{:S(2)}) %collective-permute-start.8) | collective-permute-done | bytes 389152 | tf_op jit(solution)/shard_map/ppermute | solution.py:340
  57.2 5.0 %attend.5 = (bf16[1280,384]{1,0:T(8,128)(2,1)S(1)}, f32[10,768,768]{2,1,0:T(8,128)}, f32[10,2,768]{2,1,0:T(2,128)S(1)}, bf16[768,1280]{1,0:T(8,128)(2,1)S(1)}, f32[8,128]{1,0:T(8,128)S(1)}) custom-call(bf16[384,1280]{1,0:T(8,128)(2,1)S(1)} %bitcast.67, ...), custom_call_target="tpu_custom_call", output_to_operand_aliasing={{0}: (4, {}), {1}: (5, {}), {2}: (6, {}), {3}: (7, {})} | custom-call | flops 3277499904 | tf_op jit(solution)/shard_map/attend/pallas_call | solution.py:42
  64.9 1.6 %collective-permute-start.15 = (bf16[384,1280]{1,0:T(8,128)(2,1)}, bf16[384,1280]{1,0:T(8,128)(2,1)S(1)}, u32[]{:S(2)}, u32[]{:S(2)}) collective-permute-start(bf16[384,1280]{1,0:T(8,128)(2,1)} %copy-done.13), channel_id=1, source_target_pairs={{0,16},{16,0},{1,17},{17,1},{2,18},{18,2},{3,19},{19,3},{4,20},{20... | collective-permute-start | bytes 2949128 | tf_op jit(solution)/shard_map/ppermute | solution.py:335
  69.6 5.8 %outer.1 = (bf16[1,80,2432]{2,1,0:T(8,128)(2,1)S(1)}, bf16[1,80,2432]{2,1,0:T(8,128)(2,1)S(1)}, bf16[2,80,2432]{2,1,0:T(8,128)(2,1)S(1)}, bf16[4,80,2432]{2,1,0:T(8,128)(2,1)S(1)}, f32[8,128]{1,0:T(8,128)S(1)}) custom-call(s32[8]{0:T(128)S(1)} %stack.71.refs_0_, bf16[16,80,384]{2,1,0:T(8,128)(2,1)S(1)} %bitcast.34, bf16[16,80,384]{2,1,0:T(8,128)(2,1)S(1)} %bitcast.35, ...), custom_call_target="tpu_custom_call" | custom-call | flops 3449999872 | tf_op jit(solution)/shard_map/outer/pallas_call | solution.py:42
  76.5 5.2 %project.3 = (bf16[6,80,384]{2,1,0:T(8,128)(2,1)S(1)}, bf16[6,80,384]{2,1,0:T(8,128)(2,1)S(1)}, f32[8,128]{1,0:T(8,128)S(1)}) custom-call(bf16[80,2432]{1,0:T(8,128)(2,1)S(1)} %copy-done.19, bf16[80,2432]{1,0:T(8,128)(2,1)S(1)} %copy-done.21, bf16[80,2432]{1,0:T(8,128)(2,1)S(1)} %collective-permute-done.8.refs_0_.refs_2_, bf16[160,2432]{1,0:T(8,128)(2,1)S(1)} %copy-done.15, ...), custom_call_target="tpu_custom_call" | custom-call | flops 2357499904 | tf_op jit(solution)/shard_map/project/pallas_call | solution.py:42
  82.9 4.4 %collective-permute-done.14.refs_1_ = bf16[1,80,2432]{2,1,0:T(8,128)(2,1)S(1)} collective-permute-done((bf16[1,80,2432]{2,1,0:T(8,128)(2,1)S(1)}, bf16[1,80,2432]{2,1,0:T(8,128)(2,1)S(1)}, u32[]{:S(2)}, u32[]{:S(2)}) %collective-permute-start.14) | collective-permute-done | bytes 389152 | tf_op jit(solution)/shard_map/ppermute | solution.py:335
  89.7 1.7 %collective-permute-start.18 = (bf16[1280,384]{1,0:T(8,128)(2,1)S(1)}, bf16[1280,384]{1,0:T(8,128)(2,1)S(1)}, u32[]{:S(2)}, u32[]{:S(2)}) collective-permute-start(bf16[1280,384]{1,0:T(8,128)(2,1)S(1)} %bitcast.71), channel_id=1, source_target_pairs={{0,16},{16,0},{1,17},{17,1},{2,18},{18,2},{3,19},{19,3},{4,20},{20... | collective-permute-start | bytes 2949128 | tf_op jit(solution)/shard_map/ppermute | solution.py:335
  91.4 10.9 %back.3 = (bf16[384,1280]{1,0:T(8,128)(2,1)}, f32[384,1280]{1,0:T(8,128)S(1)}, f32[384,1280]{1,0:T(8,128)S(1)}, f32[10,3,768]{2,1,0:T(4,128)S(1)}, f32[8,128]{1,0:T(8,128)S(1)}) custom-call(f32[10,768,768]{2,1,0:T(8,128)} %get-tuple-element.101.refs_0_, f32[10,2,768]{2,1,0:T(2,128)S(1)} %get-tuple-element.102.refs_1_, bf16[384,1280]{1,0:T(8,128)(2,1)S(1)} %bitcast.68, ...), custom_call_target="tpu_custom_call" | custom-call | flops 6899999744 | tf_op jit(solution)/shard_map/back/pallas_call | solution.py:42
  102.4 1.6 %collective-permute-start.21 = (bf16[80,2432]{1,0:T(8,128)(2,1)S(1)}, bf16[80,2432]{1,0:T(8,128)(2,1)S(1)}, u32[]{:S(2)}, u32[]{:S(2)}) collective-permute-start(bf16[80,2432]{1,0:T(8,128)(2,1)S(1)} %get-tuple-element.139), channel_id=1, source_target_pairs={{0,4},{4,8},{8,12},{12,0},{1,5},{5,9},{9,13},{13,1},{2,6},{6,10},{... | collective-permute-start | bytes 1167368 | tf_op jit(solution)/shard_map/ppermute | solution.py:340
  104.0 6.5 %back.4 = (bf16[384,1280]{1,0:T(8,128)(2,1)}, f32[384,1280]{1,0:T(8,128)S(1)}, f32[384,1280]{1,0:T(8,128)S(1)}, f32[10,3,768]{2,1,0:T(4,128)S(1)}, f32[8,128]{1,0:T(8,128)S(1)}) custom-call(f32[10,768,768]{2,1,0:T(8,128)} %get-tuple-element.101.refs_0_, ...), custom_call_target="tpu_custom_call", output_to_operand_aliasing={{0}: (7, {}), {1}: (8, {}), {2}: (9, {}), {3}: (10, {})} | custom-call | flops 3449999872 | tf_op jit(solution)/shard_map/back/pallas_call | solution.py:42
  110.5 3.5 %back.5 = (bf16[384,1280]{1,0:T(8,128)(2,1)}, f32[384,1280]{1,0:T(8,128)S(1)}, f32[384,1280]{1,0:T(8,128)S(1)}, f32[10,3,768]{2,1,0:T(4,128)S(1)}, f32[8,128]{1,0:T(8,128)S(1)}) custom-call(f32[10,768,768]{2,1,0:T(8,128)} %get-tuple-element.101.refs_0_, ...), custom_call_target="tpu_custom_call", output_to_operand_aliasing={{0}: (7, {}), {1}: (8, {}), {2}: (9, {}), {3}: (10, {})} | custom-call | flops 1150000000 | tf_op jit(solution)/shard_map/back/pallas_call | solution.py:42
  115.2 2.9 %collective-permute-start.22 = (bf16[80,2432]{1,0:T(8,128)(2,1)S(1)}, bf16[80,2432]{1,0:T(8,128)(2,1)S(1)}, u32[]{:S(2)}, u32[]{:S(2)}) collective-permute-start(bf16[80,2432]{1,0:T(8,128)(2,1)S(1)} %get-tuple-element.143), channel_id=1, source_target_pairs={{0,12},{4,0},{8,4},{12,8},{1,13},{5,1},{9,5},{13,9},{2,14},{6,2},{... | collective-permute-start | bytes 1167368 | tf_op jit(solution)/shard_map/ppermute | solution.py:340
  118.9 5.2 %cross.2 = (bf16[384,1280]{1,0:T(8,128)(2,1)}, bf16[384,1280]{1,0:T(8,128)(2,1)}, f32[8,128]{1,0:T(8,128)S(1)}) custom-call(bf16[384,1280]{1,0:T(8,128)(2,1)S(1)} %collective-permute-done.15.refs_7_.refs_0_, bf16[384,1280]{1,0:T(8,128)(2,1)S(1)} %bitcast.51, bf16[384,1280]{1,0:T(8,128)(2,1)S(1)} %bitcast.62, ...), custom_call_target="tpu_custom_call" | custom-call | flops 4312500224 | tf_op jit(solution)/shard_map/cross/pallas_call | solution.py:42
  126.4 5.2 %cross.3 = (bf16[384,1280]{1,0:T(8,128)(2,1)}, bf16[384,1280]{1,0:T(8,128)(2,1)}, f32[8,128]{1,0:T(8,128)S(1)}) custom-call(bf16[384,1280]{1,0:T(8,128)(2,1)S(1)} %collective-permute-done.15.refs_7_.refs_0_, bf16[384,1280]{1,0:T(8,128)(2,1)S(1)} %bitcast.52, bf16[384,1280]{1,0:T(8,128)(2,1)S(1)} %bitcast.63, ...), custom_call_target="tpu_custom_call", output_to_operand_aliasing={{0}: (7, {}), {1}: (8, {})} | custom-call | flops 4312500224 | tf_op jit(solution)/shard_map/cross/pallas_call | solution.py:42
  (110 shorter events, 33.6 us)
Async XLA Ops:
  0.6 8.3 %collective-permute-start = (bf16[80,1216]{1,0:T(8,128)(2,1)}, bf16[80,1216]{1,0:T(8,128)(2,1)S(1)}, u32[]{:S(2)}, u32[]{:S(2)}) collective-permute-start(bf16[80,1216]{1,0:T(8,128)(2,1)} %refs_1_.1), channel_id=1, source_target_pairs={{0,16},{16,0},{1,17},{17,1},{2,18},{18,2},{3,19},{19,3},{4,20},{20... | collective-permute-start | bytes 583688 | tf_op jit(solution)/shard_map/ppermute | solution.py:335
  3.6 9.8 %collective-permute-start.5 = (bf16[384,2432]{1,0:T(8,128)(2,1)}, bf16[384,2432]{1,0:T(8,128)(2,1)S(1)}, u32[]{:S(2)}, u32[]{:S(2)}) collective-permute-start(bf16[384,2432]{1,0:T(8,128)(2,1)} %bitcast.75), channel_id=1, source_target_pairs={{0,1},{1,0},{2,3},{3,2},{4,5},{5,4},{6,7},{7,6},{8,9},{9,8},{10,11... | collective-permute-start | bytes 5603336 | tf_op jit(solution)/shard_map/ppermute | solution.py:335
  7.5 17.5 %collective-permute-start.3 = (bf16[768,384]{1,0:T(8,128)(2,1)}, bf16[768,384]{1,0:T(8,128)(2,1)S(1)}, u32[]{:S(2)}, u32[]{:S(2)}) collective-permute-start(bf16[768,384]{1,0:T(8,128)(2,1)} %get-tuple-element.80), channel_id=1, source_target_pairs={{0,16},{16,0},{1,17},{17,1},{2,18},{18,2},{3,19},{19,3},{4,20},{20... | collective-permute-start | bytes 1769480 | tf_op jit(solution)/shard_map/ppermute | solution.py:335
  11.6 10.3 %collective-permute-start.4 = (bf16[80,2432]{1,0:T(8,128)(2,1)S(1)}, bf16[80,2432]{1,0:T(8,128)(2,1)S(1)}, u32[]{:S(2)}, u32[]{:S(2)}) collective-permute-start(bf16[80,2432]{1,0:T(8,128)(2,1)S(1)} %get-tuple-element.79.refs_0_), channel_id=1, source_target_pairs={{0,2},{1,3},{2,0},{3,1},{4,6},{5,7},{6,4},{7,5},{8,10},{9,11},{10,... | collective-permute-start | bytes 1167368 | tf_op jit(solution)/shard_map/ppermute | solution.py:335
  13.9 26.8 %collective-permute-start.7 = (bf16[768,512]{1,0:T(8,128)(2,1)S(1)}, bf16[768,512]{1,0:T(8,128)(2,1)S(1)}, u32[]{:S(2)}, u32[]{:S(2)}) collective-permute-start(bf16[768,512]{1,0:T(8,128)(2,1)S(1)} %get-tuple-element.87), channel_id=1, source_target_pairs={{0,16},{16,0},{1,17},{17,1},{2,18},{18,2},{3,19},{19,3},{4,20},{20... | collective-permute-start | bytes 2359304 | tf_op jit(solution)/shard_map/ppermute | solution.py:335
  15.5 16.3 %collective-permute-start.1 = (bf16[80,2432]{1,0:T(8,128)(2,1)S(1)}, bf16[80,2432]{1,0:T(8,128)(2,1)S(1)}, u32[]{:S(2)}, u32[]{:S(2)}) collective-permute-start(bf16[80,2432]{1,0:T(8,128)(2,1)S(1)} %get-tuple-element.79.refs_0_), channel_id=1, source_target_pairs={{0,4},{4,8},{8,12},{12,0},{1,5},{5,9},{9,13},{13,1},{2,6},{6,10},{... | collective-permute-start | bytes 1167368 | tf_op jit(solution)/shard_map/ppermute | solution.py:340
  17.0 17.6 %collective-permute-start.2 = (bf16[80,2432]{1,0:T(8,128)(2,1)S(1)}, bf16[80,2432]{1,0:T(8,128)(2,1)S(1)}, u32[]{:S(2)}, u32[]{:S(2)}) collective-permute-start(bf16[80,2432]{1,0:T(8,128)(2,1)S(1)} %get-tuple-element.79.refs_0_), channel_id=1, source_target_pairs={{0,12},{4,0},{8,4},{12,8},{1,13},{5,1},{9,5},{13,9},{2,14},{6,2},{... | collective-permute-start | bytes 1167368 | tf_op jit(solution)/shard_map/ppermute | solution.py:340
  34.7 21.7 %collective-permute-start.9 = (bf16[160,2432]{1,0:T(8,128)(2,1)S(1)}, bf16[160,2432]{1,0:T(8,128)(2,1)S(1)}, u32[]{:S(2)}, u32[]{:S(2)}) collective-permute-start(bf16[160,2432]{1,0:T(8,128)(2,1)S(1)} %get-tuple-element.99), channel_id=1, source_target_pairs={{0,2},{1,3},{2,0},{3,1},{4,6},{5,7},{6,4},{7,5},{8,10},{9,11},{10,... | collective-permute-start | bytes 2334728 | tf_op jit(solution)/shard_map/ppermute | solution.py:335
  36.9 20.3 %collective-permute-start.6 = (bf16[768,384]{1,0:T(8,128)(2,1)S(1)}, bf16[768,384]{1,0:T(8,128)(2,1)S(1)}, u32[]{:S(2)}, u32[]{:S(2)}) collective-permute-start(bf16[768,384]{1,0:T(8,128)(2,1)S(1)} %get-tuple-element.86), channel_id=1, source_target_pairs={{0,16},{16,0},{1,17},{17,1},{2,18},{18,2},{3,19},{19,3},{4,20},{20... | collective-permute-start | bytes 1769480 | tf_op jit(solution)/shard_map/ppermute | solution.py:335
  37.5 18.8 %collective-permute-start.8 = (bf16[80,2432]{1,0:T(8,128)(2,1)S(1)}, bf16[80,2432]{1,0:T(8,128)(2,1)S(1)}, u32[]{:S(2)}, u32[]{:S(2)}) collective-permute-start(bf16[80,2432]{1,0:T(8,128)(2,1)S(1)} %get-tuple-element.79.refs_0_), channel_id=1, source_target_pairs={{0,8},{4,12},{8,0},{12,4},{1,9},{5,13},{9,1},{13,5},{2,10},{6,14},... | collective-permute-start | bytes 1167368 | tf_op jit(solution)/shard_map/ppermute | solution.py:340
  63.5 3.0 %collective-permute-start.11 = (bf16[16,80,384]{2,1,0:T(8,128)(2,1)S(1)}, bf16[16,80,384]{2,1,0:T(8,128)(2,1)S(1)}, u32[]{:S(2)}, u32[]{:S(2)}) collective-permute-start(bf16[16,80,384]{2,1,0:T(8,128)(2,1)S(1)} %bitcast.33), channel_id=1, source_target_pairs={{0,1},{1,0},{2,3},{3,2},{4,5},{5,4},{6,7},{7,6},{8,9},{9,8},{10,11... | collective-permute-start | bytes 2949128 | tf_op jit(solution)/shard_map/ppermute | solution.py:335
  63.5 13.0 %collective-permute-start.10 = (bf16[80,2432]{1,0:T(8,128)(2,1)}, bf16[80,2432]{1,0:T(8,128)(2,1)}, u32[]{:S(2)}, u32[]{:S(2)}) collective-permute-start(bf16[80,2432]{1,0:T(8,128)(2,1)} %get-tuple-element.105), channel_id=1, source_target_pairs={{0,2},{1,3},{2,0},{3,1},{4,6},{5,7},{6,4},{7,5},{8,10},{9,11},{10,... | collective-permute-start | bytes 1167368 | tf_op jit(solution)/shard_map/ppermute | solution.py:335
  64.6 23.9 %collective-permute-start.12 = (bf16[2,80,384]{2,1,0:T(8,128)(2,1)S(1)}, bf16[2,80,384]{2,1,0:T(8,128)(2,1)S(1)}, u32[]{:S(2)}, u32[]{:S(2)}) collective-permute-start(bf16[2,80,384]{2,1,0:T(8,128)(2,1)S(1)} %copy-done.28), channel_id=1, source_target_pairs={{0,1},{1,0},{2,3},{3,2},{4,5},{5,4},{6,7},{7,6},{8,9},{9,8},{10,11... | collective-permute-start | bytes 368648 | tf_op jit(solution)/shard_map/ppermute | solution.py:335
  64.9 24.2 %collective-permute-start.15 = (bf16[384,1280]{1,0:T(8,128)(2,1)}, bf16[384,1280]{1,0:T(8,128)(2,1)S(1)}, u32[]{:S(2)}, u32[]{:S(2)}) collective-permute-start(bf16[384,1280]{1,0:T(8,128)(2,1)} %copy-done.13), channel_id=1, source_target_pairs={{0,16},{16,0},{1,17},{17,1},{2,18},{18,2},{3,19},{19,3},{4,20},{20... | collective-permute-start | bytes 2949128 | tf_op jit(solution)/shard_map/ppermute | solution.py:335
  75.4 12.0 %collective-permute-start.14 = (bf16[1,80,2432]{2,1,0:T(8,128)(2,1)S(1)}, bf16[1,80,2432]{2,1,0:T(8,128)(2,1)S(1)}, u32[]{:S(2)}, u32[]{:S(2)}) collective-permute-start(bf16[1,80,2432]{2,1,0:T(8,128)(2,1)S(1)} %get-tuple-element.113), channel_id=1, source_target_pairs={{0,2},{1,3},{2,0},{3,1},{4,6},{5,7},{6,4},{7,5},{8,10},{9,11},{10,... | collective-permute-start | bytes 1167368 | tf_op jit(solution)/shard_map/ppermute | solution.py:335
  81.8 7.2 %collective-permute-start.13 = (bf16[6,80,384]{2,1,0:T(8,128)(2,1)S(1)}, bf16[6,80,384]{2,1,0:T(8,128)(2,1)S(1)}, u32[]{:S(2)}, u32[]{:S(2)}) collective-permute-start(bf16[6,80,384]{2,1,0:T(8,128)(2,1)S(1)} %get-tuple-element.111), channel_id=1, source_target_pairs={{0,1},{1,0},{2,3},{3,2},{4,5},{5,4},{6,7},{7,6},{8,9},{9,8},{10,11... | collective-permute-start | bytes 1105928 | tf_op jit(solution)/shard_map/ppermute | solution.py:335
  81.9 20.4 %collective-permute-start.16 = (bf16[1,80,2432]{2,1,0:T(8,128)(2,1)S(1)}, bf16[1,80,2432]{2,1,0:T(8,128)(2,1)S(1)}, u32[]{:S(2)}, u32[]{:S(2)}) collective-permute-start(bf16[1,80,2432]{2,1,0:T(8,128)(2,1)S(1)} %get-tuple-element.123), channel_id=1, source_target_pairs={{0,2},{1,3},{2,0},{3,1},{4,6},{5,7},{6,4},{7,5},{8,10},{9,11},{10,... | collective-permute-start | bytes 1167368 | tf_op jit(solution)/shard_map/ppermute | solution.py:335
  87.3 27.7 %collective-permute-start.20 = (bf16[2,80,2432]{2,1,0:T(8,128)(2,1)S(1)}, bf16[2,80,2432]{2,1,0:T(8,128)(2,1)S(1)}, u32[]{:S(2)}, u32[]{:S(2)}) collective-permute-start(bf16[2,80,2432]{2,1,0:T(8,128)(2,1)S(1)} %get-tuple-element.136), channel_id=1, source_target_pairs={{0,2},{1,3},{2,0},{3,1},{4,6},{5,7},{6,4},{7,5},{8,10},{9,11},{10,... | collective-permute-start | bytes 2334728 | tf_op jit(solution)/shard_map/ppermute | solution.py:335
  88.5 22.0 %collective-permute-start.17 = (bf16[80,2432]{1,0:T(8,128)(2,1)S(1)}, bf16[80,2432]{1,0:T(8,128)(2,1)S(1)}, u32[]{:S(2)}, u32[]{:S(2)}) collective-permute-start(bf16[80,2432]{1,0:T(8,128)(2,1)S(1)} %get-tuple-element.131), channel_id=1, source_target_pairs={{0,8},{4,12},{8,0},{12,4},{1,9},{5,13},{9,1},{13,5},{2,10},{6,14},... | collective-permute-start | bytes 1167368 | tf_op jit(solution)/shard_map/ppermute | solution.py:340
  89.7 29.2 %collective-permute-start.18 = (bf16[1280,384]{1,0:T(8,128)(2,1)S(1)}, bf16[1280,384]{1,0:T(8,128)(2,1)S(1)}, u32[]{:S(2)}, u32[]{:S(2)}) collective-permute-start(bf16[1280,384]{1,0:T(8,128)(2,1)S(1)} %bitcast.71), channel_id=1, source_target_pairs={{0,16},{16,0},{1,17},{17,1},{2,18},{18,2},{3,19},{19,3},{4,20},{20... | collective-permute-start | bytes 2949128 | tf_op jit(solution)/shard_map/ppermute | solution.py:335
  102.4 15.7 %collective-permute-start.21 = (bf16[80,2432]{1,0:T(8,128)(2,1)S(1)}, bf16[80,2432]{1,0:T(8,128)(2,1)S(1)}, u32[]{:S(2)}, u32[]{:S(2)}) collective-permute-start(bf16[80,2432]{1,0:T(8,128)(2,1)S(1)} %get-tuple-element.139), channel_id=1, source_target_pairs={{0,4},{4,8},{8,12},{12,0},{1,5},{5,9},{9,13},{13,1},{2,6},{6,10},{... | collective-permute-start | bytes 1167368 | tf_op jit(solution)/shard_map/ppermute | solution.py:340
  114.0 4.9 %collective-permute-start.19 = (f32[10,3,768]{2,1,0:T(4,128)S(1)}, f32[10,3,768]{2,1,0:T(4,128)S(1)}, u32[]{:S(2)}, u32[]{:S(2)}) collective-permute-start(f32[10,3,768]{2,1,0:T(4,128)S(1)} %get-tuple-element.133), channel_id=1, source_target_pairs={{0,16},{16,0},{1,17},{17,1},{2,18},{18,2},{3,19},{19,3},{4,20},{20... | collective-permute-start | bytes 276488 | tf_op jit(solution)/shard_map/ppermute | solution.py:335
  115.2 10.3 %collective-permute-start.22 = (bf16[80,2432]{1,0:T(8,128)(2,1)S(1)}, bf16[80,2432]{1,0:T(8,128)(2,1)S(1)}, u32[]{:S(2)}, u32[]{:S(2)}) collective-permute-start(bf16[80,2432]{1,0:T(8,128)(2,1)S(1)} %get-tuple-element.143), channel_id=1, source_target_pairs={{0,12},{4,0},{8,4},{12,8},{1,13},{5,1},{9,5},{13,9},{2,14},{6,2},{... | collective-permute-start | bytes 1167368 | tf_op jit(solution)/shard_map/ppermute | solution.py:340
  125.9 5.8 %collective-permute-start.23 = (bf16[80,1216]{1,0:T(8,128)(2,1)S(1)}, bf16[80,1216]{1,0:T(8,128)(2,1)S(1)}, u32[]{:S(2)}, u32[]{:S(2)}) collective-permute-start(bf16[80,1216]{1,0:T(8,128)(2,1)S(1)} %get-tuple-element.149), channel_id=1, source_target_pairs={{0,16},{16,0},{1,17},{17,1},{2,18},{18,2},{3,19},{19,3},{4,20},{20... | collective-permute-start | bytes 583688 | tf_op jit(solution)/shard_map/ppermute | solution.py:335
  (29 other events, 105.5 us)

commit v4 on v3

--- a/solution.py
+++ b/solution.py
@@ -105,11 +105,11 @@
     v = jnp.concatenate([v_ref[...], kv_ref[n:]], 0)
     s = nt(k, stack_heads(q_ref[...]))
     top = jnp.max(s, axis=0, keepdims=True)
-    e = jnp.exp2((s - top) * (SCALE * LOG2E))
+    e = jnp.exp2((s - top) * (SCALE * LOG2E)).astype(BF16)
     p_ref[0] = e
-    inverse = 1.0 / jnp.sum(e, axis=0, keepdims=True)
+    inverse = 1.0 / jnp.sum(e.astype(F32), axis=0, keepdims=True)
     stat_ref[0] = jnp.concatenate([top, inverse], 0)
-    att_ref[...] = own_heads(mm(v.T, e.astype(BF16)) * inverse).astype(BF16)
+    att_ref[...] = own_heads(mm(v.T, e) * inverse).astype(BF16)
     far_ref[...] = kv_ref[...]
 
 
@@ -121,11 +121,11 @@
         attend_kernel, "attend",
         [q, k, v, kv], [column(n, first)] * 3 + [column(2 * n, 0)],
         [
-            ((width, n), BF16), ((count, 2 * n, 2 * n), F32),
+            ((width, n), BF16), ((2 * count, 2 * n, 2 * n), BF16),
             ((count, 2, 2 * n), F32), ((2 * n, width), BF16),
         ],
         [pl.BlockSpec((PAIR, n), lambda i: (first + i, 0)), at(2 * n, 2 * n), at(2, 2 * n), column(2 * n, first)],
-        (pairs,), after, state, us=1.9 * pairs, vmem=BIG,
+        (pairs,), after, state, us=0.4 * pairs, vmem=BIG,
     )
 
 
@@ -135,7 +135,7 @@
     v = jnp.concatenate([v_ref[...], kv_ref[n:]], 0)
     q = stack_heads(q_ref[...])
     d = spread_heads(d_ref[...])
-    p = p_ref[0] * stat_ref[0, 1:]
+    p = p_ref[0].astype(F32) * stat_ref[0, 1:]
     dp = mm(v, d)
     delta = jnp.sum(p * dp, axis=0, keepdims=True)
     ds = (p * (dp - delta)).astype(BF16)
@@ -157,7 +157,7 @@
         + [column(2 * n, first), pl.BlockSpec((PAIR, n), lambda i: (first + i, 0))],
         [((n, width), BF16)] + [((n, width), F32)] * 2 + [((width // PAIR, 3, 2 * n), F32)],
         [column(n, first)] * 3 + [at(3, 2 * n)],
-        (pairs,), after, done, us=2 * pairs, vmem=BIG,
+        (pairs,), after, done, us=0.1 if first else 2 * pairs, vmem=BIG,
     )
 
 
@@ -165,7 +165,8 @@
     q = stack_heads(q_ref[...])
     d = spread_heads(d_ref[...])
     top, inverse, delta = (stat_ref[0, i : i + 1] for i in range(3))
-    p = jnp.exp2((nt(k_ref[...], q) - top) * (SCALE * LOG2E)) * inverse
+    e = jnp.exp2((nt(k_ref[...], q) - top) * (SCALE * LOG2E)).astype(BF16)
+    p = e.astype(F32) * inverse
     ds = (p * (mm(v_ref[...], d) - delta)).astype(BF16)
     gv_ref[...] = (nt(p.astype(BF16), d) + dv_ref[...]).astype(BF16)
     gk_ref[...] = ((mm(ds, q) + dk_ref[...]) * SCALE).astype(BF16)
@@ -427,9 +428,9 @@
         (x,), token = add(stay[1:2], away[1], (BF16,), after)
         sums.append(shift(x, "band", LATE[1]))
         dq, after = backward(1, dq, (token,))
-        (dq, *share), after = backward(2, dq, (*after, sums[0]))
+        (dq, *share), after = backward(2, dq, after)
         share[2] = swap(share[2], "cam")
-        (x, base), token = add(stay[2:], away[2], (BF16, F32), after)
+        (x, base), token = add(stay[2:], away[2], (BF16, F32), (*after, sums[0]))
         sums.append(shift(x, "band", LATE[2]))
         grads, token = cross(q_far, k, v, d_far, share, (), 0, pairs // 2, (token, sums[1]))
         (mine, theirs), token = total_of(cam, [base, *sums], (token,))

time: 133 us -> 129 us (0.970)
  waiting for transfers between devices: 25 us -> 19.6 us
  starting transfers between devices: 28 us -> 31.3 us
  local copies, waits for them, and re-layouts: 12.8 us -> 10.3 us
    ppermute x6, waiting for transfers between devices: 13.5 us -> 5.52 us  [shift(): return lax.ppermute(x, axis, [(i, (i + step) % size) for i in range(size)])]
    ppermute x18, waiting for transfers between devices: 11.5 us -> 14.1 us  [swap(): return lax.ppermute(x, axis, [(i, i ^ bit) for i in range(size)])]
    unnamed x58 -> x42, local copies, waits for them, and re-layouts: 12.5 us -> 9.98 us
    ppermute x6, starting transfers between devices: 9.69 us -> 11.9 us  [shift(): return lax.ppermute(x, axis, [(i, (i + step) % size) for i in range(size)])]
  transfers between devices with their start and end apart: 24 -> 24, of which waited for: 10 -> 9; matrix products, arithmetic and copies ran while one was open for 0% -> 0% of each run, Pallas kernels for 45% -> 47%
where the time goes in v4:
time: 129 us
  Pallas kernels  66.7 us (52%)
  starting transfers between devices  31.3 us (24%)
  waiting for transfers between devices  19.6 us (15%)
  local copies, waits for them, and re-layouts  10.3 us (8%)
    pallas_call x24, Pallas kernels, run(): pl.pallas_call(wrapped, grid_spec=pltpu.PrefetchScalarGridSpec(num_scalar...  66.7 us
    ppermute x18, starting transfers between devices, swap(): return lax.ppermute(x, axis, [(i, i ^ bit) for i in range(size)])  19.4 us
    ppermute x18, waiting for transfers between devices, swap(): return lax.ppermute(x, axis, [(i, i ^ bit) for i in range(size)])  14.1 us
    ppermute x6, starting transfers between devices, shift(): return lax.ppermute(x, axis, [(i, (i + step) % size) for i in range(size)])  11.9 us
    unnamed x42, local copies, waits for them, and re-layouts  9.98 us
    ppermute x6, waiting for transfers between devices, shift(): return lax.ppermute(x, axis, [(i, (i + step) % size) for i in range(size)])  5.52 us
  transfers between devices with their start and end apart: 24, of which 9 were waited for; matrix products, arithmetic and copies ran while one was open for 0% of the time, Pallas kernels for 47%

profile of v4, /device:TPU:0, one launch (start us, length us, event | category | flops | bytes accessed | tf_op | source)
XLA Modules:
  0.0 128.8 jit_solution(17540471240301575879)
XLA Ops:
  0.6 3.0 %collective-permute-start = (bf16[80,1216]{1,0:T(8,128)(2,1)}, bf16[80,1216]{1,0:T(8,128)(2,1)S(1)}, u32[]{:S(2)}, u32[]{:S(2)}) collective-permute-start(bf16[80,1216]{1,0:T(8,128)(2,1)} %refs_1_.1), channel_id=1, source_target_pairs={{0,16},{16,0},{1,17},{17,1},{2,18},{18,2},{3,19},{19,3},{4,20},{20... | collective-permute-start | bytes 583688 | tf_op jit(solution)/shard_map/ppermute | solution.py:336
  9.1 1.8 %collective-permute-start.4 = (bf16[80,2432]{1,0:T(8,128)(2,1)S(1)}, bf16[80,2432]{1,0:T(8,128)(2,1)S(1)}, u32[]{:S(2)}, u32[]{:S(2)}) collective-permute-start(bf16[80,2432]{1,0:T(8,128)(2,1)S(1)} %get-tuple-element.79.refs_0_), channel_id=1, source_target_pairs={{0,2},{1,3},{2,0},{3,1},{4,6},{5,7},{6,4},{7,5},{8,10},{9,11},{10,... | collective-permute-start | bytes 1167368 | tf_op jit(solution)/shard_map/ppermute | solution.py:336
  10.9 1.6 %collective-permute-start.1 = (bf16[80,2432]{1,0:T(8,128)(2,1)S(1)}, bf16[80,2432]{1,0:T(8,128)(2,1)S(1)}, u32[]{:S(2)}, u32[]{:S(2)}) collective-permute-start(bf16[80,2432]{1,0:T(8,128)(2,1)S(1)} %get-tuple-element.79.refs_0_), channel_id=1, source_target_pairs={{0,4},{4,8},{8,12},{12,0},{1,5},{5,9},{9,13},{13,1},{2,6},{6,10},{... | collective-permute-start | bytes 1167368 | tf_op jit(solution)/shard_map/ppermute | solution.py:341
  12.5 2.2 %collective-permute-start.2 = (bf16[80,2432]{1,0:T(8,128)(2,1)S(1)}, bf16[80,2432]{1,0:T(8,128)(2,1)S(1)}, u32[]{:S(2)}, u32[]{:S(2)}) collective-permute-start(bf16[80,2432]{1,0:T(8,128)(2,1)S(1)} %get-tuple-element.79.refs_0_), channel_id=1, source_target_pairs={{0,12},{4,0},{8,4},{12,8},{1,13},{5,1},{9,5},{13,9},{2,14},{6,2},{... | collective-permute-start | bytes 1167368 | tf_op jit(solution)/shard_map/ppermute | solution.py:341
  16.7 2.6 %collective-permute-done.4.refs_1_ = bf16[80,2432]{1,0:T(8,128)(2,1)S(1)} collective-permute-done((bf16[80,2432]{1,0:T(8,128)(2,1)S(1)}, bf16[80,2432]{1,0:T(8,128)(2,1)S(1)}, u32[]{:S(2)}, u32[]{:S(2)}) %collective-permute-start.4) | collective-permute-done | bytes 389152 | tf_op jit(solution)/shard_map/ppermute | solution.py:336
  19.4 3.4 %project.2 = (bf16[2,80,384]{2,1,0:T(8,128)(2,1)S(1)}, bf16[2,80,384]{2,1,0:T(8,128)(2,1)S(1)}, f32[8,128]{1,0:T(8,128)S(1)}) custom-call(bf16[80,2432]{1,0:T(8,128)(2,1)S(1)} %get-tuple-element.79.refs_0_, bf16[80,2432]{1,0:T(8,128)(2,1)S(1)} %collective-permute-done.4.refs_1_, bf16[384,2432]{1,0:T(8,128)(2,1)S(1)} %bitcast.76, ...), custom_call_target="tpu_custom_call" | custom-call | flops 57500000 | tf_op jit(solution)/shard_map/project/pallas_call | solution.py:42
  25.7 4.9 %attend.3 = (bf16[1280,384]{1,0:T(8,128)(2,1)S(1)}, bf16[20,768,768]{2,1,0:T(8,128)(2,1)}, f32[10,2,768]{2,1,0:T(2,128)S(1)}, bf16[768,1280]{1,0:T(8,128)(2,1)S(1)}, f32[8,128]{1,0:T(8,128)S(1)}) custom-call(bf16[384,1280]{1,0:T(8,128)(2,1)S(1)} %bitcast.64, bf16[384,1280]{1,0:T(8,128)(2,1)S(1)} %bitcast.44, bf16[384,1280]{1,0:T(8,128)(2,1)S(1)} %bitcast.55, ...), custom_call_target="tpu_custom_call" | custom-call | flops 690000000 | tf_op jit(solution)/shard_map/attend/pallas_call | solution.py:42
  34.5 2.6 %collective-permute-start.8 = (bf16[80,2432]{1,0:T(8,128)(2,1)S(1)}, bf16[80,2432]{1,0:T(8,128)(2,1)S(1)}, u32[]{:S(2)}, u32[]{:S(2)}) collective-permute-start(bf16[80,2432]{1,0:T(8,128)(2,1)S(1)} %get-tuple-element.79.refs_0_), channel_id=1, source_target_pairs={{0,8},{4,12},{8,0},{12,4},{1,9},{5,13},{9,1},{13,5},{2,10},{6,14},... | collective-permute-start | bytes 1167368 | tf_op jit(solution)/shard_map/ppermute | solution.py:341
  37.1 3.6 %collective-permute-done.7.refs_3_ = bf16[768,512]{1,0:T(8,128)(2,1)S(1)} collective-permute-done((bf16[768,512]{1,0:T(8,128)(2,1)S(1)}, bf16[768,512]{1,0:T(8,128)(2,1)S(1)}, u32[]{:S(2)}, u32[]{:S(2)}) %collective-permute-start.7) | collective-permute-done | bytes 786464 | tf_op jit(solution)/shard_map/ppermute | solution.py:336
  40.7 6.4 %attend.4 = (bf16[1280,384]{1,0:T(8,128)(2,1)S(1)}, bf16[20,768,768]{2,1,0:T(8,128)(2,1)}, f32[10,2,768]{2,1,0:T(2,128)S(1)}, bf16[768,1280]{1,0:T(8,128)(2,1)S(1)}, f32[8,128]{1,0:T(8,128)S(1)}) custom-call(bf16[384,1280]{1,0:T(8,128)(2,1)S(1)} %bitcast.65, ...), custom_call_target="tpu_custom_call", output_to_operand_aliasing={{0}: (4, {}), {1}: (5, {}), {2}: (6, {}), {3}: (7, {})} | custom-call | flops 920000000 | tf_op jit(solution)/shard_map/attend/pallas_call | solution.py:42
  48.1 4.7 %collective-permute-done.8.refs_0_.refs_2_ = bf16[80,2432]{1,0:T(8,128)(2,1)S(1)} collective-permute-done((bf16[80,2432]{1,0:T(8,128)(2,1)S(1)}, bf16[80,2432]{1,0:T(8,128)(2,1)S(1)}, u32[]{:S(2)}, u32[]{:S(2)}) %collective-permute-start.8) | collective-permute-done | bytes 389152 | tf_op jit(solution)/shard_map/ppermute | solution.py:341
  53.7 5.0 %attend.5 = (bf16[1280,384]{1,0:T(8,128)(2,1)S(1)}, bf16[20,768,768]{2,1,0:T(8,128)(2,1)}, f32[10,2,768]{2,1,0:T(2,128)S(1)}, bf16[768,1280]{1,0:T(8,128)(2,1)S(1)}, f32[8,128]{1,0:T(8,128)S(1)}) custom-call(bf16[384,1280]{1,0:T(8,128)(2,1)S(1)} %bitcast.67, ...), custom_call_target="tpu_custom_call", output_to_operand_aliasing={{0}: (4, {}), {1}: (5, {}), {2}: (6, {}), {3}: (7, {})} | custom-call | flops 690000000 | tf_op jit(solution)/shard_map/attend/pallas_call | solution.py:42
  64.3 6.8 %outer.1 = (bf16[1,80,2432]{2,1,0:T(8,128)(2,1)S(1)}, bf16[1,80,2432]{2,1,0:T(8,128)(2,1)S(1)}, bf16[2,80,2432]{2,1,0:T(8,128)(2,1)S(1)}, bf16[4,80,2432]{2,1,0:T(8,128)(2,1)S(1)}, f32[8,128]{1,0:T(8,128)S(1)}) custom-call(s32[8]{0:T(128)S(1)} %stack.71.refs_0_, bf16[16,80,384]{2,1,0:T(8,128)(2,1)S(1)} %bitcast.34, bf16[16,80,384]{2,1,0:T(8,128)(2,1)S(1)} %bitcast.35, ...), custom_call_target="tpu_custom_call" | custom-call | flops 3449999872 | tf_op jit(solution)/shard_map/outer/pallas_call | solution.py:42
  72.4 5.5 %project.3 = (bf16[6,80,384]{2,1,0:T(8,128)(2,1)S(1)}, bf16[6,80,384]{2,1,0:T(8,128)(2,1)S(1)}, f32[8,128]{1,0:T(8,128)S(1)}) custom-call(bf16[80,2432]{1,0:T(8,128)(2,1)S(1)} %collective-permute-done.1.refs_0_, bf16[80,2432]{1,0:T(8,128)(2,1)S(1)} %copy-done.16, bf16[80,2432]{1,0:T(8,128)(2,1)S(1)} %copy-done.18, bf16[160,2432]{1,0:T(8,128)(2,1)S(1)} %copy-done.14, ...), custom_call_target="tpu_custom_call" | custom-call | flops 2357499904 | tf_op jit(solution)/shard_map/project/pallas_call | solution.py:42
  78.9 4.1 %collective-permute-done.14.refs_1_ = bf16[1,80,2432]{2,1,0:T(8,128)(2,1)S(1)} collective-permute-done((bf16[1,80,2432]{2,1,0:T(8,128)(2,1)S(1)}, bf16[1,80,2432]{2,1,0:T(8,128)(2,1)S(1)}, u32[]{:S(2)}, u32[]{:S(2)}) %collective-permute-start.14) | collective-permute-done | bytes 389152 | tf_op jit(solution)/shard_map/ppermute | solution.py:336
  84.3 2.2 %collective-permute-start.20 = (bf16[80,2432]{1,0:T(8,128)(2,1)S(1)}, bf16[80,2432]{1,0:T(8,128)(2,1)S(1)}, u32[]{:S(2)}, u32[]{:S(2)}) collective-permute-start(bf16[80,2432]{1,0:T(8,128)(2,1)S(1)} %get-tuple-element.137), channel_id=1, source_target_pairs={{0,8},{4,12},{8,0},{12,4},{1,9},{5,13},{9,1},{13,5},{2,10},{6,14},... | collective-permute-start | bytes 1167368 | tf_op jit(solution)/shard_map/ppermute | solution.py:341
  88.3 9.7 %back.3 = (bf16[384,1280]{1,0:T(8,128)(2,1)}, f32[384,1280]{1,0:T(8,128)S(1)}, f32[384,1280]{1,0:T(8,128)S(1)}, f32[10,3,768]{2,1,0:T(4,128)S(1)}, f32[8,128]{1,0:T(8,128)S(1)}) custom-call(bf16[20,768,768]{2,1,0:T(8,128)(2,1)} %get-tuple-element.101.refs_0_, f32[10,2,768]{2,1,0:T(2,128)S(1)} %get-tuple-element.102.refs_1_, bf16[384,1280]{1,0:T(8,128)(2,1)S(1)} %bitcast.68, ...), custom_call_target="tpu_custom_call" | custom-call | flops 6899999744 | tf_op jit(solution)/shard_map/back/pallas_call | solution.py:42
  98.2 2.1 %collective-permute-start.21 = (bf16[80,2432]{1,0:T(8,128)(2,1)S(1)}, bf16[80,2432]{1,0:T(8,128)(2,1)S(1)}, u32[]{:S(2)}, u32[]{:S(2)}) collective-permute-start(bf16[80,2432]{1,0:T(8,128)(2,1)S(1)} %get-tuple-element.139), channel_id=1, source_target_pairs={{0,4},{4,8},{8,12},{12,0},{1,5},{5,9},{9,13},{13,1},{2,6},{6,10},{... | collective-permute-start | bytes 1167368 | tf_op jit(solution)/shard_map/ppermute | solution.py:341
  100.3 5.7 %back.4 = (bf16[384,1280]{1,0:T(8,128)(2,1)}, f32[384,1280]{1,0:T(8,128)S(1)}, f32[384,1280]{1,0:T(8,128)S(1)}, f32[10,3,768]{2,1,0:T(4,128)S(1)}, f32[8,128]{1,0:T(8,128)S(1)}) custom-call(bf16[20,768,768]{2,1,0:T(8,128)(2,1)} %get-tuple-element.101.refs_0_, ...), custom_call_target="tpu_custom_call", output_to_operand_aliasing={{0}: (7, {}), {1}: (8, {}), {2}: (9, {}), {3}: (10, {})} | custom-call | flops 57500000 | tf_op jit(solution)/shard_map/back/pallas_call | solution.py:42
  106.0 3.1 %back.5 = (bf16[384,1280]{1,0:T(8,128)(2,1)}, f32[384,1280]{1,0:T(8,128)S(1)}, f32[384,1280]{1,0:T(8,128)S(1)}, f32[10,3,768]{2,1,0:T(4,128)S(1)}, f32[8,128]{1,0:T(8,128)S(1)}) custom-call(bf16[20,768,768]{2,1,0:T(8,128)(2,1)} %get-tuple-element.101.refs_0_, ...), custom_call_target="tpu_custom_call", output_to_operand_aliasing={{0}: (7, {}), {1}: (8, {}), {2}: (9, {}), {3}: (10, {})} | custom-call | flops 57500000 | tf_op jit(solution)/shard_map/back/pallas_call | solution.py:42
  112.3 1.7 %collective-permute-done.18.refs_4_ = f32[10,3,768]{2,1,0:T(4,128)S(1)} collective-permute-done((f32[10,3,768]{2,1,0:T(4,128)S(1)}, f32[10,3,768]{2,1,0:T(4,128)S(1)}, u32[]{:S(2)}, u32[]{:S(2)}) %collective-permute-start.18) | collective-permute-done | bytes 92192 | tf_op jit(solution)/shard_map/ppermute | solution.py:336
  114.0 5.3 %cross.2 = (bf16[384,1280]{1,0:T(8,128)(2,1)}, bf16[384,1280]{1,0:T(8,128)(2,1)}, f32[8,128]{1,0:T(8,128)S(1)}) custom-call(bf16[384,1280]{1,0:T(8,128)(2,1)S(1)} %collective-permute-done.15.refs_7_.refs_0_, bf16[384,1280]{1,0:T(8,128)(2,1)S(1)} %bitcast.51, bf16[384,1280]{1,0:T(8,128)(2,1)S(1)} %bitcast.62, ...), custom_call_target="tpu_custom_call" | custom-call | flops 4312500224 | tf_op jit(solution)/shard_map/cross/pallas_call | solution.py:42
  119.8 3.0 %collective-permute-start.23 = (bf16[80,1216]{1,0:T(8,128)(2,1)S(1)}, bf16[80,1216]{1,0:T(8,128)(2,1)S(1)}, u32[]{:S(2)}, u32[]{:S(2)}) collective-permute-start(bf16[80,1216]{1,0:T(8,128)(2,1)S(1)} %get-tuple-element.149), channel_id=1, source_target_pairs={{0,16},{16,0},{1,17},{17,1},{2,18},{18,2},{3,19},{19,3},{4,20},{20... | collective-permute-start | bytes 583688 | tf_op jit(solution)/shard_map/ppermute | solution.py:336
  122.7 5.3 %cross.3 = (bf16[384,1280]{1,0:T(8,128)(2,1)}, bf16[384,1280]{1,0:T(8,128)(2,1)}, f32[8,128]{1,0:T(8,128)S(1)}) custom-call(bf16[384,1280]{1,0:T(8,128)(2,1)S(1)} %collective-permute-done.15.refs_7_.refs_0_, bf16[384,1280]{1,0:T(8,128)(2,1)S(1)} %bitcast.52, bf16[384,1280]{1,0:T(8,128)(2,1)S(1)} %bitcast.63, ...), custom_call_target="tpu_custom_call", output_to_operand_aliasing={{0}: (7, {}), {1}: (8, {})} | custom-call | flops 4312500224 | tf_op jit(solution)/shard_map/cross/pallas_call | solution.py:42
  (94 shorter events, 31.5 us)
Async XLA Ops:
  0.6 8.3 %collective-permute-start = (bf16[80,1216]{1,0:T(8,128)(2,1)}, bf16[80,1216]{1,0:T(8,128)(2,1)S(1)}, u32[]{:S(2)}, u32[]{:S(2)}) collective-permute-start(bf16[80,1216]{1,0:T(8,128)(2,1)} %refs_1_.1), channel_id=1, source_target_pairs={{0,16},{16,0},{1,17},{17,1},{2,18},{18,2},{3,19},{19,3},{4,20},{20... | collective-permute-start | bytes 583688 | tf_op jit(solution)/shard_map/ppermute | solution.py:336
  3.6 11.1 %collective-permute-start.5 = (bf16[384,2432]{1,0:T(8,128)(2,1)}, bf16[384,2432]{1,0:T(8,128)(2,1)}, u32[]{:S(2)}, u32[]{:S(2)}) collective-permute-start(bf16[384,2432]{1,0:T(8,128)(2,1)} %bitcast.75), channel_id=1, source_target_pairs={{0,1},{1,0},{2,3},{3,2},{4,5},{5,4},{6,7},{7,6},{8,9},{9,8},{10,11... | collective-permute-start | bytes 5603336 | tf_op jit(solution)/shard_map/ppermute | solution.py:336
  7.5 16.3 %collective-permute-start.3 = (bf16[768,384]{1,0:T(8,128)(2,1)}, bf16[768,384]{1,0:T(8,128)(2,1)S(1)}, u32[]{:S(2)}, u32[]{:S(2)}) collective-permute-start(bf16[768,384]{1,0:T(8,128)(2,1)} %get-tuple-element.80), channel_id=1, source_target_pairs={{0,16},{16,0},{1,17},{17,1},{2,18},{18,2},{3,19},{19,3},{4,20},{20... | collective-permute-start | bytes 1769480 | tf_op jit(solution)/shard_map/ppermute | solution.py:336
  9.1 10.3 %collective-permute-start.4 = (bf16[80,2432]{1,0:T(8,128)(2,1)S(1)}, bf16[80,2432]{1,0:T(8,128)(2,1)S(1)}, u32[]{:S(2)}, u32[]{:S(2)}) collective-permute-start(bf16[80,2432]{1,0:T(8,128)(2,1)S(1)} %get-tuple-element.79.refs_0_), channel_id=1, source_target_pairs={{0,2},{1,3},{2,0},{3,1},{4,6},{5,7},{6,4},{7,5},{8,10},{9,11},{10,... | collective-permute-start | bytes 1167368 | tf_op jit(solution)/shard_map/ppermute | solution.py:336
  10.9 19.8 %collective-permute-start.1 = (bf16[80,2432]{1,0:T(8,128)(2,1)S(1)}, bf16[80,2432]{1,0:T(8,128)(2,1)S(1)}, u32[]{:S(2)}, u32[]{:S(2)}) collective-permute-start(bf16[80,2432]{1,0:T(8,128)(2,1)S(1)} %get-tuple-element.79.refs_0_), channel_id=1, source_target_pairs={{0,4},{4,8},{8,12},{12,0},{1,5},{5,9},{9,13},{13,1},{2,6},{6,10},{... | collective-permute-start | bytes 1167368 | tf_op jit(solution)/shard_map/ppermute | solution.py:341
  12.5 18.2 %collective-permute-start.2 = (bf16[80,2432]{1,0:T(8,128)(2,1)S(1)}, bf16[80,2432]{1,0:T(8,128)(2,1)S(1)}, u32[]{:S(2)}, u32[]{:S(2)}) collective-permute-start(bf16[80,2432]{1,0:T(8,128)(2,1)S(1)} %get-tuple-element.79.refs_0_), channel_id=1, source_target_pairs={{0,12},{4,0},{8,4},{12,8},{1,13},{5,1},{9,5},{13,9},{2,14},{6,2},{... | collective-permute-start | bytes 1167368 | tf_op jit(solution)/shard_map/ppermute | solution.py:341
  15.2 25.5 %collective-permute-start.7 = (bf16[768,512]{1,0:T(8,128)(2,1)S(1)}, bf16[768,512]{1,0:T(8,128)(2,1)S(1)}, u32[]{:S(2)}, u32[]{:S(2)}) collective-permute-start(bf16[768,512]{1,0:T(8,128)(2,1)S(1)} %get-tuple-element.87), channel_id=1, source_target_pairs={{0,16},{16,0},{1,17},{17,1},{2,18},{18,2},{3,19},{19,3},{4,20},{20... | collective-permute-start | bytes 2359304 | tf_op jit(solution)/shard_map/ppermute | solution.py:336
  31.4 21.4 %collective-permute-start.9 = (bf16[160,2432]{1,0:T(8,128)(2,1)S(1)}, bf16[160,2432]{1,0:T(8,128)(2,1)S(1)}, u32[]{:S(2)}, u32[]{:S(2)}) collective-permute-start(bf16[160,2432]{1,0:T(8,128)(2,1)S(1)} %get-tuple-element.99), channel_id=1, source_target_pairs={{0,2},{1,3},{2,0},{3,1},{4,6},{5,7},{6,4},{7,5},{8,10},{9,11},{10,... | collective-permute-start | bytes 2334728 | tf_op jit(solution)/shard_map/ppermute | solution.py:336
  33.3 20.4 %collective-permute-start.6 = (bf16[768,384]{1,0:T(8,128)(2,1)S(1)}, bf16[768,384]{1,0:T(8,128)(2,1)S(1)}, u32[]{:S(2)}, u32[]{:S(2)}) collective-permute-start(bf16[768,384]{1,0:T(8,128)(2,1)S(1)} %get-tuple-element.86), channel_id=1, source_target_pairs={{0,16},{16,0},{1,17},{17,1},{2,18},{18,2},{3,19},{19,3},{4,20},{20... | collective-permute-start | bytes 1769480 | tf_op jit(solution)/shard_map/ppermute | solution.py:336
  34.5 18.3 %collective-permute-start.8 = (bf16[80,2432]{1,0:T(8,128)(2,1)S(1)}, bf16[80,2432]{1,0:T(8,128)(2,1)S(1)}, u32[]{:S(2)}, u32[]{:S(2)}) collective-permute-start(bf16[80,2432]{1,0:T(8,128)(2,1)S(1)} %get-tuple-element.79.refs_0_), channel_id=1, source_target_pairs={{0,8},{4,12},{8,0},{12,4},{1,9},{5,13},{9,1},{13,5},{2,10},{6,14},... | collective-permute-start | bytes 1167368 | tf_op jit(solution)/shard_map/ppermute | solution.py:341
  60.1 2.7 %collective-permute-start.11 = (bf16[16,80,384]{2,1,0:T(8,128)(2,1)S(1)}, bf16[16,80,384]{2,1,0:T(8,128)(2,1)}, u32[]{:S(2)}, u32[]{:S(2)}) collective-permute-start(bf16[16,80,384]{2,1,0:T(8,128)(2,1)S(1)} %bitcast.33), channel_id=1, source_target_pairs={{0,1},{1,0},{2,3},{3,2},{4,5},{5,4},{6,7},{7,6},{8,9},{9,8},{10,11... | collective-permute-start | bytes 2949128 | tf_op jit(solution)/shard_map/ppermute | solution.py:336
  60.1 12.3 %collective-permute-start.10 = (bf16[80,2432]{1,0:T(8,128)(2,1)}, bf16[80,2432]{1,0:T(8,128)(2,1)}, u32[]{:S(2)}, u32[]{:S(2)}) collective-permute-start(bf16[80,2432]{1,0:T(8,128)(2,1)} %get-tuple-element.105), channel_id=1, source_target_pairs={{0,2},{1,3},{2,0},{3,1},{4,6},{5,7},{6,4},{7,5},{8,10},{9,11},{10,... | collective-permute-start | bytes 1167368 | tf_op jit(solution)/shard_map/ppermute | solution.py:336
  61.3 23.0 %collective-permute-start.12 = (bf16[2,80,384]{2,1,0:T(8,128)(2,1)}, bf16[2,80,384]{2,1,0:T(8,128)(2,1)S(1)}, u32[]{:S(2)}, u32[]{:S(2)}) collective-permute-start(bf16[2,80,384]{2,1,0:T(8,128)(2,1)} %copy-done.20), channel_id=1, source_target_pairs={{0,1},{1,0},{2,3},{3,2},{4,5},{5,4},{6,7},{7,6},{8,9},{9,8},{10,11... | collective-permute-start | bytes 368648 | tf_op jit(solution)/shard_map/ppermute | solution.py:336
  61.6 25.0 %collective-permute-start.15 = (bf16[384,1280]{1,0:T(8,128)(2,1)}, bf16[384,1280]{1,0:T(8,128)(2,1)S(1)}, u32[]{:S(2)}, u32[]{:S(2)}) collective-permute-start(bf16[384,1280]{1,0:T(8,128)(2,1)} %copy-done.12), channel_id=1, source_target_pairs={{0,16},{16,0},{1,17},{17,1},{2,18},{18,2},{3,19},{19,3},{4,20},{20... | collective-permute-start | bytes 2949128 | tf_op jit(solution)/shard_map/ppermute | solution.py:336
  71.1 11.9 %collective-permute-start.14 = (bf16[1,80,2432]{2,1,0:T(8,128)(2,1)S(1)}, bf16[1,80,2432]{2,1,0:T(8,128)(2,1)S(1)}, u32[]{:S(2)}, u32[]{:S(2)}) collective-permute-start(bf16[1,80,2432]{2,1,0:T(8,128)(2,1)S(1)} %get-tuple-element.113), channel_id=1, source_target_pairs={{0,2},{1,3},{2,0},{3,1},{4,6},{5,7},{6,4},{7,5},{8,10},{9,11},{10,... | collective-permute-start | bytes 1167368 | tf_op jit(solution)/shard_map/ppermute | solution.py:336
  77.8 8.7 %collective-permute-start.13 = (bf16[6,80,384]{2,1,0:T(8,128)(2,1)S(1)}, bf16[6,80,384]{2,1,0:T(8,128)(2,1)S(1)}, u32[]{:S(2)}, u32[]{:S(2)}) collective-permute-start(bf16[6,80,384]{2,1,0:T(8,128)(2,1)S(1)} %get-tuple-element.111), channel_id=1, source_target_pairs={{0,1},{1,0},{2,3},{3,2},{4,5},{5,4},{6,7},{7,6},{8,9},{9,8},{10,11... | collective-permute-start | bytes 1105928 | tf_op jit(solution)/shard_map/ppermute | solution.py:336
  78.0 20.1 %collective-permute-start.16 = (bf16[1,80,2432]{2,1,0:T(8,128)(2,1)S(1)}, bf16[1,80,2432]{2,1,0:T(8,128)(2,1)S(1)}, u32[]{:S(2)}, u32[]{:S(2)}) collective-permute-start(bf16[1,80,2432]{2,1,0:T(8,128)(2,1)S(1)} %get-tuple-element.123), channel_id=1, source_target_pairs={{0,2},{1,3},{2,0},{3,1},{4,6},{5,7},{6,4},{7,5},{8,10},{9,11},{10,... | collective-permute-start | bytes 1167368 | tf_op jit(solution)/shard_map/ppermute | solution.py:336
  83.0 28.0 %collective-permute-start.19 = (bf16[2,80,2432]{2,1,0:T(8,128)(2,1)S(1)}, bf16[2,80,2432]{2,1,0:T(8,128)(2,1)S(1)}, u32[]{:S(2)}, u32[]{:S(2)}) collective-permute-start(bf16[2,80,2432]{2,1,0:T(8,128)(2,1)S(1)} %get-tuple-element.135), channel_id=1, source_target_pairs={{0,2},{1,3},{2,0},{3,1},{4,6},{5,7},{6,4},{7,5},{8,10},{9,11},{10,... | collective-permute-start | bytes 2334728 | tf_op jit(solution)/shard_map/ppermute | solution.py:336
  84.3 26.6 %collective-permute-start.20 = (bf16[80,2432]{1,0:T(8,128)(2,1)S(1)}, bf16[80,2432]{1,0:T(8,128)(2,1)S(1)}, u32[]{:S(2)}, u32[]{:S(2)}) collective-permute-start(bf16[80,2432]{1,0:T(8,128)(2,1)S(1)} %get-tuple-element.137), channel_id=1, source_target_pairs={{0,8},{4,12},{8,0},{12,4},{1,9},{5,13},{9,1},{13,5},{2,10},{6,14},... | collective-permute-start | bytes 1167368 | tf_op jit(solution)/shard_map/ppermute | solution.py:341
  87.2 26.8 %collective-permute-start.17 = (bf16[1280,384]{1,0:T(8,128)(2,1)S(1)}, bf16[1280,384]{1,0:T(8,128)(2,1)S(1)}, u32[]{:S(2)}, u32[]{:S(2)}) collective-permute-start(bf16[1280,384]{1,0:T(8,128)(2,1)S(1)} %bitcast.71), channel_id=1, source_target_pairs={{0,16},{16,0},{1,17},{17,1},{2,18},{18,2},{3,19},{19,3},{4,20},{20... | collective-permute-start | bytes 2949128 | tf_op jit(solution)/shard_map/ppermute | solution.py:336
  98.2 15.8 %collective-permute-start.21 = (bf16[80,2432]{1,0:T(8,128)(2,1)S(1)}, bf16[80,2432]{1,0:T(8,128)(2,1)S(1)}, u32[]{:S(2)}, u32[]{:S(2)}) collective-permute-start(bf16[80,2432]{1,0:T(8,128)(2,1)S(1)} %get-tuple-element.139), channel_id=1, source_target_pairs={{0,4},{4,8},{8,12},{12,0},{1,5},{5,9},{9,13},{13,1},{2,6},{6,10},{... | collective-permute-start | bytes 1167368 | tf_op jit(solution)/shard_map/ppermute | solution.py:341
  109.1 4.9 %collective-permute-start.18 = (f32[10,3,768]{2,1,0:T(4,128)S(1)}, f32[10,3,768]{2,1,0:T(4,128)S(1)}, u32[]{:S(2)}, u32[]{:S(2)}) collective-permute-start(f32[10,3,768]{2,1,0:T(4,128)S(1)} %get-tuple-element.132), channel_id=1, source_target_pairs={{0,16},{16,0},{1,17},{17,1},{2,18},{18,2},{3,19},{19,3},{4,20},{20... | collective-permute-start | bytes 276488 | tf_op jit(solution)/shard_map/ppermute | solution.py:336
  111.1 8.2 %collective-permute-start.22 = (bf16[80,2432]{1,0:T(8,128)(2,1)S(1)}, bf16[80,2432]{1,0:T(8,128)(2,1)S(1)}, u32[]{:S(2)}, u32[]{:S(2)}) collective-permute-start(bf16[80,2432]{1,0:T(8,128)(2,1)S(1)} %get-tuple-element.143), channel_id=1, source_target_pairs={{0,12},{4,0},{8,4},{12,8},{1,13},{5,1},{9,5},{13,9},{2,14},{6,2},{... | collective-permute-start | bytes 1167368 | tf_op jit(solution)/shard_map/ppermute | solution.py:341
  119.8 8.2 %collective-permute-start.23 = (bf16[80,1216]{1,0:T(8,128)(2,1)S(1)}, bf16[80,1216]{1,0:T(8,128)(2,1)S(1)}, u32[]{:S(2)}, u32[]{:S(2)}) collective-permute-start(bf16[80,1216]{1,0:T(8,128)(2,1)S(1)} %get-tuple-element.149), channel_id=1, source_target_pairs={{0,16},{16,0},{1,17},{17,1},{2,18},{18,2},{3,19},{19,3},{4,20},{20... | collective-permute-start | bytes 583688 | tf_op jit(solution)/shard_map/ppermute | solution.py:336
  (21 other events, 78.9 us)

commit v5 on v4

--- a/solution.py
+++ b/solution.py
@@ -17,7 +17,7 @@
 TOKEN = (8, 128)
 BIG = 36
 FLOPS_PER_US = 1150e6 * 0.5
-CHUNKS = (3, 4, 3)
+CHUNKS = (3, 5, 2)
 PARTS = (6, 3, 1)
 
 
@@ -262,7 +262,7 @@
 def outer(slots, a_own, a_other, own, other, groups, after):
     _, rows, n = a_own.shape
     depth = own.shape[1]
-    count, tile = sum(groups), 5 * PAIR
+    count, tile = sum(groups), depth
 
     def kernel(slot_ref, *refs):
         mine, theirs, (own_ref, other_ref), outs = refs[:count], refs[count : 2 * count], refs[2 * count : 2 * count + 2], refs[2 * count + 2 :]

time: 129 us -> 127 us (0.984)
  Pallas kernels: 66.7 us -> 64.9 us
  waiting for transfers between devices: 19.6 us -> 18.1 us
    ppermute x6, waiting for transfers between devices: 5.52 us -> 0.63 us  [shift(): return lax.ppermute(x, axis, [(i, (i + step) % size) for i in range(size)])]
    ppermute x18, waiting for transfers between devices: 14.1 us -> 17.5 us  [swap(): return lax.ppermute(x, axis, [(i, i ^ bit) for i in range(size)])]
    pallas_call x24, Pallas kernels: 66.7 us -> 64.9 us  [run(): pl.pallas_call(wrapped, grid_spec=pltpu.PrefetchScalarGridSpec(num_scalar...]
  transfers between devices with their start and end apart: 24 -> 24, of which waited for: 9 -> 10; matrix products, arithmetic and copies ran while one was open for 0% -> 0% of each run, Pallas kernels for 47% -> 47%
where the time goes in v5:
time: 127 us
  Pallas kernels  64.9 us (51%)
  starting transfers between devices  32.4 us (26%)
  waiting for transfers between devices  18.1 us (14%)
  local copies, waits for them, and re-layouts  10.3 us (8%)
    pallas_call x24, Pallas kernels, run(): pl.pallas_call(wrapped, grid_spec=pltpu.PrefetchScalarGridSpec(num_scalar...  64.9 us
    ppermute x18, starting transfers between devices, swap(): return lax.ppermute(x, axis, [(i, i ^ bit) for i in range(size)])  19.3 us
    ppermute x18, waiting for transfers between devices, swap(): return lax.ppermute(x, axis, [(i, i ^ bit) for i in range(size)])  17.5 us
    ppermute x6, starting transfers between devices, shift(): return lax.ppermute(x, axis, [(i, (i + step) % size) for i in range(size)])  13.2 us
    unnamed x42, local copies, waits for them, and re-layouts  10 us
  transfers between devices with their start and end apart: 24, of which 10 were waited for; matrix products, arithmetic and copies ran while one was open for 0% of the time, Pallas kernels for 47%

profile of v5, /device:TPU:0, one launch (start us, length us, event | category | flops | bytes accessed | tf_op | source)
XLA Modules:
  0.0 126.6 jit_solution(821087979958567220)
XLA Ops:
  0.6 3.0 %collective-permute-start = (bf16[80,1216]{1,0:T(8,128)(2,1)}, bf16[80,1216]{1,0:T(8,128)(2,1)S(1)}, u32[]{:S(2)}, u32[]{:S(2)}) collective-permute-start(bf16[80,1216]{1,0:T(8,128)(2,1)} %refs_1_.1), channel_id=1, source_target_pairs={{0,16},{16,0},{1,17},{17,1},{2,18},{18,2},{3,19},{19,3},{4,20},{20... | collective-permute-start | bytes 583688 | tf_op jit(solution)/shard_map/ppermute | solution.py:336
  9.1 1.8 %collective-permute-start.4 = (bf16[80,2432]{1,0:T(8,128)(2,1)S(1)}, bf16[80,2432]{1,0:T(8,128)(2,1)S(1)}, u32[]{:S(2)}, u32[]{:S(2)}) collective-permute-start(bf16[80,2432]{1,0:T(8,128)(2,1)S(1)} %get-tuple-element.79.refs_0_), channel_id=1, source_target_pairs={{0,2},{1,3},{2,0},{3,1},{4,6},{5,7},{6,4},{7,5},{8,10},{9,11},{10,... | collective-permute-start | bytes 1167368 | tf_op jit(solution)/shard_map/ppermute | solution.py:336
  10.9 1.6 %collective-permute-start.1 = (bf16[80,2432]{1,0:T(8,128)(2,1)S(1)}, bf16[80,2432]{1,0:T(8,128)(2,1)S(1)}, u32[]{:S(2)}, u32[]{:S(2)}) collective-permute-start(bf16[80,2432]{1,0:T(8,128)(2,1)S(1)} %get-tuple-element.79.refs_0_), channel_id=1, source_target_pairs={{0,4},{4,8},{8,12},{12,0},{1,5},{5,9},{9,13},{13,1},{2,6},{6,10},{... | collective-permute-start | bytes 1167368 | tf_op jit(solution)/shard_map/ppermute | solution.py:341
  12.5 2.2 %collective-permute-start.2 = (bf16[80,2432]{1,0:T(8,128)(2,1)S(1)}, bf16[80,2432]{1,0:T(8,128)(2,1)S(1)}, u32[]{:S(2)}, u32[]{:S(2)}) collective-permute-start(bf16[80,2432]{1,0:T(8,128)(2,1)S(1)} %get-tuple-element.79.refs_0_), channel_id=1, source_target_pairs={{0,12},{4,0},{8,4},{12,8},{1,13},{5,1},{9,5},{13,9},{2,14},{6,2},{... | collective-permute-start | bytes 1167368 | tf_op jit(solution)/shard_map/ppermute | solution.py:341
  15.3 1.5 %collective-permute-start.7 = (bf16[768,640]{1,0:T(8,128)(2,1)S(1)}, bf16[768,640]{1,0:T(8,128)(2,1)S(1)}, u32[]{:S(2)}, u32[]{:S(2)}) collective-permute-start(bf16[768,640]{1,0:T(8,128)(2,1)S(1)} %get-tuple-element.87), channel_id=1, source_target_pairs={{0,16},{16,0},{1,17},{17,1},{2,18},{18,2},{3,19},{19,3},{4,20},{20... | collective-permute-start | bytes 2949128 | tf_op jit(solution)/shard_map/ppermute | solution.py:336
  16.9 2.5 %collective-permute-done.4.refs_1_ = bf16[80,2432]{1,0:T(8,128)(2,1)S(1)} collective-permute-done((bf16[80,2432]{1,0:T(8,128)(2,1)S(1)}, bf16[80,2432]{1,0:T(8,128)(2,1)S(1)}, u32[]{:S(2)}, u32[]{:S(2)}) %collective-permute-start.4) | collective-permute-done | bytes 389152 | tf_op jit(solution)/shard_map/ppermute | solution.py:336
  19.4 3.4 %project.2 = (bf16[2,80,384]{2,1,0:T(8,128)(2,1)S(1)}, bf16[2,80,384]{2,1,0:T(8,128)(2,1)S(1)}, f32[8,128]{1,0:T(8,128)S(1)}) custom-call(bf16[80,2432]{1,0:T(8,128)(2,1)S(1)} %get-tuple-element.79.refs_0_, bf16[80,2432]{1,0:T(8,128)(2,1)S(1)} %collective-permute-done.4.refs_1_, bf16[384,2432]{1,0:T(8,128)(2,1)S(1)} %bitcast.76, ...), custom_call_target="tpu_custom_call" | custom-call | flops 57500000 | tf_op jit(solution)/shard_map/project/pallas_call | solution.py:42
  25.7 4.9 %attend.3 = (bf16[1280,384]{1,0:T(8,128)(2,1)S(1)}, bf16[20,768,768]{2,1,0:T(8,128)(2,1)}, f32[10,2,768]{2,1,0:T(2,128)S(1)}, bf16[768,1280]{1,0:T(8,128)(2,1)S(1)}, f32[8,128]{1,0:T(8,128)S(1)}) custom-call(bf16[384,1280]{1,0:T(8,128)(2,1)S(1)} %bitcast.64, bf16[384,1280]{1,0:T(8,128)(2,1)S(1)} %bitcast.44, bf16[384,1280]{1,0:T(8,128)(2,1)S(1)} %bitcast.55, ...), custom_call_target="tpu_custom_call" | custom-call | flops 690000000 | tf_op jit(solution)/shard_map/attend/pallas_call | solution.py:42
  32.9 2.6 %collective-permute-start.8 = (bf16[80,2432]{1,0:T(8,128)(2,1)S(1)}, bf16[80,2432]{1,0:T(8,128)(2,1)S(1)}, u32[]{:S(2)}, u32[]{:S(2)}) collective-permute-start(bf16[80,2432]{1,0:T(8,128)(2,1)S(1)} %get-tuple-element.79.refs_0_), channel_id=1, source_target_pairs={{0,8},{4,12},{8,0},{12,4},{1,9},{5,13},{9,1},{13,5},{2,10},{6,14},... | collective-permute-start | bytes 1167368 | tf_op jit(solution)/shard_map/ppermute | solution.py:341
  37.0 7.9 %collective-permute-done.7.refs_3_ = bf16[768,640]{1,0:T(8,128)(2,1)S(1)} collective-permute-done((bf16[768,640]{1,0:T(8,128)(2,1)S(1)}, bf16[768,640]{1,0:T(8,128)(2,1)S(1)}, u32[]{:S(2)}, u32[]{:S(2)}) %collective-permute-start.7) | collective-permute-done | bytes 983072 | tf_op jit(solution)/shard_map/ppermute | solution.py:336
  44.9 7.7 %attend.4 = (bf16[1280,384]{1,0:T(8,128)(2,1)S(1)}, bf16[20,768,768]{2,1,0:T(8,128)(2,1)}, f32[10,2,768]{2,1,0:T(2,128)S(1)}, bf16[768,1280]{1,0:T(8,128)(2,1)S(1)}, f32[8,128]{1,0:T(8,128)S(1)}) custom-call(bf16[384,1280]{1,0:T(8,128)(2,1)S(1)} %bitcast.65, ...), custom_call_target="tpu_custom_call", output_to_operand_aliasing={{0}: (4, {}), {1}: (5, {}), {2}: (6, {}), {3}: (7, {})} | custom-call | flops 1150000000 | tf_op jit(solution)/shard_map/attend/pallas_call | solution.py:42
  54.5 3.6 %attend.5 = (bf16[1280,384]{1,0:T(8,128)(2,1)S(1)}, bf16[20,768,768]{2,1,0:T(8,128)(2,1)}, f32[10,2,768]{2,1,0:T(2,128)S(1)}, bf16[768,1280]{1,0:T(8,128)(2,1)S(1)}, f32[8,128]{1,0:T(8,128)S(1)}) custom-call(bf16[384,1280]{1,0:T(8,128)(2,1)S(1)} %bitcast.67, ...), custom_call_target="tpu_custom_call", output_to_operand_aliasing={{0}: (4, {}), {1}: (5, {}), {2}: (6, {}), {3}: (7, {})} | custom-call | flops 460000000 | tf_op jit(solution)/shard_map/attend/pallas_call | solution.py:42
  63.7 5.0 %outer.1 = (bf16[1,80,2432]{2,1,0:T(8,128)(2,1)S(1)}, bf16[1,80,2432]{2,1,0:T(8,128)(2,1)S(1)}, bf16[2,80,2432]{2,1,0:T(8,128)(2,1)S(1)}, bf16[4,80,2432]{2,1,0:T(8,128)(2,1)S(1)}, f32[8,128]{1,0:T(8,128)S(1)}) custom-call(s32[8]{0:T(128)S(1)} %stack.71.refs_0_, bf16[16,80,384]{2,1,0:T(8,128)(2,1)S(1)} %bitcast.34, bf16[16,80,384]{2,1,0:T(8,128)(2,1)S(1)} %bitcast.35, ...), custom_call_target="tpu_custom_call" | custom-call | flops 3449999872 | tf_op jit(solution)/shard_map/outer/pallas_call | solution.py:42
  68.8 1.6 %collective-permute-start.14 = (bf16[1,80,2432]{2,1,0:T(8,128)(2,1)S(1)}, bf16[1,80,2432]{2,1,0:T(8,128)(2,1)S(1)}, u32[]{:S(2)}, u32[]{:S(2)}) collective-permute-start(bf16[1,80,2432]{2,1,0:T(8,128)(2,1)S(1)} %get-tuple-element.113), channel_id=1, source_target_pairs={{0,2},{1,3},{2,0},{3,1},{4,6},{5,7},{6,4},{7,5},{8,10},{9,11},{10,... | collective-permute-start | bytes 1167368 | tf_op jit(solution)/shard_map/ppermute | solution.py:336
  71.3 5.5 %project.3 = (bf16[6,80,384]{2,1,0:T(8,128)(2,1)S(1)}, bf16[6,80,384]{2,1,0:T(8,128)(2,1)S(1)}, f32[8,128]{1,0:T(8,128)S(1)}) custom-call(bf16[80,2432]{1,0:T(8,128)(2,1)S(1)} %collective-permute-done.1.refs_0_, bf16[80,2432]{1,0:T(8,128)(2,1)S(1)} %copy-done.16, bf16[80,2432]{1,0:T(8,128)(2,1)S(1)} %copy-done.18, bf16[160,2432]{1,0:T(8,128)(2,1)S(1)} %copy-done.14, ...), custom_call_target="tpu_custom_call" | custom-call | flops 2357499904 | tf_op jit(solution)/shard_map/project/pallas_call | solution.py:42
  76.9 1.6 %collective-permute-start.16 = (bf16[1,80,2432]{2,1,0:T(8,128)(2,1)S(1)}, bf16[1,80,2432]{2,1,0:T(8,128)(2,1)S(1)}, u32[]{:S(2)}, u32[]{:S(2)}) collective-permute-start(bf16[1,80,2432]{2,1,0:T(8,128)(2,1)S(1)} %get-tuple-element.123), channel_id=1, source_target_pairs={{0,2},{1,3},{2,0},{3,1},{4,6},{5,7},{6,4},{7,5},{8,10},{9,11},{10,... | collective-permute-start | bytes 1167368 | tf_op jit(solution)/shard_map/ppermute | solution.py:336
  81.5 2.7 %collective-permute-start.20 = (bf16[80,2432]{1,0:T(8,128)(2,1)S(1)}, bf16[80,2432]{1,0:T(8,128)(2,1)S(1)}, u32[]{:S(2)}, u32[]{:S(2)}) collective-permute-start(bf16[80,2432]{1,0:T(8,128)(2,1)S(1)} %get-tuple-element.137), channel_id=1, source_target_pairs={{0,8},{4,12},{8,0},{12,4},{1,9},{5,13},{9,1},{13,5},{2,10},{6,14},... | collective-permute-start | bytes 1167368 | tf_op jit(solution)/shard_map/ppermute | solution.py:341
  87.4 9.7 %back.3 = (bf16[384,1280]{1,0:T(8,128)(2,1)}, f32[384,1280]{1,0:T(8,128)S(1)}, f32[384,1280]{1,0:T(8,128)S(1)}, f32[10,3,768]{2,1,0:T(4,128)S(1)}, f32[8,128]{1,0:T(8,128)S(1)}) custom-call(bf16[20,768,768]{2,1,0:T(8,128)(2,1)} %get-tuple-element.101.refs_0_, f32[10,2,768]{2,1,0:T(2,128)S(1)} %get-tuple-element.102.refs_1_, bf16[384,1280]{1,0:T(8,128)(2,1)S(1)} %bitcast.68, ...), custom_call_target="tpu_custom_call" | custom-call | flops 6899999744 | tf_op jit(solution)/shard_map/back/pallas_call | solution.py:42
  97.2 1.8 %collective-permute-start.21 = (bf16[80,2432]{1,0:T(8,128)(2,1)S(1)}, bf16[80,2432]{1,0:T(8,128)(2,1)S(1)}, u32[]{:S(2)}, u32[]{:S(2)}) collective-permute-start(bf16[80,2432]{1,0:T(8,128)(2,1)S(1)} %get-tuple-element.139), channel_id=1, source_target_pairs={{0,4},{4,8},{8,12},{12,0},{1,5},{5,9},{9,13},{13,1},{2,6},{6,10},{... | collective-permute-start | bytes 1167368 | tf_op jit(solution)/shard_map/ppermute | solution.py:341
  99.0 5.7 %back.4 = (bf16[384,1280]{1,0:T(8,128)(2,1)}, f32[384,1280]{1,0:T(8,128)S(1)}, f32[384,1280]{1,0:T(8,128)S(1)}, f32[10,3,768]{2,1,0:T(4,128)S(1)}, f32[8,128]{1,0:T(8,128)S(1)}) custom-call(bf16[20,768,768]{2,1,0:T(8,128)(2,1)} %get-tuple-element.101.refs_0_, ...), custom_call_target="tpu_custom_call", output_to_operand_aliasing={{0}: (7, {}), {1}: (8, {}), {2}: (9, {}), {3}: (10, {})} | custom-call | flops 57500000 | tf_op jit(solution)/shard_map/back/pallas_call | solution.py:42
  104.7 3.1 %back.5 = (bf16[384,1280]{1,0:T(8,128)(2,1)}, f32[384,1280]{1,0:T(8,128)S(1)}, f32[384,1280]{1,0:T(8,128)S(1)}, f32[10,3,768]{2,1,0:T(4,128)S(1)}, f32[8,128]{1,0:T(8,128)S(1)}) custom-call(bf16[20,768,768]{2,1,0:T(8,128)(2,1)} %get-tuple-element.101.refs_0_, ...), custom_call_target="tpu_custom_call", output_to_operand_aliasing={{0}: (7, {}), {1}: (8, {}), {2}: (9, {}), {3}: (10, {})} | custom-call | flops 57500000 | tf_op jit(solution)/shard_map/back/pallas_call | solution.py:42
  109.0 2.3 %collective-permute-start.22 = (bf16[80,2432]{1,0:T(8,128)(2,1)S(1)}, bf16[80,2432]{1,0:T(8,128)(2,1)S(1)}, u32[]{:S(2)}, u32[]{:S(2)}) collective-permute-start(bf16[80,2432]{1,0:T(8,128)(2,1)S(1)} %get-tuple-element.143), channel_id=1, source_target_pairs={{0,12},{4,0},{8,4},{12,8},{1,13},{5,1},{9,5},{13,9},{2,14},{6,2},{... | collective-permute-start | bytes 1167368 | tf_op jit(solution)/shard_map/ppermute | solution.py:341
  112.7 5.3 %cross.2 = (bf16[384,1280]{1,0:T(8,128)(2,1)}, bf16[384,1280]{1,0:T(8,128)(2,1)}, f32[8,128]{1,0:T(8,128)S(1)}) custom-call(bf16[384,1280]{1,0:T(8,128)(2,1)S(1)} %collective-permute-done.15.refs_7_.refs_0_, bf16[384,1280]{1,0:T(8,128)(2,1)S(1)} %bitcast.51, bf16[384,1280]{1,0:T(8,128)(2,1)S(1)} %bitcast.62, ...), custom_call_target="tpu_custom_call" | custom-call | flops 4312500224 | tf_op jit(solution)/shard_map/cross/pallas_call | solution.py:42
  120.5 5.3 %cross.3 = (bf16[384,1280]{1,0:T(8,128)(2,1)}, bf16[384,1280]{1,0:T(8,128)(2,1)}, f32[8,128]{1,0:T(8,128)S(1)}) custom-call(bf16[384,1280]{1,0:T(8,128)(2,1)S(1)} %collective-permute-done.15.refs_7_.refs_0_, bf16[384,1280]{1,0:T(8,128)(2,1)S(1)} %bitcast.52, bf16[384,1280]{1,0:T(8,128)(2,1)S(1)} %bitcast.63, ...), custom_call_target="tpu_custom_call", output_to_operand_aliasing={{0}: (7, {}), {1}: (8, {})} | custom-call | flops 4312500224 | tf_op jit(solution)/shard_map/cross/pallas_call | solution.py:42
  (94 shorter events, 33.3 us)
Async XLA Ops:
  0.6 8.3 %collective-permute-start = (bf16[80,1216]{1,0:T(8,128)(2,1)}, bf16[80,1216]{1,0:T(8,128)(2,1)S(1)}, u32[]{:S(2)}, u32[]{:S(2)}) collective-permute-start(bf16[80,1216]{1,0:T(8,128)(2,1)} %refs_1_.1), channel_id=1, source_target_pairs={{0,16},{16,0},{1,17},{17,1},{2,18},{18,2},{3,19},{19,3},{4,20},{20... | collective-permute-start | bytes 583688 | tf_op jit(solution)/shard_map/ppermute | solution.py:336
  3.6 11.1 %collective-permute-start.5 = (bf16[384,2432]{1,0:T(8,128)(2,1)}, bf16[384,2432]{1,0:T(8,128)(2,1)}, u32[]{:S(2)}, u32[]{:S(2)}) collective-permute-start(bf16[384,2432]{1,0:T(8,128)(2,1)} %bitcast.75), channel_id=1, source_target_pairs={{0,1},{1,0},{2,3},{3,2},{4,5},{5,4},{6,7},{7,6},{8,9},{9,8},{10,11... | collective-permute-start | bytes 5603336 | tf_op jit(solution)/shard_map/ppermute | solution.py:336
  7.5 16.3 %collective-permute-start.3 = (bf16[768,384]{1,0:T(8,128)(2,1)}, bf16[768,384]{1,0:T(8,128)(2,1)S(1)}, u32[]{:S(2)}, u32[]{:S(2)}) collective-permute-start(bf16[768,384]{1,0:T(8,128)(2,1)} %get-tuple-element.80), channel_id=1, source_target_pairs={{0,16},{16,0},{1,17},{17,1},{2,18},{18,2},{3,19},{19,3},{4,20},{20... | collective-permute-start | bytes 1769480 | tf_op jit(solution)/shard_map/ppermute | solution.py:336
  9.1 10.3 %collective-permute-start.4 = (bf16[80,2432]{1,0:T(8,128)(2,1)S(1)}, bf16[80,2432]{1,0:T(8,128)(2,1)S(1)}, u32[]{:S(2)}, u32[]{:S(2)}) collective-permute-start(bf16[80,2432]{1,0:T(8,128)(2,1)S(1)} %get-tuple-element.79.refs_0_), channel_id=1, source_target_pairs={{0,2},{1,3},{2,0},{3,1},{4,6},{5,7},{6,4},{7,5},{8,10},{9,11},{10,... | collective-permute-start | bytes 1167368 | tf_op jit(solution)/shard_map/ppermute | solution.py:336
  10.9 19.8 %collective-permute-start.1 = (bf16[80,2432]{1,0:T(8,128)(2,1)S(1)}, bf16[80,2432]{1,0:T(8,128)(2,1)S(1)}, u32[]{:S(2)}, u32[]{:S(2)}) collective-permute-start(bf16[80,2432]{1,0:T(8,128)(2,1)S(1)} %get-tuple-element.79.refs_0_), channel_id=1, source_target_pairs={{0,4},{4,8},{8,12},{12,0},{1,5},{5,9},{9,13},{13,1},{2,6},{6,10},{... | collective-permute-start | bytes 1167368 | tf_op jit(solution)/shard_map/ppermute | solution.py:341
  12.5 18.2 %collective-permute-start.2 = (bf16[80,2432]{1,0:T(8,128)(2,1)S(1)}, bf16[80,2432]{1,0:T(8,128)(2,1)S(1)}, u32[]{:S(2)}, u32[]{:S(2)}) collective-permute-start(bf16[80,2432]{1,0:T(8,128)(2,1)S(1)} %get-tuple-element.79.refs_0_), channel_id=1, source_target_pairs={{0,12},{4,0},{8,4},{12,8},{1,13},{5,1},{9,5},{13,9},{2,14},{6,2},{... | collective-permute-start | bytes 1167368 | tf_op jit(solution)/shard_map/ppermute | solution.py:341
  15.3 29.6 %collective-permute-start.7 = (bf16[768,640]{1,0:T(8,128)(2,1)S(1)}, bf16[768,640]{1,0:T(8,128)(2,1)S(1)}, u32[]{:S(2)}, u32[]{:S(2)}) collective-permute-start(bf16[768,640]{1,0:T(8,128)(2,1)S(1)} %get-tuple-element.87), channel_id=1, source_target_pairs={{0,16},{16,0},{1,17},{17,1},{2,18},{18,2},{3,19},{19,3},{4,20},{20... | collective-permute-start | bytes 2949128 | tf_op jit(solution)/shard_map/ppermute | solution.py:336
  31.4 22.2 %collective-permute-start.9 = (bf16[160,2432]{1,0:T(8,128)(2,1)S(1)}, bf16[160,2432]{1,0:T(8,128)(2,1)S(1)}, u32[]{:S(2)}, u32[]{:S(2)}) collective-permute-start(bf16[160,2432]{1,0:T(8,128)(2,1)S(1)} %get-tuple-element.99), channel_id=1, source_target_pairs={{0,2},{1,3},{2,0},{3,1},{4,6},{5,7},{6,4},{7,5},{8,10},{9,11},{10,... | collective-permute-start | bytes 2334728 | tf_op jit(solution)/shard_map/ppermute | solution.py:336
  32.9 20.7 %collective-permute-start.8 = (bf16[80,2432]{1,0:T(8,128)(2,1)S(1)}, bf16[80,2432]{1,0:T(8,128)(2,1)S(1)}, u32[]{:S(2)}, u32[]{:S(2)}) collective-permute-start(bf16[80,2432]{1,0:T(8,128)(2,1)S(1)} %get-tuple-element.79.refs_0_), channel_id=1, source_target_pairs={{0,8},{4,12},{8,0},{12,4},{1,9},{5,13},{9,1},{13,5},{2,10},{6,14},... | collective-permute-start | bytes 1167368 | tf_op jit(solution)/shard_map/ppermute | solution.py:341
  35.8 18.7 %collective-permute-start.6 = (bf16[768,256]{1,0:T(8,128)(2,1)S(1)}, bf16[768,256]{1,0:T(8,128)(2,1)S(1)}, u32[]{:S(2)}, u32[]{:S(2)}) collective-permute-start(bf16[768,256]{1,0:T(8,128)(2,1)S(1)} %get-tuple-element.86), channel_id=1, source_target_pairs={{0,16},{16,0},{1,17},{17,1},{2,18},{18,2},{3,19},{19,3},{4,20},{20... | collective-permute-start | bytes 1179656 | tf_op jit(solution)/shard_map/ppermute | solution.py:336
  59.5 2.7 %collective-permute-start.11 = (bf16[16,80,384]{2,1,0:T(8,128)(2,1)S(1)}, bf16[16,80,384]{2,1,0:T(8,128)(2,1)}, u32[]{:S(2)}, u32[]{:S(2)}) collective-permute-start(bf16[16,80,384]{2,1,0:T(8,128)(2,1)S(1)} %bitcast.33), channel_id=1, source_target_pairs={{0,1},{1,0},{2,3},{3,2},{4,5},{5,4},{6,7},{7,6},{8,9},{9,8},{10,11... | collective-permute-start | bytes 2949128 | tf_op jit(solution)/shard_map/ppermute | solution.py:336
  59.5 11.8 %collective-permute-start.10 = (bf16[80,2432]{1,0:T(8,128)(2,1)}, bf16[80,2432]{1,0:T(8,128)(2,1)}, u32[]{:S(2)}, u32[]{:S(2)}) collective-permute-start(bf16[80,2432]{1,0:T(8,128)(2,1)} %get-tuple-element.105), channel_id=1, source_target_pairs={{0,2},{1,3},{2,0},{3,1},{4,6},{5,7},{6,4},{7,5},{8,10},{9,11},{10,... | collective-permute-start | bytes 1167368 | tf_op jit(solution)/shard_map/ppermute | solution.py:336
  61.2 20.3 %collective-permute-start.12 = (bf16[2,80,384]{2,1,0:T(8,128)(2,1)}, bf16[2,80,384]{2,1,0:T(8,128)(2,1)S(1)}, u32[]{:S(2)}, u32[]{:S(2)}) collective-permute-start(bf16[2,80,384]{2,1,0:T(8,128)(2,1)} %copy-done.20), channel_id=1, source_target_pairs={{0,1},{1,0},{2,3},{3,2},{4,5},{5,4},{6,7},{7,6},{8,9},{9,8},{10,11... | collective-permute-start | bytes 368648 | tf_op jit(solution)/shard_map/ppermute | solution.py:336
  61.4 24.2 %collective-permute-start.15 = (bf16[384,1280]{1,0:T(8,128)(2,1)}, bf16[384,1280]{1,0:T(8,128)(2,1)S(1)}, u32[]{:S(2)}, u32[]{:S(2)}) collective-permute-start(bf16[384,1280]{1,0:T(8,128)(2,1)} %copy-done.12), channel_id=1, source_target_pairs={{0,16},{16,0},{1,17},{17,1},{2,18},{18,2},{3,19},{19,3},{4,20},{20... | collective-permute-start | bytes 2949128 | tf_op jit(solution)/shard_map/ppermute | solution.py:336
  68.8 11.1 %collective-permute-start.14 = (bf16[1,80,2432]{2,1,0:T(8,128)(2,1)S(1)}, bf16[1,80,2432]{2,1,0:T(8,128)(2,1)S(1)}, u32[]{:S(2)}, u32[]{:S(2)}) collective-permute-start(bf16[1,80,2432]{2,1,0:T(8,128)(2,1)S(1)} %get-tuple-element.113), channel_id=1, source_target_pairs={{0,2},{1,3},{2,0},{3,1},{4,6},{5,7},{6,4},{7,5},{8,10},{9,11},{10,... | collective-permute-start | bytes 1167368 | tf_op jit(solution)/shard_map/ppermute | solution.py:336
  76.7 8.8 %collective-permute-start.13 = (bf16[6,80,384]{2,1,0:T(8,128)(2,1)S(1)}, bf16[6,80,384]{2,1,0:T(8,128)(2,1)S(1)}, u32[]{:S(2)}, u32[]{:S(2)}) collective-permute-start(bf16[6,80,384]{2,1,0:T(8,128)(2,1)S(1)} %get-tuple-element.111), channel_id=1, source_target_pairs={{0,1},{1,0},{2,3},{3,2},{4,5},{5,4},{6,7},{7,6},{8,9},{9,8},{10,11... | collective-permute-start | bytes 1105928 | tf_op jit(solution)/shard_map/ppermute | solution.py:336
  76.9 20.2 %collective-permute-start.16 = (bf16[1,80,2432]{2,1,0:T(8,128)(2,1)S(1)}, bf16[1,80,2432]{2,1,0:T(8,128)(2,1)S(1)}, u32[]{:S(2)}, u32[]{:S(2)}) collective-permute-start(bf16[1,80,2432]{2,1,0:T(8,128)(2,1)S(1)} %get-tuple-element.123), channel_id=1, source_target_pairs={{0,2},{1,3},{2,0},{3,1},{4,6},{5,7},{6,4},{7,5},{8,10},{9,11},{10,... | collective-permute-start | bytes 1167368 | tf_op jit(solution)/shard_map/ppermute | solution.py:336
  79.9 28.9 %collective-permute-start.19 = (bf16[2,80,2432]{2,1,0:T(8,128)(2,1)S(1)}, bf16[2,80,2432]{2,1,0:T(8,128)(2,1)S(1)}, u32[]{:S(2)}, u32[]{:S(2)}) collective-permute-start(bf16[2,80,2432]{2,1,0:T(8,128)(2,1)S(1)} %get-tuple-element.135), channel_id=1, source_target_pairs={{0,2},{1,3},{2,0},{3,1},{4,6},{5,7},{6,4},{7,5},{8,10},{9,11},{10,... | collective-permute-start | bytes 2334728 | tf_op jit(solution)/shard_map/ppermute | solution.py:336
  81.5 27.3 %collective-permute-start.20 = (bf16[80,2432]{1,0:T(8,128)(2,1)S(1)}, bf16[80,2432]{1,0:T(8,128)(2,1)S(1)}, u32[]{:S(2)}, u32[]{:S(2)}) collective-permute-start(bf16[80,2432]{1,0:T(8,128)(2,1)S(1)} %get-tuple-element.137), channel_id=1, source_target_pairs={{0,8},{4,12},{8,0},{12,4},{1,9},{5,13},{9,1},{13,5},{2,10},{6,14},... | collective-permute-start | bytes 1167368 | tf_op jit(solution)/shard_map/ppermute | solution.py:341
  86.2 26.5 %collective-permute-start.17 = (bf16[1280,384]{1,0:T(8,128)(2,1)S(1)}, bf16[1280,384]{1,0:T(8,128)(2,1)S(1)}, u32[]{:S(2)}, u32[]{:S(2)}) collective-permute-start(bf16[1280,384]{1,0:T(8,128)(2,1)S(1)} %bitcast.71), channel_id=1, source_target_pairs={{0,16},{16,0},{1,17},{17,1},{2,18},{18,2},{3,19},{19,3},{4,20},{20... | collective-permute-start | bytes 2949128 | tf_op jit(solution)/shard_map/ppermute | solution.py:336
  97.2 15.5 %collective-permute-start.21 = (bf16[80,2432]{1,0:T(8,128)(2,1)S(1)}, bf16[80,2432]{1,0:T(8,128)(2,1)S(1)}, u32[]{:S(2)}, u32[]{:S(2)}) collective-permute-start(bf16[80,2432]{1,0:T(8,128)(2,1)S(1)} %get-tuple-element.139), channel_id=1, source_target_pairs={{0,4},{4,8},{8,12},{12,0},{1,5},{5,9},{9,13},{13,1},{2,6},{6,10},{... | collective-permute-start | bytes 1167368 | tf_op jit(solution)/shard_map/ppermute | solution.py:341
  107.8 4.9 %collective-permute-start.18 = (f32[10,3,768]{2,1,0:T(4,128)S(1)}, f32[10,3,768]{2,1,0:T(4,128)S(1)}, u32[]{:S(2)}, u32[]{:S(2)}) collective-permute-start(f32[10,3,768]{2,1,0:T(4,128)S(1)} %get-tuple-element.132), channel_id=1, source_target_pairs={{0,16},{16,0},{1,17},{17,1},{2,18},{18,2},{3,19},{19,3},{4,20},{20... | collective-permute-start | bytes 276488 | tf_op jit(solution)/shard_map/ppermute | solution.py:336
  109.0 9.6 %collective-permute-start.22 = (bf16[80,2432]{1,0:T(8,128)(2,1)S(1)}, bf16[80,2432]{1,0:T(8,128)(2,1)S(1)}, u32[]{:S(2)}, u32[]{:S(2)}) collective-permute-start(bf16[80,2432]{1,0:T(8,128)(2,1)S(1)} %get-tuple-element.143), channel_id=1, source_target_pairs={{0,12},{4,0},{8,4},{12,8},{1,13},{5,1},{9,5},{13,9},{2,14},{6,2},{... | collective-permute-start | bytes 1167368 | tf_op jit(solution)/shard_map/ppermute | solution.py:341
  119.1 6.7 %collective-permute-start.23 = (bf16[80,1216]{1,0:T(8,128)(2,1)S(1)}, bf16[80,1216]{1,0:T(8,128)(2,1)S(1)}, u32[]{:S(2)}, u32[]{:S(2)}) collective-permute-start(bf16[80,1216]{1,0:T(8,128)(2,1)S(1)} %get-tuple-element.149), channel_id=1, source_target_pairs={{0,16},{16,0},{1,17},{17,1},{2,18},{18,2},{3,19},{19,3},{4,20},{20... | collective-permute-start | bytes 583688 | tf_op jit(solution)/shard_map/ppermute | solution.py:336
  (21 other events, 74.6 us)

commit v6 on v5

--- a/solution.py
+++ b/solution.py
@@ -224,10 +224,11 @@
 
     def kernel(*refs):
         left = jnp.concatenate([r[...] for r in refs[:parts]], 0)
-        for ref, out in zip(refs[parts : parts + 2], refs[parts + 2 :]):
-            res = nt(left, ref[...]).astype(BF16)
+        both = jnp.concatenate([r[...] for r in refs[parts : parts + 2]], 0)
+        res = nt(left, both).astype(BF16)
+        for i, out in enumerate(refs[parts + 2 :]):
             for j in range(count):
-                out[j] = res[j * rows : (j + 1) * rows]
+                out[j] = res[j * rows : (j + 1) * rows, i * PAIR : (i + 1) * PAIR]
 
     tokens = pl.BlockSpec((PAIR, depth), lambda i: (i, 0))
     return run(

time: 127 us -> 127 us (level)
  Pallas kernels: 64.9 us -> 63.4 us
  waiting for transfers between devices: 18.1 us -> 19.6 us
    ppermute x18, waiting for transfers between devices: 17.5 us -> 18.9 us  [swap(): return lax.ppermute(x, axis, [(i, i ^ bit) for i in range(size)])]
    pallas_call x24, Pallas kernels: 64.9 us -> 63.4 us  [run(): pl.pallas_call(wrapped, grid_spec=pltpu.PrefetchScalarGridSpec(num_scalar...]
  transfers between devices with their start and end apart: 24 -> 24, of which waited for: 10 -> 10; matrix products, arithmetic and copies ran while one was open for 0% -> 0% of each run, Pallas kernels for 47% -> 46%
where the time goes in v6:
time: 127 us
  Pallas kernels  63.4 us (50%)
  starting transfers between devices  32.4 us (26%)
  waiting for transfers between devices  19.6 us (15%)
  local copies, waits for them, and re-layouts  10.3 us (8%)
    pallas_call x24, Pallas kernels, run(): pl.pallas_call(wrapped, grid_spec=pltpu.PrefetchScalarGridSpec(num_scalar...  63.4 us
    ppermute x18, starting transfers between devices, swap(): return lax.ppermute(x, axis, [(i, i ^ bit) for i in range(size)])  19.3 us
    ppermute x18, waiting for transfers between devices, swap(): return lax.ppermute(x, axis, [(i, i ^ bit) for i in range(size)])  18.9 us
    ppermute x6, starting transfers between devices, shift(): return lax.ppermute(x, axis, [(i, (i + step) % size) for i in range(size)])  13.2 us
    unnamed x42, local copies, waits for them, and re-layouts  10 us
  transfers between devices with their start and end apart: 24, of which 10 were waited for; matrix products, arithmetic and copies ran while one was open for 0% of the time, Pallas kernels for 46%

profile of v6, /device:TPU:0, one launch (start us, length us, event | category | flops | bytes accessed | tf_op | source)
XLA Modules:
  0.0 126.6 jit_solution(15761377869131879748)
XLA Ops:
  0.6 3.0 %collective-permute-start = (bf16[80,1216]{1,0:T(8,128)(2,1)}, bf16[80,1216]{1,0:T(8,128)(2,1)S(1)}, u32[]{:S(2)}, u32[]{:S(2)}) collective-permute-start(bf16[80,1216]{1,0:T(8,128)(2,1)} %refs_1_.1), channel_id=1, source_target_pairs={{0,16},{16,0},{1,17},{17,1},{2,18},{18,2},{3,19},{19,3},{4,20},{20... | collective-permute-start | bytes 583688 | tf_op jit(solution)/shard_map/ppermute | solution.py:337
  9.1 1.8 %collective-permute-start.4 = (bf16[80,2432]{1,0:T(8,128)(2,1)S(1)}, bf16[80,2432]{1,0:T(8,128)(2,1)S(1)}, u32[]{:S(2)}, u32[]{:S(2)}) collective-permute-start(bf16[80,2432]{1,0:T(8,128)(2,1)S(1)} %get-tuple-element.79.refs_0_), channel_id=1, source_target_pairs={{0,2},{1,3},{2,0},{3,1},{4,6},{5,7},{6,4},{7,5},{8,10},{9,11},{10,... | collective-permute-start | bytes 1167368 | tf_op jit(solution)/shard_map/ppermute | solution.py:337
  10.9 1.6 %collective-permute-start.1 = (bf16[80,2432]{1,0:T(8,128)(2,1)S(1)}, bf16[80,2432]{1,0:T(8,128)(2,1)S(1)}, u32[]{:S(2)}, u32[]{:S(2)}) collective-permute-start(bf16[80,2432]{1,0:T(8,128)(2,1)S(1)} %get-tuple-element.79.refs_0_), channel_id=1, source_target_pairs={{0,4},{4,8},{8,12},{12,0},{1,5},{5,9},{9,13},{13,1},{2,6},{6,10},{... | collective-permute-start | bytes 1167368 | tf_op jit(solution)/shard_map/ppermute | solution.py:342
  12.5 2.2 %collective-permute-start.2 = (bf16[80,2432]{1,0:T(8,128)(2,1)S(1)}, bf16[80,2432]{1,0:T(8,128)(2,1)S(1)}, u32[]{:S(2)}, u32[]{:S(2)}) collective-permute-start(bf16[80,2432]{1,0:T(8,128)(2,1)S(1)} %get-tuple-element.79.refs_0_), channel_id=1, source_target_pairs={{0,12},{4,0},{8,4},{12,8},{1,13},{5,1},{9,5},{13,9},{2,14},{6,2},{... | collective-permute-start | bytes 1167368 | tf_op jit(solution)/shard_map/ppermute | solution.py:342
  16.9 2.5 %collective-permute-done.4.refs_1_ = bf16[80,2432]{1,0:T(8,128)(2,1)S(1)} collective-permute-done((bf16[80,2432]{1,0:T(8,128)(2,1)S(1)}, bf16[80,2432]{1,0:T(8,128)(2,1)S(1)}, u32[]{:S(2)}, u32[]{:S(2)}) %collective-permute-start.4) | collective-permute-done | bytes 389152 | tf_op jit(solution)/shard_map/ppermute | solution.py:337
  19.4 3.4 %project.2 = (bf16[2,80,384]{2,1,0:T(8,128)(2,1)S(1)}, bf16[2,80,384]{2,1,0:T(8,128)(2,1)S(1)}, f32[8,128]{1,0:T(8,128)S(1)}) custom-call(bf16[80,2432]{1,0:T(8,128)(2,1)S(1)} %get-tuple-element.79.refs_0_, bf16[80,2432]{1,0:T(8,128)(2,1)S(1)} %collective-permute-done.4.refs_1_, bf16[384,2432]{1,0:T(8,128)(2,1)S(1)} %bitcast.76, ...), custom_call_target="tpu_custom_call" | custom-call | flops 57500000 | tf_op jit(solution)/shard_map/project/pallas_call | solution.py:42
  25.7 4.9 %attend.3 = (bf16[1280,384]{1,0:T(8,128)(2,1)S(1)}, bf16[20,768,768]{2,1,0:T(8,128)(2,1)}, f32[10,2,768]{2,1,0:T(2,128)S(1)}, bf16[768,1280]{1,0:T(8,128)(2,1)S(1)}, f32[8,128]{1,0:T(8,128)S(1)}) custom-call(bf16[384,1280]{1,0:T(8,128)(2,1)S(1)} %bitcast.64, bf16[384,1280]{1,0:T(8,128)(2,1)S(1)} %bitcast.44, bf16[384,1280]{1,0:T(8,128)(2,1)S(1)} %bitcast.55, ...), custom_call_target="tpu_custom_call" | custom-call | flops 690000000 | tf_op jit(solution)/shard_map/attend/pallas_call | solution.py:42
  32.9 2.6 %collective-permute-start.8 = (bf16[80,2432]{1,0:T(8,128)(2,1)S(1)}, bf16[80,2432]{1,0:T(8,128)(2,1)S(1)}, u32[]{:S(2)}, u32[]{:S(2)}) collective-permute-start(bf16[80,2432]{1,0:T(8,128)(2,1)S(1)} %get-tuple-element.79.refs_0_), channel_id=1, source_target_pairs={{0,8},{4,12},{8,0},{12,4},{1,9},{5,13},{9,1},{13,5},{2,10},{6,14},... | collective-permute-start | bytes 1167368 | tf_op jit(solution)/shard_map/ppermute | solution.py:342
  37.0 7.9 %collective-permute-done.7.refs_3_ = bf16[768,640]{1,0:T(8,128)(2,1)S(1)} collective-permute-done((bf16[768,640]{1,0:T(8,128)(2,1)S(1)}, bf16[768,640]{1,0:T(8,128)(2,1)S(1)}, u32[]{:S(2)}, u32[]{:S(2)}) %collective-permute-start.7) | collective-permute-done | bytes 983072 | tf_op jit(solution)/shard_map/ppermute | solution.py:337
  44.9 7.7 %attend.4 = (bf16[1280,384]{1,0:T(8,128)(2,1)S(1)}, bf16[20,768,768]{2,1,0:T(8,128)(2,1)}, f32[10,2,768]{2,1,0:T(2,128)S(1)}, bf16[768,1280]{1,0:T(8,128)(2,1)S(1)}, f32[8,128]{1,0:T(8,128)S(1)}) custom-call(bf16[384,1280]{1,0:T(8,128)(2,1)S(1)} %bitcast.65, ...), custom_call_target="tpu_custom_call", output_to_operand_aliasing={{0}: (4, {}), {1}: (5, {}), {2}: (6, {}), {3}: (7, {})} | custom-call | flops 1150000000 | tf_op jit(solution)/shard_map/attend/pallas_call | solution.py:42
  54.5 3.6 %attend.5 = (bf16[1280,384]{1,0:T(8,128)(2,1)S(1)}, bf16[20,768,768]{2,1,0:T(8,128)(2,1)}, f32[10,2,768]{2,1,0:T(2,128)S(1)}, bf16[768,1280]{1,0:T(8,128)(2,1)S(1)}, f32[8,128]{1,0:T(8,128)S(1)}) custom-call(bf16[384,1280]{1,0:T(8,128)(2,1)S(1)} %bitcast.67, ...), custom_call_target="tpu_custom_call", output_to_operand_aliasing={{0}: (4, {}), {1}: (5, {}), {2}: (6, {}), {3}: (7, {})} | custom-call | flops 460000000 | tf_op jit(solution)/shard_map/attend/pallas_call | solution.py:42
  63.7 5.0 %outer.1 = (bf16[1,80,2432]{2,1,0:T(8,128)(2,1)S(1)}, bf16[1,80,2432]{2,1,0:T(8,128)(2,1)S(1)}, bf16[2,80,2432]{2,1,0:T(8,128)(2,1)S(1)}, bf16[4,80,2432]{2,1,0:T(8,128)(2,1)S(1)}, f32[8,128]{1,0:T(8,128)S(1)}) custom-call(s32[8]{0:T(128)S(1)} %stack.71.refs_0_, bf16[16,80,384]{2,1,0:T(8,128)(2,1)S(1)} %bitcast.34, bf16[16,80,384]{2,1,0:T(8,128)(2,1)S(1)} %bitcast.35, ...), custom_call_target="tpu_custom_call" | custom-call | flops 3449999872 | tf_op jit(solution)/shard_map/outer/pallas_call | solution.py:42
  68.8 1.6 %collective-permute-start.14 = (bf16[1,80,2432]{2,1,0:T(8,128)(2,1)S(1)}, bf16[1,80,2432]{2,1,0:T(8,128)(2,1)S(1)}, u32[]{:S(2)}, u32[]{:S(2)}) collective-permute-start(bf16[1,80,2432]{2,1,0:T(8,128)(2,1)S(1)} %get-tuple-element.113), channel_id=1, source_target_pairs={{0,2},{1,3},{2,0},{3,1},{4,6},{5,7},{6,4},{7,5},{8,10},{9,11},{10,... | collective-permute-start | bytes 1167368 | tf_op jit(solution)/shard_map/ppermute | solution.py:337
  71.3 4.1 %project.3 = (bf16[6,80,384]{2,1,0:T(8,128)(2,1)S(1)}, bf16[6,80,384]{2,1,0:T(8,128)(2,1)S(1)}, f32[8,128]{1,0:T(8,128)S(1)}) custom-call(bf16[80,2432]{1,0:T(8,128)(2,1)S(1)} %collective-permute-done.1.refs_0_, bf16[80,2432]{1,0:T(8,128)(2,1)S(1)} %copy-done.16, bf16[80,2432]{1,0:T(8,128)(2,1)S(1)} %copy-done.18, bf16[160,2432]{1,0:T(8,128)(2,1)S(1)} %copy-done.14, ...), custom_call_target="tpu_custom_call" | custom-call | flops 2357499904 | tf_op jit(solution)/shard_map/project/pallas_call | solution.py:42
  75.5 1.6 %collective-permute-start.16 = (bf16[1,80,2432]{2,1,0:T(8,128)(2,1)S(1)}, bf16[1,80,2432]{2,1,0:T(8,128)(2,1)S(1)}, u32[]{:S(2)}, u32[]{:S(2)}) collective-permute-start(bf16[1,80,2432]{2,1,0:T(8,128)(2,1)S(1)} %get-tuple-element.123), channel_id=1, source_target_pairs={{0,2},{1,3},{2,0},{3,1},{4,6},{5,7},{6,4},{7,5},{8,10},{9,11},{10,... | collective-permute-start | bytes 1167368 | tf_op jit(solution)/shard_map/ppermute | solution.py:337
  77.1 3.6 %collective-permute-done.14.refs_1_ = bf16[1,80,2432]{2,1,0:T(8,128)(2,1)S(1)} collective-permute-done((bf16[1,80,2432]{2,1,0:T(8,128)(2,1)S(1)}, bf16[1,80,2432]{2,1,0:T(8,128)(2,1)S(1)}, u32[]{:S(2)}, u32[]{:S(2)}) %collective-permute-start.14) | collective-permute-done | bytes 389152 | tf_op jit(solution)/shard_map/ppermute | solution.py:337
  82.3 2.7 %collective-permute-start.20 = (bf16[80,2432]{1,0:T(8,128)(2,1)S(1)}, bf16[80,2432]{1,0:T(8,128)(2,1)S(1)}, u32[]{:S(2)}, u32[]{:S(2)}) collective-permute-start(bf16[80,2432]{1,0:T(8,128)(2,1)S(1)} %get-tuple-element.137), channel_id=1, source_target_pairs={{0,8},{4,12},{8,0},{12,4},{1,9},{5,13},{9,1},{13,5},{2,10},{6,14},... | collective-permute-start | bytes 1167368 | tf_op jit(solution)/shard_map/ppermute | solution.py:342
  87.4 9.7 %back.3 = (bf16[384,1280]{1,0:T(8,128)(2,1)}, f32[384,1280]{1,0:T(8,128)S(1)}, f32[384,1280]{1,0:T(8,128)S(1)}, f32[10,3,768]{2,1,0:T(4,128)S(1)}, f32[8,128]{1,0:T(8,128)S(1)}) custom-call(bf16[20,768,768]{2,1,0:T(8,128)(2,1)} %get-tuple-element.101.refs_0_, f32[10,2,768]{2,1,0:T(2,128)S(1)} %get-tuple-element.102.refs_1_, bf16[384,1280]{1,0:T(8,128)(2,1)S(1)} %bitcast.68, ...), custom_call_target="tpu_custom_call" | custom-call | flops 6899999744 | tf_op jit(solution)/shard_map/back/pallas_call | solution.py:42
  97.2 1.8 %collective-permute-start.21 = (bf16[80,2432]{1,0:T(8,128)(2,1)S(1)}, bf16[80,2432]{1,0:T(8,128)(2,1)S(1)}, u32[]{:S(2)}, u32[]{:S(2)}) collective-permute-start(bf16[80,2432]{1,0:T(8,128)(2,1)S(1)} %get-tuple-element.139), channel_id=1, source_target_pairs={{0,4},{4,8},{8,12},{12,0},{1,5},{5,9},{9,13},{13,1},{2,6},{6,10},{... | collective-permute-start | bytes 1167368 | tf_op jit(solution)/shard_map/ppermute | solution.py:342
  99.0 5.7 %back.4 = (bf16[384,1280]{1,0:T(8,128)(2,1)}, f32[384,1280]{1,0:T(8,128)S(1)}, f32[384,1280]{1,0:T(8,128)S(1)}, f32[10,3,768]{2,1,0:T(4,128)S(1)}, f32[8,128]{1,0:T(8,128)S(1)}) custom-call(bf16[20,768,768]{2,1,0:T(8,128)(2,1)} %get-tuple-element.101.refs_0_, ...), custom_call_target="tpu_custom_call", output_to_operand_aliasing={{0}: (7, {}), {1}: (8, {}), {2}: (9, {}), {3}: (10, {})} | custom-call | flops 57500000 | tf_op jit(solution)/shard_map/back/pallas_call | solution.py:42
  104.7 3.1 %back.5 = (bf16[384,1280]{1,0:T(8,128)(2,1)}, f32[384,1280]{1,0:T(8,128)S(1)}, f32[384,1280]{1,0:T(8,128)S(1)}, f32[10,3,768]{2,1,0:T(4,128)S(1)}, f32[8,128]{1,0:T(8,128)S(1)}) custom-call(bf16[20,768,768]{2,1,0:T(8,128)(2,1)} %get-tuple-element.101.refs_0_, ...), custom_call_target="tpu_custom_call", output_to_operand_aliasing={{0}: (7, {}), {1}: (8, {}), {2}: (9, {}), {3}: (10, {})} | custom-call | flops 57500000 | tf_op jit(solution)/shard_map/back/pallas_call | solution.py:42
  109.0 2.3 %collective-permute-start.22 = (bf16[80,2432]{1,0:T(8,128)(2,1)S(1)}, bf16[80,2432]{1,0:T(8,128)(2,1)S(1)}, u32[]{:S(2)}, u32[]{:S(2)}) collective-permute-start(bf16[80,2432]{1,0:T(8,128)(2,1)S(1)} %get-tuple-element.143), channel_id=1, source_target_pairs={{0,12},{4,0},{8,4},{12,8},{1,13},{5,1},{9,5},{13,9},{2,14},{6,2},{... | collective-permute-start | bytes 1167368 | tf_op jit(solution)/shard_map/ppermute | solution.py:342
  112.7 5.3 %cross.2 = (bf16[384,1280]{1,0:T(8,128)(2,1)}, bf16[384,1280]{1,0:T(8,128)(2,1)}, f32[8,128]{1,0:T(8,128)S(1)}) custom-call(bf16[384,1280]{1,0:T(8,128)(2,1)S(1)} %collective-permute-done.15.refs_7_.refs_0_, bf16[384,1280]{1,0:T(8,128)(2,1)S(1)} %bitcast.51, bf16[384,1280]{1,0:T(8,128)(2,1)S(1)} %bitcast.62, ...), custom_call_target="tpu_custom_call" | custom-call | flops 4312500224 | tf_op jit(solution)/shard_map/cross/pallas_call | solution.py:42
  120.5 5.3 %cross.3 = (bf16[384,1280]{1,0:T(8,128)(2,1)}, bf16[384,1280]{1,0:T(8,128)(2,1)}, f32[8,128]{1,0:T(8,128)S(1)}) custom-call(bf16[384,1280]{1,0:T(8,128)(2,1)S(1)} %collective-permute-done.15.refs_7_.refs_0_, bf16[384,1280]{1,0:T(8,128)(2,1)S(1)} %bitcast.52, bf16[384,1280]{1,0:T(8,128)(2,1)S(1)} %bitcast.63, ...), custom_call_target="tpu_custom_call", output_to_operand_aliasing={{0}: (7, {}), {1}: (8, {})} | custom-call | flops 4312500224 | tf_op jit(solution)/shard_map/cross/pallas_call | solution.py:42
  (94 shorter events, 32.6 us)
Async XLA Ops:
  0.6 8.3 %collective-permute-start = (bf16[80,1216]{1,0:T(8,128)(2,1)}, bf16[80,1216]{1,0:T(8,128)(2,1)S(1)}, u32[]{:S(2)}, u32[]{:S(2)}) collective-permute-start(bf16[80,1216]{1,0:T(8,128)(2,1)} %refs_1_.1), channel_id=1, source_target_pairs={{0,16},{16,0},{1,17},{17,1},{2,18},{18,2},{3,19},{19,3},{4,20},{20... | collective-permute-start | bytes 583688 | tf_op jit(solution)/shard_map/ppermute | solution.py:337
  3.6 11.1 %collective-permute-start.5 = (bf16[384,2432]{1,0:T(8,128)(2,1)}, bf16[384,2432]{1,0:T(8,128)(2,1)}, u32[]{:S(2)}, u32[]{:S(2)}) collective-permute-start(bf16[384,2432]{1,0:T(8,128)(2,1)} %bitcast.75), channel_id=1, source_target_pairs={{0,1},{1,0},{2,3},{3,2},{4,5},{5,4},{6,7},{7,6},{8,9},{9,8},{10,11... | collective-permute-start | bytes 5603336 | tf_op jit(solution)/shard_map/ppermute | solution.py:337
  7.5 16.3 %collective-permute-start.3 = (bf16[768,384]{1,0:T(8,128)(2,1)}, bf16[768,384]{1,0:T(8,128)(2,1)S(1)}, u32[]{:S(2)}, u32[]{:S(2)}) collective-permute-start(bf16[768,384]{1,0:T(8,128)(2,1)} %get-tuple-element.80), channel_id=1, source_target_pairs={{0,16},{16,0},{1,17},{17,1},{2,18},{18,2},{3,19},{19,3},{4,20},{20... | collective-permute-start | bytes 1769480 | tf_op jit(solution)/shard_map/ppermute | solution.py:337
  9.1 10.3 %collective-permute-start.4 = (bf16[80,2432]{1,0:T(8,128)(2,1)S(1)}, bf16[80,2432]{1,0:T(8,128)(2,1)S(1)}, u32[]{:S(2)}, u32[]{:S(2)}) collective-permute-start(bf16[80,2432]{1,0:T(8,128)(2,1)S(1)} %get-tuple-element.79.refs_0_), channel_id=1, source_target_pairs={{0,2},{1,3},{2,0},{3,1},{4,6},{5,7},{6,4},{7,5},{8,10},{9,11},{10,... | collective-permute-start | bytes 1167368 | tf_op jit(solution)/shard_map/ppermute | solution.py:337
  10.9 19.8 %collective-permute-start.1 = (bf16[80,2432]{1,0:T(8,128)(2,1)S(1)}, bf16[80,2432]{1,0:T(8,128)(2,1)S(1)}, u32[]{:S(2)}, u32[]{:S(2)}) collective-permute-start(bf16[80,2432]{1,0:T(8,128)(2,1)S(1)} %get-tuple-element.79.refs_0_), channel_id=1, source_target_pairs={{0,4},{4,8},{8,12},{12,0},{1,5},{5,9},{9,13},{13,1},{2,6},{6,10},{... | collective-permute-start | bytes 1167368 | tf_op jit(solution)/shard_map/ppermute | solution.py:342
  12.5 18.2 %collective-permute-start.2 = (bf16[80,2432]{1,0:T(8,128)(2,1)S(1)}, bf16[80,2432]{1,0:T(8,128)(2,1)S(1)}, u32[]{:S(2)}, u32[]{:S(2)}) collective-permute-start(bf16[80,2432]{1,0:T(8,128)(2,1)S(1)} %get-tuple-element.79.refs_0_), channel_id=1, source_target_pairs={{0,12},{4,0},{8,4},{12,8},{1,13},{5,1},{9,5},{13,9},{2,14},{6,2},{... | collective-permute-start | bytes 1167368 | tf_op jit(solution)/shard_map/ppermute | solution.py:342
  15.3 29.6 %collective-permute-start.7 = (bf16[768,640]{1,0:T(8,128)(2,1)S(1)}, bf16[768,640]{1,0:T(8,128)(2,1)S(1)}, u32[]{:S(2)}, u32[]{:S(2)}) collective-permute-start(bf16[768,640]{1,0:T(8,128)(2,1)S(1)} %get-tuple-element.87), channel_id=1, source_target_pairs={{0,16},{16,0},{1,17},{17,1},{2,18},{18,2},{3,19},{19,3},{4,20},{20... | collective-permute-start | bytes 2949128 | tf_op jit(solution)/shard_map/ppermute | solution.py:337
  31.4 22.2 %collective-permute-start.9 = (bf16[160,2432]{1,0:T(8,128)(2,1)S(1)}, bf16[160,2432]{1,0:T(8,128)(2,1)S(1)}, u32[]{:S(2)}, u32[]{:S(2)}) collective-permute-start(bf16[160,2432]{1,0:T(8,128)(2,1)S(1)} %get-tuple-element.99), channel_id=1, source_target_pairs={{0,2},{1,3},{2,0},{3,1},{4,6},{5,7},{6,4},{7,5},{8,10},{9,11},{10,... | collective-permute-start | bytes 2334728 | tf_op jit(solution)/shard_map/ppermute | solution.py:337
  32.9 20.7 %collective-permute-start.8 = (bf16[80,2432]{1,0:T(8,128)(2,1)S(1)}, bf16[80,2432]{1,0:T(8,128)(2,1)S(1)}, u32[]{:S(2)}, u32[]{:S(2)}) collective-permute-start(bf16[80,2432]{1,0:T(8,128)(2,1)S(1)} %get-tuple-element.79.refs_0_), channel_id=1, source_target_pairs={{0,8},{4,12},{8,0},{12,4},{1,9},{5,13},{9,1},{13,5},{2,10},{6,14},... | collective-permute-start | bytes 1167368 | tf_op jit(solution)/shard_map/ppermute | solution.py:342
  35.8 18.7 %collective-permute-start.6 = (bf16[768,256]{1,0:T(8,128)(2,1)S(1)}, bf16[768,256]{1,0:T(8,128)(2,1)S(1)}, u32[]{:S(2)}, u32[]{:S(2)}) collective-permute-start(bf16[768,256]{1,0:T(8,128)(2,1)S(1)} %get-tuple-element.86), channel_id=1, source_target_pairs={{0,16},{16,0},{1,17},{17,1},{2,18},{18,2},{3,19},{19,3},{4,20},{20... | collective-permute-start | bytes 1179656 | tf_op jit(solution)/shard_map/ppermute | solution.py:337
  59.5 2.7 %collective-permute-start.11 = (bf16[16,80,384]{2,1,0:T(8,128)(2,1)S(1)}, bf16[16,80,384]{2,1,0:T(8,128)(2,1)}, u32[]{:S(2)}, u32[]{:S(2)}) collective-permute-start(bf16[16,80,384]{2,1,0:T(8,128)(2,1)S(1)} %bitcast.33), channel_id=1, source_target_pairs={{0,1},{1,0},{2,3},{3,2},{4,5},{5,4},{6,7},{7,6},{8,9},{9,8},{10,11... | collective-permute-start | bytes 2949128 | tf_op jit(solution)/shard_map/ppermute | solution.py:337
  59.5 11.8 %collective-permute-start.10 = (bf16[80,2432]{1,0:T(8,128)(2,1)}, bf16[80,2432]{1,0:T(8,128)(2,1)}, u32[]{:S(2)}, u32[]{:S(2)}) collective-permute-start(bf16[80,2432]{1,0:T(8,128)(2,1)} %get-tuple-element.105), channel_id=1, source_target_pairs={{0,2},{1,3},{2,0},{3,1},{4,6},{5,7},{6,4},{7,5},{8,10},{9,11},{10,... | collective-permute-start | bytes 1167368 | tf_op jit(solution)/shard_map/ppermute | solution.py:337
  61.2 21.1 %collective-permute-start.12 = (bf16[2,80,384]{2,1,0:T(8,128)(2,1)}, bf16[2,80,384]{2,1,0:T(8,128)(2,1)S(1)}, u32[]{:S(2)}, u32[]{:S(2)}) collective-permute-start(bf16[2,80,384]{2,1,0:T(8,128)(2,1)} %copy-done.20), channel_id=1, source_target_pairs={{0,1},{1,0},{2,3},{3,2},{4,5},{5,4},{6,7},{7,6},{8,9},{9,8},{10,11... | collective-permute-start | bytes 368648 | tf_op jit(solution)/shard_map/ppermute | solution.py:337
  61.4 24.2 %collective-permute-start.15 = (bf16[384,1280]{1,0:T(8,128)(2,1)}, bf16[384,1280]{1,0:T(8,128)(2,1)S(1)}, u32[]{:S(2)}, u32[]{:S(2)}) collective-permute-start(bf16[384,1280]{1,0:T(8,128)(2,1)} %copy-done.12), channel_id=1, source_target_pairs={{0,16},{16,0},{1,17},{17,1},{2,18},{18,2},{3,19},{19,3},{4,20},{20... | collective-permute-start | bytes 2949128 | tf_op jit(solution)/shard_map/ppermute | solution.py:337
  68.8 11.9 %collective-permute-start.14 = (bf16[1,80,2432]{2,1,0:T(8,128)(2,1)S(1)}, bf16[1,80,2432]{2,1,0:T(8,128)(2,1)S(1)}, u32[]{:S(2)}, u32[]{:S(2)}) collective-permute-start(bf16[1,80,2432]{2,1,0:T(8,128)(2,1)S(1)} %get-tuple-element.113), channel_id=1, source_target_pairs={{0,2},{1,3},{2,0},{3,1},{4,6},{5,7},{6,4},{7,5},{8,10},{9,11},{10,... | collective-permute-start | bytes 1167368 | tf_op jit(solution)/shard_map/ppermute | solution.py:337
  75.3 10.3 %collective-permute-start.13 = (bf16[6,80,384]{2,1,0:T(8,128)(2,1)S(1)}, bf16[6,80,384]{2,1,0:T(8,128)(2,1)S(1)}, u32[]{:S(2)}, u32[]{:S(2)}) collective-permute-start(bf16[6,80,384]{2,1,0:T(8,128)(2,1)S(1)} %get-tuple-element.111), channel_id=1, source_target_pairs={{0,1},{1,0},{2,3},{3,2},{4,5},{5,4},{6,7},{7,6},{8,9},{9,8},{10,11... | collective-permute-start | bytes 1105928 | tf_op jit(solution)/shard_map/ppermute | solution.py:337
  75.5 21.6 %collective-permute-start.16 = (bf16[1,80,2432]{2,1,0:T(8,128)(2,1)S(1)}, bf16[1,80,2432]{2,1,0:T(8,128)(2,1)S(1)}, u32[]{:S(2)}, u32[]{:S(2)}) collective-permute-start(bf16[1,80,2432]{2,1,0:T(8,128)(2,1)S(1)} %get-tuple-element.123), channel_id=1, source_target_pairs={{0,2},{1,3},{2,0},{3,1},{4,6},{5,7},{6,4},{7,5},{8,10},{9,11},{10,... | collective-permute-start | bytes 1167368 | tf_op jit(solution)/shard_map/ppermute | solution.py:337
  80.7 28.1 %collective-permute-start.19 = (bf16[2,80,2432]{2,1,0:T(8,128)(2,1)S(1)}, bf16[2,80,2432]{2,1,0:T(8,128)(2,1)S(1)}, u32[]{:S(2)}, u32[]{:S(2)}) collective-permute-start(bf16[2,80,2432]{2,1,0:T(8,128)(2,1)S(1)} %get-tuple-element.135), channel_id=1, source_target_pairs={{0,2},{1,3},{2,0},{3,1},{4,6},{5,7},{6,4},{7,5},{8,10},{9,11},{10,... | collective-permute-start | bytes 2334728 | tf_op jit(solution)/shard_map/ppermute | solution.py:337
  82.3 26.5 %collective-permute-start.20 = (bf16[80,2432]{1,0:T(8,128)(2,1)S(1)}, bf16[80,2432]{1,0:T(8,128)(2,1)S(1)}, u32[]{:S(2)}, u32[]{:S(2)}) collective-permute-start(bf16[80,2432]{1,0:T(8,128)(2,1)S(1)} %get-tuple-element.137), channel_id=1, source_target_pairs={{0,8},{4,12},{8,0},{12,4},{1,9},{5,13},{9,1},{13,5},{2,10},{6,14},... | collective-permute-start | bytes 1167368 | tf_op jit(solution)/shard_map/ppermute | solution.py:342
  86.2 26.5 %collective-permute-start.17 = (bf16[1280,384]{1,0:T(8,128)(2,1)S(1)}, bf16[1280,384]{1,0:T(8,128)(2,1)S(1)}, u32[]{:S(2)}, u32[]{:S(2)}) collective-permute-start(bf16[1280,384]{1,0:T(8,128)(2,1)S(1)} %bitcast.71), channel_id=1, source_target_pairs={{0,16},{16,0},{1,17},{17,1},{2,18},{18,2},{3,19},{19,3},{4,20},{20... | collective-permute-start | bytes 2949128 | tf_op jit(solution)/shard_map/ppermute | solution.py:337
  97.2 15.5 %collective-permute-start.21 = (bf16[80,2432]{1,0:T(8,128)(2,1)S(1)}, bf16[80,2432]{1,0:T(8,128)(2,1)S(1)}, u32[]{:S(2)}, u32[]{:S(2)}) collective-permute-start(bf16[80,2432]{1,0:T(8,128)(2,1)S(1)} %get-tuple-element.139), channel_id=1, source_target_pairs={{0,4},{4,8},{8,12},{12,0},{1,5},{5,9},{9,13},{13,1},{2,6},{6,10},{... | collective-permute-start | bytes 1167368 | tf_op jit(solution)/shard_map/ppermute | solution.py:342
  107.8 4.9 %collective-permute-start.18 = (f32[10,3,768]{2,1,0:T(4,128)S(1)}, f32[10,3,768]{2,1,0:T(4,128)S(1)}, u32[]{:S(2)}, u32[]{:S(2)}) collective-permute-start(f32[10,3,768]{2,1,0:T(4,128)S(1)} %get-tuple-element.132), channel_id=1, source_target_pairs={{0,16},{16,0},{1,17},{17,1},{2,18},{18,2},{3,19},{19,3},{4,20},{20... | collective-permute-start | bytes 276488 | tf_op jit(solution)/shard_map/ppermute | solution.py:337
  109.0 9.6 %collective-permute-start.22 = (bf16[80,2432]{1,0:T(8,128)(2,1)S(1)}, bf16[80,2432]{1,0:T(8,128)(2,1)S(1)}, u32[]{:S(2)}, u32[]{:S(2)}) collective-permute-start(bf16[80,2432]{1,0:T(8,128)(2,1)S(1)} %get-tuple-element.143), channel_id=1, source_target_pairs={{0,12},{4,0},{8,4},{12,8},{1,13},{5,1},{9,5},{13,9},{2,14},{6,2},{... | collective-permute-start | bytes 1167368 | tf_op jit(solution)/shard_map/ppermute | solution.py:342
  119.1 6.7 %collective-permute-start.23 = (bf16[80,1216]{1,0:T(8,128)(2,1)S(1)}, bf16[80,1216]{1,0:T(8,128)(2,1)S(1)}, u32[]{:S(2)}, u32[]{:S(2)}) collective-permute-start(bf16[80,1216]{1,0:T(8,128)(2,1)S(1)} %get-tuple-element.149), channel_id=1, source_target_pairs={{0,16},{16,0},{1,17},{17,1},{2,18},{18,2},{3,19},{19,3},{4,20},{20... | collective-permute-start | bytes 583688 | tf_op jit(solution)/shard_map/ppermute | solution.py:337
  (21 other events, 74.6 us)
